TPU v7x, 256 devices: a whole 4x4x8 slice. The times are simulated.
256 devices in a mesh: col: 64 (over y, z, core), tok: 4 (over x).
Axes of the slice: x: 4, y: 4, z: 8, core: 2. Of those that a mesh axis runs over, the one named last changes fastest.
Arguments:
- krylov_basis: bfloat16 [8, 8192, 8192], P(None, 'tok', 'col'), as said below
- hessian_product: float32 [8192, 8192], P('tok', 'col'), as said below
- output_grads: bfloat16 [4096, 8192], P('col', 'tok'), may hold values from -0.26367188 to 0.26367188
- layer_inputs: bfloat16 [4096, 8192], P('tok', 'col'), may hold values from -6 to 6
- rotation: float32 [8, 4], replicated, may hold values from -3 to 3
Outputs:
- new_vector: bfloat16 [8192, 8192], P('tok', 'col')
- hessenberg: float32 [9], replicated
- influence: float32 [8, 4], replicated
Inputs may be any that keep to these rules, and one draw needn't show every extreme that they name: `krylov_basis`: entries of order 1 / 8192. `hessian_product`: entries of order 1 / 8192.
All inputs are finite; a program needn't handle non-finite values.
Results may differ from a plain program's by a relative error of at most 0.005.
Values may be sent and summed in bfloat16 or wider, within the bound.
No kernel may reach another device: no remote copies, remote signals or barrier semaphores. Data moves between devices by JAX's collectives and lax.ppermute only.
A program may use at most 128 MiB of HBM per device.

v0:
```python
import jax
import jax.numpy as jnp
from jax import lax
from jax.sharding import PartitionSpec as P

LEN = 512
SEQS = 8


def global_sum(value):
    return lax.psum(value, ("col", "tok"))


def on_device(krylov_basis, hessian_product, output_grads, layer_inputs, rotation):
    highest = lax.Precision.HIGHEST
    out_rows = krylov_basis.shape[1]
    in_cols = krylov_basis.shape[2]
    grad_rows = lax.all_gather(output_grads, "col", axis=0, tiled=True)
    input_rows = lax.all_gather(layer_inputs, "tok", axis=0, tiled=True)
    tiles = jnp.einsum(
        "slo,sli->soi",
        grad_rows.reshape(SEQS, LEN, out_rows),
        input_rows.reshape(SEQS, LEN, in_cols),
        preferred_element_type=jnp.float32,
    )
    partial_coords = jnp.einsum("soi,koi->sk", tiles, krylov_basis, precision=highest)
    first_dots = global_sum(
        jnp.einsum("koi,oi->k", krylov_basis, hessian_product, precision=highest)
    )
    remainder = hessian_product - jnp.einsum(
        "k,koi->oi", first_dots, krylov_basis, precision=highest
    )
    second_dots = global_sum(jnp.einsum("koi,oi->k", krylov_basis, remainder, precision=highest))
    remainder = remainder - jnp.einsum("k,koi->oi", second_dots, krylov_basis, precision=highest)
    squares, coordinates = global_sum((jnp.sum(remainder * remainder), partial_coords))
    length = jnp.sqrt(squares + 1e-06)
    new_vector = (remainder / length).astype(jnp.bfloat16)
    hessenberg = jnp.concatenate([first_dots + second_dots, length[None]])
    influence = jnp.dot(coordinates, rotation, precision=highest)
    return (new_vector, hessenberg, influence)


def solution(mesh):
    return jax.shard_map(
        on_device,
        mesh=mesh,
        in_specs=(P(None, "tok", "col"), P("tok", "col"), P("col", "tok"), P("tok", "col"), P()),
        out_specs=(P("tok", "col"), P(), P()),
        check_vma=False,
    )
```

profile of v0, /device:TPU:1, one launch (start us, length us, event | category | flops | bytes accessed | tf_op | source)
XLA Modules:
  0.0 309.2 jit_solution(17551409052493741941)
XLA Ops:
  7.2 0.0 copy-start
  7.2 0.0 copy-start.2
  7.2 0.0 all-gather.5.cloned.1.call-start
  7.2 0.7 all-gather.5.cloned.1.call-update
  7.9 0.0 all-gather.3.cloned.1.call-start
  8.0 0.7 all-gather.3.cloned.1.call-update
  8.7 3.6 %fusion = f32[8]{0:T(128)S(1)} fusion(f32[128,2048]{0,1:T(8,128)} %bitcast.29, bf16[8,2048,128]{2,1,0:T(8,128)(2,1)} %param.5), kind=kLoop, calls=%fused_computation.2 | loop fusion | flops 6291448 | bytes 5242912 | tf_op jit(solution)/shard_map/koi,oi->k/dot_general | solution.py:28
  12.2 82.0 %psum.28 = f32[8]{0:T(128)S(1)} all-reduce(f32[8]{0:T(128)S(1)} %fusion), channel_id=1, replica_groups=mesh['col'=64,'tok'=4] {'col','tok'}, use_global_device_ids=true, to_apply=%region_0.0 | all-reduce | flops 8 | bytes 64 | tf_op jit(solution)/shard_map/psum | solution.py:11
  94.2 0.0 copy-start.1
  94.2 7.7 %fusion.4 = f32[1,2048,128]{2,0,1:T(1,128)S(1)} fusion(bf16[8,2048,128]{2,1,0:T(8,128)(2,1)} %param.5, f32[8]{0:T(128)S(1)} %psum.28), kind=kOutput, calls=%fused_computation.6 | convolution fusion | flops 25165824 | bytes 5242912 | tf_op jit(solution)/shard_map/k,koi->oi/dot_general | solution.py:30
  101.9 0.0 copy-done.2
  101.9 0.1 sub.6
  102.0 0.0 copy-done.1
  102.0 1.2 fusion.1
  103.2 74.1 %psum.29 = f32[8]{0:T(128)S(1)} all-reduce(f32[8]{0:T(128)S(1)} %fusion.1), channel_id=1, replica_groups=mesh['col'=64,'tok'=4] {'col','tok'}, use_global_device_ids=true, to_apply=%region_1.0 | all-reduce | flops 8 | bytes 64 | tf_op jit(solution)/shard_map/psum | solution.py:11
  177.3 6.7 %copy.22 = bf16[8,2048,128]{1,0,2:T(8,128)(2,1)} copy(bf16[8,2048,128]{2,1,0:T(8,128)(2,1)} %param.5) | data formatting | bytes 8388608 | tf_op args[0]
  184.0 7.1 %fusion.2 = f32[1,2048,128]{2,0,1:T(1,128)S(1)} fusion(bf16[8,2048,128]{2,1,0:T(8,128)(2,1)} %param.5, f32[8]{0:T(128)S(1)} %psum.29), kind=kOutput, calls=%fused_computation.4 | convolution fusion | flops 25165824 | bytes 5242912 | tf_op jit(solution)/shard_map/k,koi->oi/dot_general | solution.py:34
  191.2 0.9 multiply_reduce_fusion
  192.1 0.0 all-gather.5.cloned.1.call-done
  192.1 0.0 all-gather.3.cloned.1.call-done
  192.1 11.0 %fusion.8 = f32[8,2048,128]{2,1,0:T(8,128)} fusion(bf16[8,512,2048]{2,1,0:T(8,128)(2,1)} %bitcast.27, bf16[8,512,128]{2,1,0:T(8,128)(2,1)} %bitcast.32), kind=kOutput, calls=%fused_computation.14 | convolution fusion | flops 2147483648 | bytes 26214400 | tf_op jit(solution)/shard_map/slo,sli->soi/dot_general | solution.py:20
  203.0 9.4 %copy.21 = f32[8,2048,128]{1,0,2:T(8,128)} copy(f32[8,2048,128]{2,1,0:T(8,128)} %fusion.8) | data formatting | bytes 16777216 | tf_op jit(solution)/shard_map/slo,sli->soi/dot_general | solution.py:20
  212.5 13.5 %convolution_bitcast_fusion = f32[8,8]{1,0:T(8,128)S(1)} fusion(f32[8,2048,128]{1,0,2:T(8,128)} %copy.21, bf16[8,2048,128]{1,0,2:T(8,128)(2,1)} %copy.22), kind=kOutput, calls=%fused_computation.8 | convolution fusion | flops 201326592 | bytes 12583168 | tf_op jit(solution)/shard_map/soi,koi->sk/dot_general | solution.py:26
  226.0 73.5 %all-reduce = (f32[]{:T(128)}, f32[8,8]{1,0:T(8,128)S(1)}) all-reduce(f32[]{:T(128)} %get-tuple-element.5, f32[8,8]{1,0:T(8,128)S(1)} %convolution_bitcast_fusion), channel_id=1, replica_groups=mesh['col'=64,'tok'=4] {'col','tok'}, use_global_device_ids=true, to_apply=%region_3.0 | all-reduce | flops 65 | bytes 520 | tf_op jit(solution)/shard_map/psum | solution.py:11
  300.2 0.9 divide_convert_fusion
  301.1 0.0 copy-done
  301.1 0.7 fusion.9
  301.8 0.6 pad_maximum_fusion
  (1 shorter events, 0.0 us)
Async XLA Ops:
  7.2 293.9 %copy-start = (f32[8,4]{0,1:T(4,128)S(1)}, f32[8,4]{0,1:T(4,128)}, u32[]{:S(2)}) copy-start(f32[8,4]{0,1:T(4,128)} %param.9) | copy-start | bytes 388
  7.2 94.7 %copy-start.2 = (f32[2048,128]{1,0:T(8,128)S(1)}, f32[2048,128]{1,0:T(8,128)}, u32[]{:S(2)}) copy-start(f32[2048,128]{1,0:T(8,128)} %param.6) | copy-start | bytes 3145732
  7.2 184.9 %all-gather.5.cloned.1.call-start = ((), (), s32[]{:S(2)}) async-start(), calls=%async_computation.1 | async-start | bytes 1310720 | tf_op jit(solution)/shard_map/all_gather | solution.py:19
  7.9 184.1 %all-gather.3.cloned.1.call-start = ((), (), s32[]{:S(2)}) async-start(), calls=%async_computation | async-start | bytes 17039360 | tf_op jit(solution)/shard_map/all_gather | solution.py:18
  94.2 7.8 %copy-start.1 = (bf16[8,2048,128]{2,1,0:T(8,128)(2,1)S(1)}, bf16[8,2048,128]{2,1,0:T(8,128)(2,1)}, u32[]{:S(2)}) copy-start(bf16[8,2048,128]{2,1,0:T(8,128)(2,1)} %param.5) | copy-start | bytes 12582916
Sparse Core Ops, SparseCore 0:
  9.8 29.5 all-gather.4
  42.3 102.6 all-gather.2
where the time goes:
time: 310 us; the launch traced here: 309 us
  blocking collectives  230 us (74%)
  matrix products  40 us (13%)
  local copies, waits for them, and re-layouts  16.1 us (5%)
  between operations  14.8 us (5%)
  other arithmetic  7.19 us (2%)
    psum x3, blocking collectives, global_sum(): return lax.psum(value, ('col', 'tok'))  230 us
    dot_general x1, matrix products, on_device(): jnp.einsum('soi,koi->sk', tiles, krylov_basis, precision=highest)  13.5 us
    dot_general x1, matrix products, on_device(): jnp.einsum('slo,sli->soi', grad_rows.reshape(SEQS, LEN, out_rows), input_...  11 us
    dot_general x1, local copies, waits for them, and re-layouts, on_device(): jnp.einsum('slo,sli->soi', grad_rows.reshape(SEQS, LEN, out_rows), input_...  9.41 us
    dot_general x1, matrix products, on_device(): jnp.einsum('k,koi->oi', first_dots, krylov_basis, precision=highest)  7.68 us
    dot_general x1, matrix products, on_device(): jnp.einsum('k,koi->oi', second_dots, krylov_basis, precision=highest)  7.13 us
    unnamed x7, local copies, waits for them, and re-layouts  6.73 us
  transfers between devices with their start and end apart: 2, of which 0 were waited for; matrix products, arithmetic and copies ran while one was open for 9% of the time, Pallas kernels for 0%

commit v1 on v0

v1 whole, which is shorter than its diff:
```python
import functools

import jax
import jax.numpy as jnp
from jax import lax
from jax.experimental import pallas as pl
from jax.experimental.pallas import tpu as pltpu
from jax.sharding import PartitionSpec as P

LEN = 512
SEQS = 8
K = 8
TOP = 4
YS = 4
ZS = 8
XS = 4
CHIP = 128
WIDE = 512
FIRST = 16
PAIRS = [(k, l) for k in range(K) for l in range(k, K)]
HIGHEST = lax.Precision.HIGHEST
MB = 2**20


def toward(value, axis, sign):
    size = lax.axis_size(axis)
    axes = ("core", axis) if axis == "x" else (axis, "core")

    def place(i, core):
        return core * size + i if axis == "x" else i * 2 + core

    pairs = [
        (place(i, core), place((i + (sign if core == 0 else -sign)) % size, core))
        for i in range(size)
        for core in range(2)
    ]
    return lax.ppermute(value, axes, pairs)


def swap_core(value):
    return lax.ppermute(value, "core", [(0, 1), (1, 0)])


def together(*values):
    return lax.optimization_barrier(values)


def sum_over(value, axes):
    copies = jnp.broadcast_to(value[None], (lax.axis_size(axes),) + value.shape)
    return jnp.sum(lax.all_to_all(copies, axes, 0, 0), axis=0)


def sum_everywhere(value):
    return sum_over(sum_over(value, ("z", "core")), ("y", "x"))


def lane_sums(rows):
    return lax.dot_general(
        jnp.ones((8, 128), jnp.float32),
        rows,
        (((1,), (1,)), ((), ())),
        precision=HIGHEST,
        preferred_element_type=jnp.float32,
    )


def gram_kernel(basis_ref, field_ref, out_ref, rows_ref):
    count = len(PAIRS) + K + 1

    def step(at, totals):
        rows = pl.ds(pl.multiple_of(at * 16, 16), 16)
        stack = [basis_ref[k, rows, :].astype(jnp.float32) for k in range(K)]
        field = field_ref[rows, :]
        terms = [stack[k] * stack[l] for k, l in PAIRS] + [stack[k] * field for k in range(K)]
        terms.append(field * field)
        return tuple(t + (a[:8] + a[8:]) for t, a in zip(totals, terms))

    zero = jnp.zeros((8, 128), jnp.float32)
    totals = lax.fori_loop(0, field_ref.shape[0] // 16, step, (zero,) * count)
    rows_ref[...] = jnp.zeros_like(rows_ref)
    for at, total in enumerate(totals):
        rows_ref[FIRST + at : FIRST + at + 1, :] = jnp.sum(total, axis=0, keepdims=True)
    sums = lane_sums(rows_ref[...])
    row = lax.broadcasted_iota(jnp.int32, (8, 128), 0)
    out_ref[...] = jnp.where(row == 0, sums, 0.0)


def gram(basis, field):
    return pl.pallas_call(
        gram_kernel,
        out_shape=jax.ShapeDtypeStruct((8, 128), jnp.float32),
        in_specs=[pl.BlockSpec(memory_space=pltpu.VMEM)] * 2,
        out_specs=pl.BlockSpec(memory_space=pltpu.VMEM),
        scratch_shapes=[pltpu.VMEM((128, 128), jnp.float32)],
        compiler_params=pltpu.CompilerParams(vmem_limit_bytes=8 * MB),
        cost_estimate=pl.CostEstimate(flops=24 * MB, bytes_accessed=18 * MB, transcendentals=0),
        name="gram",
    )(basis, field)


def weigh(sums_ref):
    def overlap(k, l):
        return sums_ref[0, FIRST + PAIRS.index((min(k, l), max(k, l)))]

    def times(vector):
        product = []
        for k in range(K):
            total = overlap(k, 0) * vector[0]
            for l in range(1, K):
                total += overlap(k, l) * vector[l]
            product.append(total)
        return product

    first = [sums_ref[0, FIRST + len(PAIRS) + k] for k in range(K)]
    whole = sums_ref[0, FIRST + len(PAIRS) + K]
    weights = [f + (f - t) for f, t in zip(first, times(first))]
    squares = whole
    for weight, dot, turned in zip(weights, first, times(weights)):
        squares += weight * (turned - (dot + dot))
    return weights, squares, whole


def take_off(weights, basis_ref, field_ref, rows):
    rest = field_ref[rows, :]
    for k in range(K):
        rest = rest - weights[k] * basis_ref[k, rows, :].astype(jnp.float32)
    return rest


def squares_kernel(sums_ref, basis_ref, field_ref, out_ref):
    weights = weigh(sums_ref)[0]

    def step(at, total):
        rest = take_off(weights, basis_ref, field_ref, pl.ds(pl.multiple_of(at * 16, 16), 16))
        square = rest * rest
        return total + (square[:8] + square[8:])

    out_ref[...] = lax.fori_loop(
        0, field_ref.shape[0] // 16, step, jnp.zeros((8, 128), jnp.float32)
    )


def squared_length(sums, basis, field):
    vmem = pl.BlockSpec(memory_space=pltpu.VMEM)
    parts = pl.pallas_call(
        squares_kernel,
        out_shape=jax.ShapeDtypeStruct((8, 128), jnp.float32),
        in_specs=[pl.BlockSpec(memory_space=pltpu.SMEM), vmem, vmem],
        out_specs=vmem,
        compiler_params=pltpu.CompilerParams(vmem_limit_bytes=8 * MB),
        name="squares",
    )(sums, basis, field)
    return jnp.sum(sum_everywhere(parts))


def finish_kernel(given, scalars_ref, squares_ref, sums_ref, rotation_ref, basis_ref, field_ref, *out_refs):
    new_ref, hessenberg_ref, influence_ref, little_ref = out_refs
    weights, squares, whole = weigh(scalars_ref)
    little_ref[0] = jnp.where(squares * 256.0 < whole, 1, 0)
    if given:
        squares = squares_ref[0]
    length = jnp.sqrt(jnp.full((16, 128), squares, jnp.float32) + 1e-06)
    scale = 1.0 / length

    def step(at, carry):
        rows = pl.ds(pl.multiple_of(at * 16, 16), 16)
        rest = take_off(weights, basis_ref, field_ref, rows)
        new_ref[rows, :] = (rest * scale).astype(jnp.bfloat16)
        return carry

    lax.fori_loop(0, field_ref.shape[0] // 16, step, 0, unroll=4)
    lane = lax.broadcasted_iota(jnp.int32, (8, 128), 1)
    row = length[:8]
    for k in range(K):
        row = jnp.where(lane == k, weights[k], row)
    hessenberg_ref[...] = row[0:1, : K + 1]
    influence_ref[...] = jnp.dot(
        jnp.where(lane < K, sums_ref[...], 0.0),
        rotation_ref[...],
        precision=HIGHEST,
        preferred_element_type=jnp.float32,
    )[:, :TOP]


def finish(given, squares, sums, rotation, basis, field):
    vmem, smem = (pl.BlockSpec(memory_space=m) for m in (pltpu.VMEM, pltpu.SMEM))
    return pl.pallas_call(
        functools.partial(finish_kernel, given),
        out_shape=[
            jax.ShapeDtypeStruct(field.shape, jnp.bfloat16),
            jax.ShapeDtypeStruct((1, K + 1), jnp.float32),
            jax.ShapeDtypeStruct((SEQS, TOP), jnp.float32),
            jax.ShapeDtypeStruct((1,), jnp.int32),
        ],
        in_specs=[smem, smem] + [vmem] * 4,
        out_specs=[vmem] * 3 + [smem],
        compiler_params=pltpu.CompilerParams(vmem_limit_bytes=8 * MB),
        cost_estimate=pl.CostEstimate(flops=6 * MB, bytes_accessed=6 * MB, transcendentals=0),
        name="finish",
    )(sums, squares, sums, rotation, basis, field)


def turn_basis_kernel(core_ref, own_ref, other_ref, out_ref):
    out_ref[0, :128, :] = own_ref[0].T
    out_ref[0, 128:, :] = other_ref[0].T


def turn_basis(core, basis, other):
    half = other.shape[1] // 2
    return pl.pallas_call(
        turn_basis_kernel,
        out_shape=jax.ShapeDtypeStruct((K, 256, half), jnp.bfloat16),
        grid_spec=pltpu.PrefetchScalarGridSpec(
            num_scalar_prefetch=1,
            grid=(K,),
            in_specs=[pl.BlockSpec((1, half, 128), lambda k, core: (k, core[0], 0))] * 2,
            out_specs=pl.BlockSpec((1, 256, half), lambda k, core: (k, 0, 0)),
        ),
        compiler_params=pltpu.CompilerParams(vmem_limit_bytes=8 * MB),
        cost_estimate=pl.CostEstimate(flops=0, bytes_accessed=8 * MB, transcendentals=0),
        name="turn_basis",
    )(core, basis, other)


def turn_inputs_kernel(core_ref, own_ref, other_ref, out_ref):
    for at, ref in enumerate((own_ref, other_ref)):
        parts = ref[...].reshape(-1, 2, CHIP // 2, 128)
        turned = jnp.concatenate([parts[:, 1:], parts[:, :1]], axis=1)
        parts = jnp.where(core_ref[0] == 1, turned, parts)
        out_ref[at * 128 : (at + 1) * 128, :] = parts.reshape(-1, 128).T


def turn_inputs(core, own, other):
    vmem = pl.BlockSpec(memory_space=pltpu.VMEM)
    return pl.pallas_call(
        turn_inputs_kernel,
        out_shape=jax.ShapeDtypeStruct((256, own.shape[0]), jnp.bfloat16),
        in_specs=[pl.BlockSpec(memory_space=pltpu.SMEM), vmem, vmem],
        out_specs=vmem,
        compiler_params=pltpu.CompilerParams(vmem_limit_bytes=8 * MB),
        cost_estimate=pl.CostEstimate(flops=0, bytes_accessed=MB, transcendentals=0),
        name="turn_inputs",
    )(core, own, other)


def keep_parts(parts_ref, slot, tile):
    high = tile.astype(jnp.bfloat16)
    parts_ref[2 * slot] = high
    parts_ref[2 * slot + 1] = (tile - high.astype(jnp.float32)).astype(jnp.bfloat16)


def products(parts_ref, count, basis_ref, first):
    def step(at, total):
        rows = pl.ds(pl.multiple_of(at * 32, 32), 32)
        tiles = parts_ref[: 2 * count, rows, :].reshape(count * 64, WIDE)
        basis = basis_ref[:, rows, first : first + WIDE].reshape(256, WIDE)
        return total + lax.dot_general(
            tiles, basis, (((1,), (1,)), ((), ())), preferred_element_type=jnp.float32
        )

    cross = lax.fori_loop(0, 8, step, jnp.zeros((count * 64, 256), jnp.float32))
    row = lax.broadcasted_iota(jnp.int32, cross.shape, 0)
    lane = lax.broadcasted_iota(jnp.int32, cross.shape, 1)
    cross = jnp.where(lax.rem(row, 32) == lax.rem(lane, 32), cross, 0.0)
    sums = jnp.sum(cross.reshape(count, 64, 256), axis=1)
    owner = lax.broadcasted_iota(jnp.int32, (256, 128), 0) // 32
    pick = (owner == lax.broadcasted_iota(jnp.int32, (256, 128), 1)).astype(jnp.float32)
    return jnp.dot(sums, pick, precision=HIGHEST, preferred_element_type=jnp.float32)


class Place:
    def __init__(self, ref):
        self.y, self.z, self.x, self.sign = (ref[i] for i in range(4))

    def y_slot(self, y):
        return lax.rem(self.sign * (self.y - y) + 2 * YS, YS)

    def z_slot(self, z):
        return lax.rem(self.sign * (self.z - z) + 2 * ZS, ZS)

    def x_slot(self, x):
        return lax.rem(self.sign * (self.x - x) + 2 * XS, XS)

    def y_of(self, slot):
        return lax.rem(self.y - self.sign * slot + 2 * YS, YS)


def chip_rows(slot):
    return pl.ds(pl.multiple_of(slot * CHIP, CHIP), CHIP)


def example_tile(place, inputs_ref, y, part, block):
    grads = jnp.concatenate([block(place.z_slot(part * 4 + j)) for j in range(4)], axis=0)
    cols = pl.ds(pl.multiple_of(part * LEN, LEN), LEN)
    inputs = inputs_ref[place.x_slot(y), :, cols]
    return jnp.dot(inputs, grads, preferred_element_type=jnp.float32)


def rows_example(place, inputs_ref, parts_ref, at, slot_y, ref):
    y = place.y_of(slot_y)
    for part in range(2):
        tile = example_tile(place, inputs_ref, y, part, lambda d: ref[chip_rows(d), :])
        keep_parts(parts_ref, at + part, tile)
    return [y * 2, y * 2 + 1]


def near_kernel(place_ref, basis_ref, before_ref, *refs):
    left, right, (out_ref, left_ref, inputs_ref, parts_ref) = refs[4:11], refs[11:14], refs[14:]
    for slot in range(XS):
        inputs_ref[slot] = refs[slot][...]
    place = Place(place_ref)
    out_ref[...] = before_ref[...]
    for slot, ref in zip((0, 1, 2, 3, 5, 6, 7), left):
        left_ref[slot] = ref[...]
    left_ref[4] = jnp.zeros_like(left_ref[4])

    def one(example, carry):
        y = example // 2
        rows = chip_rows(place.y_slot(y))
        tile = example_tile(
            place, inputs_ref, y, lax.rem(example, 2), lambda d: left_ref[d, rows, :]
        )
        keep_parts(parts_ref, example, tile)
        return carry

    lax.fori_loop(0, SEQS, one, 0)
    out_ref[...] += products(parts_ref, SEQS, basis_ref, 0)

    owners = []
    for at, (slot_y, ref) in enumerate(zip((0, 1, 3), right)):
        owners += rows_example(place, inputs_ref, parts_ref, 2 * at, slot_y, ref)
    sums = products(parts_ref, len(owners), basis_ref, WIDE)
    for at, owner in enumerate(owners):
        out_ref[pl.ds(owner, 1), :] += sums[at : at + 1]


def far_kernel(place_ref, basis_ref, before_ref, *refs):
    left_ref, right_ref, out_ref, inputs_ref, parts_ref = refs[4:]
    for slot in range(XS):
        inputs_ref[slot] = refs[slot][...]
    place = Place(place_ref)
    out_ref[...] = before_ref[...]
    z = lax.rem(place.z + 4, ZS)
    owners = []
    for slot_y in range(YS):
        y = place.y_of(slot_y)
        tile = jnp.dot(
            inputs_ref[place.x_slot(y), :, chip_rows(z)],
            left_ref[slot_y * CHIP : (slot_y + 1) * CHIP, :],
            preferred_element_type=jnp.float32,
        )
        keep_parts(parts_ref, slot_y, tile)
        owners.append(y * 2 + z // 4)
    left = products(parts_ref, YS, basis_ref, 0)
    owners += rows_example(place, inputs_ref, parts_ref, 0, 2, right_ref)
    right = products(parts_ref, 2, basis_ref, WIDE)
    for at, owner in enumerate(owners):
        row = left[at : at + 1] if at < YS else right[at - YS : at - YS + 1]
        out_ref[pl.ds(owner, 1), :] += row


def project(kernel, place, inputs, basis, before, grads, slots, scratch):
    vmem = pl.BlockSpec(memory_space=pltpu.VMEM)
    return pl.pallas_call(
        kernel,
        out_shape=jax.ShapeDtypeStruct((8, 128), jnp.float32),
        in_specs=[pl.BlockSpec(memory_space=pltpu.SMEM)] + [vmem] * (2 + len(inputs) + len(grads)),
        out_specs=vmem,
        scratch_shapes=scratch
        + [
            pltpu.VMEM((XS,) + inputs[0].shape, jnp.bfloat16),
            pltpu.VMEM((2 * slots, 256, WIDE), jnp.bfloat16),
        ],
        compiler_params=pltpu.CompilerParams(vmem_limit_bytes=16 * MB),
        cost_estimate=pl.CostEstimate(
            flops=sum(512 * g.size for g in grads) + 512 * MB * slots,
            bytes_accessed=4 * MB,
            transcendentals=0,
        ),
        name=kernel.__name__,
    )(place, basis, before, *inputs, *grads)


def on_device(krylov_basis, hessian_product, output_grads, layer_inputs, rotation):
    core = lax.axis_index("core")
    place = [lax.axis_index(axis) for axis in ("y", "z", "x")] + [1 - 2 * core]
    place = jnp.stack(place).astype(jnp.int32)
    core_id = core[None].astype(jnp.int32)
    half = krylov_basis.shape[1] // 2

    both = (output_grads, swap_core(output_grads))
    a, b = (
        jnp.concatenate(
            [lax.dynamic_slice_in_dim(g, core * half + at * WIDE, WIDE, 1) for g in both]
        )
        for at in range(2)
    )
    b1, b7 = toward(b, "z", 1), toward(b, "z", -1)
    a1, a3 = toward(a, "y", 1), toward(a, "y", -1)
    b1, krylov, layer = together(b1, krylov_basis, layer_inputs)
    x0 = turn_inputs(core_id, layer, swap_core(layer))
    x1, x3 = toward(x0, "x", 1), toward(x0, "x", -1)
    basis = turn_basis(core_id, krylov, swap_core(krylov))
    b2, b6 = toward(b1, "z", 1), toward(b7, "z", -1)
    a2 = toward(a1, "y", 1)
    l0 = jnp.concatenate([a, a1, a2, a3])
    l1, l7 = toward(l0, "z", 1), toward(l0, "z", -1)
    b3, b5 = toward(b2, "z", 1), toward(b6, "z", -1)
    b4 = toward(b3, "z", 1)
    b4, basis = together(b4, basis)
    r0 = jnp.concatenate([b, b1, b2, b3, b4, b5, b6, b7])
    x2 = toward(x1, "x", 1)
    r1, r3 = toward(r0, "y", 1), toward(r0, "y", -1)
    sums = gram(krylov_basis, hessian_product)
    l1, l7, sums = together(l1, l7, sums)
    l2, l6 = toward(l1, "z", 1), toward(l7, "z", -1)
    l2, l6, x2 = together(l2, l6, x2)
    l3, l5 = toward(l2, "z", 1), toward(l6, "z", -1)
    r2 = toward(r1, "y", 1)
    l4 = toward(l3, "z", 1)

    inputs = [x0, x1, x2, x3]
    near = [l0, l1, l2, l3, l5, l6, l7, r0, r1, r3]
    copy = pltpu.VMEM((ZS, YS * CHIP, WIDE), jnp.bfloat16)
    sums = project(near_kernel, place, inputs, basis, sums, near, SEQS, [copy])
    sums = project(far_kernel, place, inputs, basis, sums, [l4, r2], YS, [])
    sums = sum_everywhere(sums)

    rotation = jnp.pad(rotation, ((0, 128 - K), (0, 128 - TOP)))
    none = jnp.zeros((1,), jnp.float32)
    *results, little = finish(False, none, sums, rotation, krylov_basis, hessian_product)

    def measured(results):
        squares = squared_length(sums, krylov_basis, hessian_product)[None]
        return tuple(
            finish(True, squares, sums, rotation, krylov_basis, hessian_product)[:3]
        )

    new_vector, hessenberg, influence = lax.cond(
        little[0] == 1, measured, lambda results: tuple(results), results
    )
    return new_vector, hessenberg[0], influence


def solution(mesh):
    chips = jax.sharding.Mesh(mesh.devices.reshape(YS, ZS, 2, XS), ("y", "z", "core", "x"))
    col, tok = ("y", "z", "core"), "x"
    return jax.shard_map(
        on_device,
        mesh=chips,
        in_specs=(P(None, tok, col), P(tok, col), P(col, tok), P(tok, col), P()),
        out_specs=(P(tok, col), P(), P()),
        check_vma=False,
    )
```

time: 310 us -> 143 us (0.46)
  blocking collectives: 230 us -> 13.1 us
  starting transfers between devices: 0.08 us -> 44.2 us
  matrix products: 40 us -> 0 us
  Pallas kernels: 0 us -> 34.5 us
  waiting for transfers between devices: 1.38 us -> 34.1 us
  between operations: 14.8 us -> 1.61 us
  other arithmetic: 7.19 us -> 0.13 us
    psum x3 -> x0, blocking collectives: 230 us -> none  [global_sum(): return lax.psum(value, ('col', 'tok'))]
    dot_general x5 -> x0, matrix products: 40 us -> none  [the longest x1 13.5 us: on_device(): jnp.einsum('soi,koi->sk', tiles, krylov_basis, precision=highest)]
    ppermute x0 -> x26, starting transfers between devices: none -> 36.9 us  [the longest x23 31.7 us: toward(): return lax.ppermute(value, axes, pairs)]
    pallas_call x0 -> x6, Pallas kernels: none -> 34.5 us  [the longest x2 18.6 us: project(): pl.pallas_call(kernel, out_shape=jax.ShapeDtypeStruct((8, 128), jnp.float...]
    ppermute x0 -> x26, waiting for transfers between devices: none -> 27.7 us  [the longest x23 27.2 us: toward(): return lax.ppermute(value, axes, pairs)]
    all_to_all x0 -> x1, blocking collectives: none -> 13.1 us  [sum_over(): return jnp.sum(lax.all_to_all(copies, axes, 0, 0), axis=0)]
    dot_general x1 -> x0, local copies, waits for them, and re-layouts: 9.41 us -> none  [on_device(): jnp.einsum('slo,sli->soi', grad_rows.reshape(SEQS, LEN, out_rows), input_...]
    unnamed x7 -> x46, local copies, waits for them, and re-layouts: 6.73 us -> 14.2 us
  transfers between devices with their start and end apart: 2 -> 27, of which waited for: 0 -> 9; matrix products, arithmetic and copies ran while one was open for 9% -> 1% of each run, Pallas kernels for 0% -> 16%
where the time goes in v1:
time: 143 us
  starting transfers between devices  44.2 us (31%)
  Pallas kernels  34.5 us (24%)
  waiting for transfers between devices  34.1 us (24%)
  local copies, waits for them, and re-layouts  14.9 us (10%)
  blocking collectives  13.1 us (9%)
  between operations  1.61 us (1%)
    ppermute x23, starting transfers between devices, toward(): return lax.ppermute(value, axes, pairs)  31.7 us
    ppermute x23, waiting for transfers between devices, toward(): return lax.ppermute(value, axes, pairs)  27.2 us
    pallas_call x2, Pallas kernels, project(): pl.pallas_call(kernel, out_shape=jax.ShapeDtypeStruct((8, 128), jnp.float...  18.6 us
    unnamed x46, local copies, waits for them, and re-layouts  14.2 us
    all_to_all x1, blocking collectives, sum_over(): return jnp.sum(lax.all_to_all(copies, axes, 0, 0), axis=0)  13.1 us
    all_to_all x1, starting transfers between devices, sum_over(): return jnp.sum(lax.all_to_all(copies, axes, 0, 0), axis=0)  7.26 us
    all_to_all x1, waiting for transfers between devices, sum_over(): return jnp.sum(lax.all_to_all(copies, axes, 0, 0), axis=0)  6.42 us
    pallas_call x1, Pallas kernels, gram(): pl.pallas_call(gram_kernel, out_shape=jax.ShapeDtypeStruct((8, 128), jnp....  6.23 us
  transfers between devices with their start and end apart: 27, of which 9 were waited for; matrix products, arithmetic and copies ran while one was open for 1% of the time, Pallas kernels for 16%

profile of v1, /device:TPU:1, one launch (start us, length us, event | category | flops | bytes accessed | tf_op | source)
XLA Modules:
  0.0 142.6 jit_solution(2464954808695610244)
XLA Ops:
  0.6 3.3 %collective-permute-start = (bf16[64,2048]{1,0:T(8,128)(2,1)}, bf16[64,2048]{1,0:T(8,128)(2,1)S(1)}, u32[]{:S(2)}, u32[]{:S(2)}) collective-permute-start(bf16[64,2048]{1,0:T(8,128)(2,1)} %param.9), channel_id=1, source_target_pairs={{0,4},{4,0},{1,5},{5,1},{2,6},{6,2},{3,7},{7,3},{8,12},{12,8},{9,1... | collective-permute-start | bytes 786440 | tf_op jit(solution)/shard_map/ppermute | solution.py:41
  5.4 3.9 %collective-permute-start.1 = (bf16[128,512]{1,0:T(8,128)(2,1)S(1)}, bf16[128,512]{1,0:T(8,128)(2,1)S(1)}, u32[]{:S(2)}, u32[]{:S(2)}) collective-permute-start(bf16[128,512]{1,0:T(8,128)(2,1)S(1)} %pad_maximum_fusion), channel_id=1, source_target_pairs={{0,8},{4,60},{8,16},{12,4},{16,24},{20,12},{24,32},{28,20},{32,40}... | collective-permute-start | bytes 393224 | tf_op jit(solution)/shard_map/ppermute | solution.py:37
  9.3 1.9 %collective-permute-done.1 = bf16[128,512]{1,0:T(8,128)(2,1)S(1)} collective-permute-done((bf16[128,512]{1,0:T(8,128)(2,1)S(1)}, bf16[128,512]{1,0:T(8,128)(2,1)S(1)}, u32[]{:S(2)}, u32[]{:S(2)}) %collective-permute-start.1) | collective-permute-done | bytes 131104 | tf_op jit(solution)/shard_map/ppermute | solution.py:37
  11.2 1.7 %collective-permute-start.5 = (bf16[8,2048,128]{2,1,0:T(8,128)(2,1)}, bf16[8,2048,128]{2,1,0:T(8,128)(2,1)S(1)}, u32[]{:S(2)}, u32[]{:S(2)}) collective-permute-start(bf16[8,2048,128]{2,1,0:T(8,128)(2,1)} %basis_ref.3), channel_id=1, source_target_pairs={{0,4},{4,0},{1,5},{5,1},{2,6},{6,2},{3,7},{7,3},{8,12},{12,8},{9,1... | collective-permute-start | bytes 12582920 | tf_op jit(solution)/shard_map/ppermute | solution.py:41
  12.9 2.8 %collective-permute-start.6 = (bf16[128,512]{1,0:T(8,128)(2,1)S(1)}, bf16[128,512]{1,0:T(8,128)(2,1)S(1)}, u32[]{:S(2)}, u32[]{:S(2)}) collective-permute-start(bf16[128,512]{1,0:T(8,128)(2,1)S(1)} %pad_maximum_fusion.1), channel_id=1, source_target_pairs={{0,64},{4,196},{64,128},{68,4},{128,192},{132,68},{192,0},{196,132... | collective-permute-start | bytes 393224 | tf_op jit(solution)/shard_map/ppermute | solution.py:37
  15.7 2.7 %collective-permute-start.2 = (bf16[128,512]{1,0:T(8,128)(2,1)S(1)}, bf16[128,512]{1,0:T(8,128)(2,1)S(1)}, u32[]{:S(2)}, u32[]{:S(2)}) collective-permute-start(bf16[128,512]{1,0:T(8,128)(2,1)S(1)} %collective-permute-done.1), channel_id=1, source_target_pairs={{0,8},{4,60},{8,16},{12,4},{16,24},{20,12},{24,32},{28,20},{32,40}... | collective-permute-start | bytes 393224 | tf_op jit(solution)/shard_map/ppermute | solution.py:37
  18.4 3.4 %collective-permute-start.7 = (bf16[128,512]{1,0:T(8,128)(2,1)S(1)}, bf16[128,512]{1,0:T(8,128)(2,1)S(1)}, u32[]{:S(2)}, u32[]{:S(2)}) collective-permute-start(bf16[128,512]{1,0:T(8,128)(2,1)S(1)} %collective-permute-done.6), channel_id=1, source_target_pairs={{0,64},{4,196},{64,128},{68,4},{128,192},{132,68},{192,0},{196,132... | collective-permute-start | bytes 393224 | tf_op jit(solution)/shard_map/ppermute | solution.py:37
  22.1 1.6 %collective-permute-done.7 = bf16[128,512]{1,0:T(8,128)(2,1)S(1)} collective-permute-done((bf16[128,512]{1,0:T(8,128)(2,1)S(1)}, bf16[128,512]{1,0:T(8,128)(2,1)S(1)}, u32[]{:S(2)}, u32[]{:S(2)}) %collective-permute-start.7) | collective-permute-done | bytes 131104 | tf_op jit(solution)/shard_map/ppermute | solution.py:37
  23.7 1.9 %collective-permute-start.3 = (bf16[128,512]{1,0:T(8,128)(2,1)S(1)}, bf16[128,512]{1,0:T(8,128)(2,1)S(1)}, u32[]{:S(2)}, u32[]{:S(2)}) collective-permute-start(bf16[128,512]{1,0:T(8,128)(2,1)S(1)} %collective-permute-done.2), channel_id=1, source_target_pairs={{0,8},{4,60},{8,16},{12,4},{16,24},{20,12},{24,32},{28,20},{32,40}... | collective-permute-start | bytes 393224 | tf_op jit(solution)/shard_map/ppermute | solution.py:37
  25.6 1.5 %collective-permute-start.9 = (bf16[512,512]{1,0:T(8,128)(2,1)S(1)}, bf16[512,512]{1,0:T(8,128)(2,1)S(1)}, u32[]{:S(2)}, u32[]{:S(2)}) collective-permute-start(bf16[512,512]{1,0:T(8,128)(2,1)S(1)} %constant_dynamic-update-slice_fusion.refs_4_), channel_id=1, source_target_pairs={{0,8},{4,60},{8,16},{12,4},{16,24},{20,12},{24,32},{28,20},{32,40}... | collective-permute-start | bytes 1572872 | tf_op jit(solution)/shard_map/ppermute | solution.py:37
  27.1 1.5 %collective-permute-done.3 = bf16[128,512]{1,0:T(8,128)(2,1)S(1)} collective-permute-done((bf16[128,512]{1,0:T(8,128)(2,1)S(1)}, bf16[128,512]{1,0:T(8,128)(2,1)S(1)}, u32[]{:S(2)}, u32[]{:S(2)}) %collective-permute-start.3) | collective-permute-done | bytes 131104 | tf_op jit(solution)/shard_map/ppermute | solution.py:37
  28.6 3.4 %collective-permute-start.4 = (bf16[128,512]{1,0:T(8,128)(2,1)S(1)}, bf16[128,512]{1,0:T(8,128)(2,1)S(1)}, u32[]{:S(2)}, u32[]{:S(2)}) collective-permute-start(bf16[128,512]{1,0:T(8,128)(2,1)S(1)} %collective-permute-done.3), channel_id=1, source_target_pairs={{0,8},{4,60},{8,16},{12,4},{16,24},{20,12},{24,32},{28,20},{32,40}... | collective-permute-start | bytes 393224 | tf_op jit(solution)/shard_map/ppermute | solution.py:37
  33.5 2.7 %collective-permute-start.12 = (bf16[256,1024]{1,0:T(8,128)(2,1)S(1)}, bf16[256,1024]{1,0:T(8,128)(2,1)S(1)}, u32[]{:S(2)}, u32[]{:S(2)}) collective-permute-start(bf16[256,1024]{1,0:T(8,128)(2,1)S(1)} %turn_inputs.1.refs_0_), channel_id=1, source_target_pairs={{0,1},{4,7},{1,2},{5,4},{2,3},{6,5},{3,0},{7,6},{8,9},{12,15},{9,1... | collective-permute-start | bytes 1572872 | tf_op jit(solution)/shard_map/ppermute | solution.py:37
  36.2 4.8 %turn_basis.1.basis_ref = bf16[8,256,1024]{2,1,0:T(8,128)(2,1)S(1)} custom-call(s32[1]{0:T(128)} %bitcast.5.core_ref, bf16[8,2048,128]{2,1,0:T(8,128)(2,1)} %basis_ref.3, bf16[8,2048,128]{2,1,0:T(8,128)(2,1)S(1)} %collective-permute-done.5.other_ref), custom_call_target="tpu_custom_call" | custom-call | bytes 8388608 | tf_op jit(solution)/shard_map/turn_basis/pallas_call | solution.py:210
  41.1 2.0 %copy-done = bf16[8,256,1024]{2,1,0:T(8,128)(2,1)} copy-done((bf16[8,256,1024]{2,1,0:T(8,128)(2,1)}, bf16[8,256,1024]{2,1,0:T(8,128)(2,1)S(1)}, u32[]{:S(2)}) %copy-start) | copy-done | bytes 4194328
  43.1 1.6 %collective-permute-start.22 = (bf16[1024,512]{1,0:T(8,128)(2,1)S(1)}, bf16[1024,512]{1,0:T(8,128)(2,1)S(1)}, u32[]{:S(2)}, u32[]{:S(2)}) collective-permute-start(bf16[1024,512]{1,0:T(8,128)(2,1)S(1)} %constant_dynamic-update-slice_fusion.5.refs_11_), channel_id=1, source_target_pairs={{0,64},{4,196},{64,128},{68,4},{128,192},{132,68},{192,0},{196,132... | collective-permute-start | bytes 3145736 | tf_op jit(solution)/shard_map/ppermute | solution.py:37
  44.7 6.2 %gram.1.before_ref = f32[8,128]{1,0:T(8,128)S(1)} custom-call(bf16[8,2048,128]{2,1,0:T(8,128)(2,1)S(1)} %copy-done.13, f32[2048,128]{1,0:T(8,128)S(1)} %copy-done.14), custom_call_target="tpu_custom_call" | custom-call | flops 25165824 | bytes 18874368 | tf_op jit(solution)/shard_map/gram/pallas_call | solution.py:89
  51.0 2.7 %collective-permute-start.13 = (bf16[512,512]{1,0:T(8,128)(2,1)S(1)}, bf16[512,512]{1,0:T(8,128)(2,1)}, u32[]{:S(2)}, u32[]{:S(2)}) collective-permute-start(bf16[512,512]{1,0:T(8,128)(2,1)S(1)} %collective-permute-done.9.refs_5_), channel_id=1, source_target_pairs={{0,8},{4,60},{8,16},{12,4},{16,24},{20,12},{24,32},{28,20},{32,40}... | collective-permute-start | bytes 1572872 | tf_op jit(solution)/shard_map/ppermute | solution.py:37
  57.0 5.8 %collective-permute-done.13.refs_6_ = bf16[512,512]{1,0:T(8,128)(2,1)} collective-permute-done((bf16[512,512]{1,0:T(8,128)(2,1)S(1)}, bf16[512,512]{1,0:T(8,128)(2,1)}, u32[]{:S(2)}, u32[]{:S(2)}) %collective-permute-start.13) | collective-permute-done | bytes 524320 | tf_op jit(solution)/shard_map/ppermute | solution.py:37
  62.8 4.6 %collective-permute-done.14.refs_9_ = bf16[512,512]{1,0:T(8,128)(2,1)} collective-permute-done((bf16[512,512]{1,0:T(8,128)(2,1)S(1)}, bf16[512,512]{1,0:T(8,128)(2,1)}, u32[]{:S(2)}, u32[]{:S(2)}) %collective-permute-start.14) | collective-permute-done | bytes 524320 | tf_op jit(solution)/shard_map/ppermute | solution.py:37
  68.2 1.4 %collective-permute-start.16 = (bf16[256,1024]{1,0:T(8,128)(2,1)S(1)}, bf16[256,1024]{1,0:T(8,128)(2,1)}, u32[]{:S(2)}, u32[]{:S(2)}) collective-permute-start(bf16[256,1024]{1,0:T(8,128)(2,1)S(1)} %turn_inputs.1.refs_0_), channel_id=1, source_target_pairs={{0,3},{4,5},{1,0},{5,6},{2,1},{6,7},{3,2},{7,4},{8,11},{12,13},{9,... | collective-permute-start | bytes 1572872 | tf_op jit(solution)/shard_map/ppermute | solution.py:37
  69.6 1.5 %collective-permute-start.18 = (bf16[512,512]{1,0:T(8,128)(2,1)}, bf16[512,512]{1,0:T(8,128)(2,1)}, u32[]{:S(2)}, u32[]{:S(2)}) collective-permute-start(bf16[512,512]{1,0:T(8,128)(2,1)} %collective-permute-done.14.refs_9_), channel_id=1, source_target_pairs={{0,56},{4,12},{8,0},{12,20},{16,8},{20,28},{24,16},{28,36},{32,24}... | collective-permute-start | bytes 1572872 | tf_op jit(solution)/shard_map/ppermute | solution.py:37
  71.1 1.1 collective-permute-start.25
  72.3 6.6 %collective-permute-done.17.refs_7_ = bf16[512,512]{1,0:T(8,128)(2,1)} collective-permute-done((bf16[512,512]{1,0:T(8,128)(2,1)}, bf16[512,512]{1,0:T(8,128)(2,1)}, u32[]{:S(2)}, u32[]{:S(2)}) %collective-permute-start.17) | collective-permute-done | bytes 524320 | tf_op jit(solution)/shard_map/ppermute | solution.py:37
  78.9 5.0 %collective-permute-done.18.refs_8_ = bf16[512,512]{1,0:T(8,128)(2,1)} collective-permute-done((bf16[512,512]{1,0:T(8,128)(2,1)}, bf16[512,512]{1,0:T(8,128)(2,1)}, u32[]{:S(2)}, u32[]{:S(2)}) %collective-permute-start.18) | collective-permute-done | bytes 524320 | tf_op jit(solution)/shard_map/ppermute | solution.py:37
  83.9 2.2 %copy-done.1 = bf16[8,256,1024]{2,1,0:T(8,128)(2,1)S(1)} copy-done((bf16[8,256,1024]{2,1,0:T(8,128)(2,1)S(1)}, bf16[8,256,1024]{2,1,0:T(8,128)(2,1)}, u32[]{:S(2)}) %copy-start.1) | copy-done | bytes 4194328
  90.3 11.9 %near_kernel.1.before_ref = f32[8,128]{1,0:T(8,128)S(1)} custom-call(s32[4]{0:T(128)S(1)} %pad_add_fusion.place_ref, bf16[8,256,1024]{2,1,0:T(8,128)(2,1)S(1)} %copy-done.1, f32[8,128]{1,0:T(8,128)S(1)} %gram.1.before_ref, bf16[256,1024]{1,0:T(8,128)(2,1)S(1)} %turn_inputs.1.refs_0_, bf16[256,1024]{1,0:T(8,128)(2,1)S(1)} %copy-done.6, ...), custom_call_target="tpu_custom_call" | custom-call | flops 6039797760 | bytes 4194304 | tf_op jit(solution)/shard_map/near_kernel/pallas_call | solution.py:364
  102.3 6.7 %far_kernel.1 = f32[8,128]{1,0:T(8,128)S(1)} custom-call(s32[4]{0:T(128)S(1)} %pad_add_fusion.place_ref, bf16[8,256,1024]{2,1,0:T(8,128)(2,1)S(1)} %copy-done.1, f32[8,128]{1,0:T(8,128)S(1)} %near_kernel.1.before_ref, bf16[256,1024]{1,0:T(8,128)(2,1)S(1)} %turn_inputs.1.refs_0_, bf16[256,1024]{1,0:T(8,128)(2,1)S(1)} %copy-done.7, ...), custom_call_target="tpu_custom_call" | custom-call | flops 2550136832 | bytes 4194304 | tf_op jit(solution)/shard_map/far_kernel/pallas_call | solution.py:364
  109.0 13.1 %all_to_all.20 = f32[16,8,128]{2,1,0:T(8,128)S(1)} all-to-all(f32[16,8,128]{2,1,0:T(8,128)S(1)} %broadcast_in_dim.13), channel_id=1, replica_groups=mesh['y'=4,'z'=8,'core'=2,'x'=4] {'z','core'}, dimensions={0} | all-to-all | bytes 131072 | tf_op jit(solution)/shard_map/all_to_all | solution.py:50
  122.8 7.3 %all-to-all-start.3 = ((f32[16,8,128]{2,1,0:T(8,128)}), f32[16,8,128]{2,1,0:T(8,128)S(1)}, u32[]{:S(2)}, u32[]{:S(2)}) async-start(f32[16,8,128]{2,1,0:T(8,128)} %broadcast_in_dim.14), calls=%async_computation.3 | async-start | bytes 131072 | tf_op jit(solution)/shard_map/all_to_all | solution.py:50
  130.1 6.4 %all-to-all-done.3 = f32[16,8,128]{2,1,0:T(8,128)S(1)} async-done(((f32[16,8,128]{2,1,0:T(8,128)}), f32[16,8,128]{2,1,0:T(8,128)S(1)}, u32[]{:S(2)}, u32[]{:S(2)}) %all-to-all-start.3) | async-done | bytes 65568 | tf_op jit(solution)/shard_map/all_to_all | solution.py:50
  136.6 4.7 %finish.3 = (bf16[2048,128]{1,0:T(8,128)(2,1)}, f32[1,9]{1,0:T(1,128)}, f32[8,4]{1,0:T(8,128)S(1)}, s32[1]{0:T(128)}) custom-call(f32[8,128]{1,0:T(8,128)S(1)} %reduce_sum.41.scalars_ref.sums_ref, f32[1]{0:T(128)} %constant.38.clone.1.squares_ref, f32[8,128]{1,0:T(8,128)S(1)} %reduce_sum.41.scalars_ref.sums_ref, f32[128,128]{1,0:T(8,128)S(1)} %pad.4.rotation_ref, ...), custom_call_target="tpu_custom_call" | custom-call | flops 6291456 | bytes 6291456 | tf_op jit(solution)/shard_map/finish/pallas_call | solution.py:187
  (86 shorter events, 13.0 us)
Async XLA Ops:
  0.6 4.7 %collective-permute-start = (bf16[64,2048]{1,0:T(8,128)(2,1)}, bf16[64,2048]{1,0:T(8,128)(2,1)S(1)}, u32[]{:S(2)}, u32[]{:S(2)}) collective-permute-start(bf16[64,2048]{1,0:T(8,128)(2,1)} %param.9), channel_id=1, source_target_pairs={{0,4},{4,0},{1,5},{5,1},{2,6},{6,2},{3,7},{7,3},{8,12},{12,8},{9,1... | collective-permute-start | bytes 786440 | tf_op jit(solution)/shard_map/ppermute | solution.py:41
  5.4 5.9 %collective-permute-start.1 = (bf16[128,512]{1,0:T(8,128)(2,1)S(1)}, bf16[128,512]{1,0:T(8,128)(2,1)S(1)}, u32[]{:S(2)}, u32[]{:S(2)}) collective-permute-start(bf16[128,512]{1,0:T(8,128)(2,1)S(1)} %pad_maximum_fusion), channel_id=1, source_target_pairs={{0,8},{4,60},{8,16},{12,4},{16,24},{20,12},{24,32},{28,20},{32,40}... | collective-permute-start | bytes 393224 | tf_op jit(solution)/shard_map/ppermute | solution.py:37
  11.2 22.2 %collective-permute-start.5 = (bf16[8,2048,128]{2,1,0:T(8,128)(2,1)}, bf16[8,2048,128]{2,1,0:T(8,128)(2,1)S(1)}, u32[]{:S(2)}, u32[]{:S(2)}) collective-permute-start(bf16[8,2048,128]{2,1,0:T(8,128)(2,1)} %basis_ref.3), channel_id=1, source_target_pairs={{0,4},{4,0},{1,5},{5,1},{2,6},{6,2},{3,7},{7,3},{8,12},{12,8},{9,1... | collective-permute-start | bytes 12582920 | tf_op jit(solution)/shard_map/ppermute | solution.py:41
  12.9 5.5 %collective-permute-start.6 = (bf16[128,512]{1,0:T(8,128)(2,1)S(1)}, bf16[128,512]{1,0:T(8,128)(2,1)S(1)}, u32[]{:S(2)}, u32[]{:S(2)}) collective-permute-start(bf16[128,512]{1,0:T(8,128)(2,1)S(1)} %pad_maximum_fusion.1), channel_id=1, source_target_pairs={{0,64},{4,196},{64,128},{68,4},{128,192},{132,68},{192,0},{196,132... | collective-permute-start | bytes 393224 | tf_op jit(solution)/shard_map/ppermute | solution.py:37
  15.7 9.9 %collective-permute-start.8 = (bf16[128,512]{1,0:T(8,128)(2,1)S(1)}, bf16[128,512]{1,0:T(8,128)(2,1)S(1)}, u32[]{:S(2)}, u32[]{:S(2)}) collective-permute-start(bf16[128,512]{1,0:T(8,128)(2,1)S(1)} %pad_maximum_fusion.1), channel_id=1, source_target_pairs={{0,192},{4,68},{64,0},{68,132},{128,64},{132,196},{192,128},{196,4... | collective-permute-start | bytes 393224 | tf_op jit(solution)/shard_map/ppermute | solution.py:37
  15.7 6.1 %collective-permute-start.19 = (bf16[128,512]{1,0:T(8,128)(2,1)S(1)}, bf16[128,512]{1,0:T(8,128)(2,1)S(1)}, u32[]{:S(2)}, u32[]{:S(2)}) collective-permute-start(bf16[128,512]{1,0:T(8,128)(2,1)S(1)} %pad_maximum_fusion), channel_id=1, source_target_pairs={{0,56},{4,12},{8,0},{12,20},{16,8},{20,28},{24,16},{28,36},{32,24}... | collective-permute-start | bytes 393224 | tf_op jit(solution)/shard_map/ppermute | solution.py:37
  15.7 6.4 %collective-permute-start.2 = (bf16[128,512]{1,0:T(8,128)(2,1)S(1)}, bf16[128,512]{1,0:T(8,128)(2,1)S(1)}, u32[]{:S(2)}, u32[]{:S(2)}) collective-permute-start(bf16[128,512]{1,0:T(8,128)(2,1)S(1)} %collective-permute-done.1), channel_id=1, source_target_pairs={{0,8},{4,60},{8,16},{12,4},{16,24},{20,12},{24,32},{28,20},{32,40}... | collective-permute-start | bytes 393224 | tf_op jit(solution)/shard_map/ppermute | solution.py:37
  18.4 5.3 %collective-permute-start.7 = (bf16[128,512]{1,0:T(8,128)(2,1)S(1)}, bf16[128,512]{1,0:T(8,128)(2,1)S(1)}, u32[]{:S(2)}, u32[]{:S(2)}) collective-permute-start(bf16[128,512]{1,0:T(8,128)(2,1)S(1)} %collective-permute-done.6), channel_id=1, source_target_pairs={{0,64},{4,196},{64,128},{68,4},{128,192},{132,68},{192,0},{196,132... | collective-permute-start | bytes 393224 | tf_op jit(solution)/shard_map/ppermute | solution.py:37
  21.8 10.3 %collective-permute-start.11 = (bf16[1024,128]{1,0:T(8,128)(2,1)}, bf16[1024,128]{1,0:T(8,128)(2,1)S(1)}, u32[]{:S(2)}, u32[]{:S(2)}) collective-permute-start(bf16[1024,128]{1,0:T(8,128)(2,1)} %own_ref.1), channel_id=1, source_target_pairs={{0,4},{4,0},{1,5},{5,1},{2,6},{6,2},{3,7},{7,3},{8,12},{12,8},{9,1... | collective-permute-start | bytes 786440 | tf_op jit(solution)/shard_map/ppermute | solution.py:41
  22.1 9.9 %collective-permute-start.20 = (bf16[128,512]{1,0:T(8,128)(2,1)S(1)}, bf16[128,512]{1,0:T(8,128)(2,1)S(1)}, u32[]{:S(2)}, u32[]{:S(2)}) collective-permute-start(bf16[128,512]{1,0:T(8,128)(2,1)S(1)} %collective-permute-done.19), channel_id=1, source_target_pairs={{0,56},{4,12},{8,0},{12,20},{16,8},{20,28},{24,16},{28,36},{32,24}... | collective-permute-start | bytes 393224 | tf_op jit(solution)/shard_map/ppermute | solution.py:37
  23.7 4.9 %collective-permute-start.3 = (bf16[128,512]{1,0:T(8,128)(2,1)S(1)}, bf16[128,512]{1,0:T(8,128)(2,1)S(1)}, u32[]{:S(2)}, u32[]{:S(2)}) collective-permute-start(bf16[128,512]{1,0:T(8,128)(2,1)S(1)} %collective-permute-done.2), channel_id=1, source_target_pairs={{0,8},{4,60},{8,16},{12,4},{16,24},{20,12},{24,32},{28,20},{32,40}... | collective-permute-start | bytes 393224 | tf_op jit(solution)/shard_map/ppermute | solution.py:37
  25.6 25.3 %collective-permute-start.9 = (bf16[512,512]{1,0:T(8,128)(2,1)S(1)}, bf16[512,512]{1,0:T(8,128)(2,1)S(1)}, u32[]{:S(2)}, u32[]{:S(2)}) collective-permute-start(bf16[512,512]{1,0:T(8,128)(2,1)S(1)} %constant_dynamic-update-slice_fusion.refs_4_), channel_id=1, source_target_pairs={{0,8},{4,60},{8,16},{12,4},{16,24},{20,12},{24,32},{28,20},{32,40}... | collective-permute-start | bytes 1572872 | tf_op jit(solution)/shard_map/ppermute | solution.py:37
  28.6 14.4 %collective-permute-start.4 = (bf16[128,512]{1,0:T(8,128)(2,1)S(1)}, bf16[128,512]{1,0:T(8,128)(2,1)S(1)}, u32[]{:S(2)}, u32[]{:S(2)}) collective-permute-start(bf16[128,512]{1,0:T(8,128)(2,1)S(1)} %collective-permute-done.3), channel_id=1, source_target_pairs={{0,8},{4,60},{8,16},{12,4},{16,24},{20,12},{24,32},{28,20},{32,40}... | collective-permute-start | bytes 393224 | tf_op jit(solution)/shard_map/ppermute | solution.py:37
  32.1 11.0 %collective-permute-start.21 = (bf16[128,512]{1,0:T(8,128)(2,1)S(1)}, bf16[128,512]{1,0:T(8,128)(2,1)S(1)}, u32[]{:S(2)}, u32[]{:S(2)}) collective-permute-start(bf16[128,512]{1,0:T(8,128)(2,1)S(1)} %collective-permute-done.20), channel_id=1, source_target_pairs={{0,56},{4,12},{8,0},{12,20},{16,8},{20,28},{24,16},{28,36},{32,24}... | collective-permute-start | bytes 393224 | tf_op jit(solution)/shard_map/ppermute | solution.py:37
  32.2 18.8 %collective-permute-start.10 = (bf16[512,512]{1,0:T(8,128)(2,1)S(1)}, bf16[512,512]{1,0:T(8,128)(2,1)S(1)}, u32[]{:S(2)}, u32[]{:S(2)}) collective-permute-start(bf16[512,512]{1,0:T(8,128)(2,1)S(1)} %constant_dynamic-update-slice_fusion.refs_4_), channel_id=1, source_target_pairs={{0,56},{4,12},{8,0},{12,20},{16,8},{20,28},{24,16},{28,36},{32,24}... | collective-permute-start | bytes 1572872 | tf_op jit(solution)/shard_map/ppermute | solution.py:37
  33.4 11.3 %copy-start.13 = (bf16[8,2048,128]{2,1,0:T(8,128)(2,1)S(1)}, bf16[8,2048,128]{2,1,0:T(8,128)(2,1)}, u32[]{:S(2)}) copy-start(bf16[8,2048,128]{2,1,0:T(8,128)(2,1)} %basis_ref.3) | copy-start | bytes 12582916
  33.5 21.8 %collective-permute-start.12 = (bf16[256,1024]{1,0:T(8,128)(2,1)S(1)}, bf16[256,1024]{1,0:T(8,128)(2,1)S(1)}, u32[]{:S(2)}, u32[]{:S(2)}) collective-permute-start(bf16[256,1024]{1,0:T(8,128)(2,1)S(1)} %turn_inputs.1.refs_0_), channel_id=1, source_target_pairs={{0,1},{4,7},{1,2},{5,4},{2,3},{6,5},{3,0},{7,6},{8,9},{12,15},{9,1... | collective-permute-start | bytes 1572872 | tf_op jit(solution)/shard_map/ppermute | solution.py:37
  43.1 28.0 %collective-permute-start.22 = (bf16[1024,512]{1,0:T(8,128)(2,1)S(1)}, bf16[1024,512]{1,0:T(8,128)(2,1)S(1)}, u32[]{:S(2)}, u32[]{:S(2)}) collective-permute-start(bf16[1024,512]{1,0:T(8,128)(2,1)S(1)} %constant_dynamic-update-slice_fusion.5.refs_11_), channel_id=1, source_target_pairs={{0,64},{4,196},{64,128},{68,4},{128,192},{132,68},{192,0},{196,132... | collective-permute-start | bytes 3145736 | tf_op jit(solution)/shard_map/ppermute | solution.py:37
  51.0 11.9 %collective-permute-start.13 = (bf16[512,512]{1,0:T(8,128)(2,1)S(1)}, bf16[512,512]{1,0:T(8,128)(2,1)}, u32[]{:S(2)}, u32[]{:S(2)}) collective-permute-start(bf16[512,512]{1,0:T(8,128)(2,1)S(1)} %collective-permute-done.9.refs_5_), channel_id=1, source_target_pairs={{0,8},{4,60},{8,16},{12,4},{16,24},{20,12},{24,32},{28,20},{32,40}... | collective-permute-start | bytes 1572872 | tf_op jit(solution)/shard_map/ppermute | solution.py:37
  54.4 12.9 %collective-permute-start.14 = (bf16[512,512]{1,0:T(8,128)(2,1)S(1)}, bf16[512,512]{1,0:T(8,128)(2,1)}, u32[]{:S(2)}, u32[]{:S(2)}) collective-permute-start(bf16[512,512]{1,0:T(8,128)(2,1)S(1)} %collective-permute-done.10.refs_10_), channel_id=1, source_target_pairs={{0,56},{4,12},{8,0},{12,20},{16,8},{20,28},{24,16},{28,36},{32,24}... | collective-permute-start | bytes 1572872 | tf_op jit(solution)/shard_map/ppermute | solution.py:37
  55.2 12.1 %collective-permute-start.15 = (bf16[256,1024]{1,0:T(8,128)(2,1)S(1)}, bf16[256,1024]{1,0:T(8,128)(2,1)S(1)}, u32[]{:S(2)}, u32[]{:S(2)}) collective-permute-start(bf16[256,1024]{1,0:T(8,128)(2,1)S(1)} %collective-permute-done.12.refs_1_), channel_id=1, source_target_pairs={{0,1},{4,7},{1,2},{5,4},{2,3},{6,5},{3,0},{7,6},{8,9},{12,15},{9,1... | collective-permute-start | bytes 1572872 | tf_op jit(solution)/shard_map/ppermute | solution.py:37
  57.0 26.9 %collective-permute-start.23 = (bf16[1024,512]{1,0:T(8,128)(2,1)S(1)}, bf16[1024,512]{1,0:T(8,128)(2,1)}, u32[]{:S(2)}, u32[]{:S(2)}) collective-permute-start(bf16[1024,512]{1,0:T(8,128)(2,1)S(1)} %constant_dynamic-update-slice_fusion.5.refs_11_), channel_id=1, source_target_pairs={{0,192},{4,68},{64,0},{68,132},{128,64},{132,196},{192,128},{196,4... | collective-permute-start | bytes 3145736 | tf_op jit(solution)/shard_map/ppermute | solution.py:37
  68.2 10.7 %collective-permute-start.17 = (bf16[512,512]{1,0:T(8,128)(2,1)}, bf16[512,512]{1,0:T(8,128)(2,1)}, u32[]{:S(2)}, u32[]{:S(2)}) collective-permute-start(bf16[512,512]{1,0:T(8,128)(2,1)} %collective-permute-done.13.refs_6_), channel_id=1, source_target_pairs={{0,8},{4,60},{8,16},{12,4},{16,24},{20,12},{24,32},{28,20},{32,40}... | collective-permute-start | bytes 1572872 | tf_op jit(solution)/shard_map/ppermute | solution.py:37
  68.2 10.7 %collective-permute-start.16 = (bf16[256,1024]{1,0:T(8,128)(2,1)S(1)}, bf16[256,1024]{1,0:T(8,128)(2,1)}, u32[]{:S(2)}, u32[]{:S(2)}) collective-permute-start(bf16[256,1024]{1,0:T(8,128)(2,1)S(1)} %turn_inputs.1.refs_0_), channel_id=1, source_target_pairs={{0,3},{4,5},{1,0},{5,6},{2,1},{6,7},{3,2},{7,4},{8,11},{12,13},{9,... | collective-permute-start | bytes 1572872 | tf_op jit(solution)/shard_map/ppermute | solution.py:37
  69.6 14.3 %collective-permute-start.18 = (bf16[512,512]{1,0:T(8,128)(2,1)}, bf16[512,512]{1,0:T(8,128)(2,1)}, u32[]{:S(2)}, u32[]{:S(2)}) collective-permute-start(bf16[512,512]{1,0:T(8,128)(2,1)} %collective-permute-done.14.refs_9_), channel_id=1, source_target_pairs={{0,56},{4,12},{8,0},{12,20},{16,8},{20,28},{24,16},{28,36},{32,24}... | collective-permute-start | bytes 1572872 | tf_op jit(solution)/shard_map/ppermute | solution.py:37
  71.1 31.1 %collective-permute-start.25 = (bf16[1024,512]{1,0:T(8,128)(2,1)S(1)}, bf16[1024,512]{1,0:T(8,128)(2,1)}, u32[]{:S(2)}, u32[]{:S(2)}) collective-permute-start(bf16[1024,512]{1,0:T(8,128)(2,1)S(1)} %collective-permute-done.22.refs_12_), channel_id=1, source_target_pairs={{0,64},{4,196},{64,128},{68,4},{128,192},{132,68},{192,0},{196,132... | collective-permute-start | bytes 3145736 | tf_op jit(solution)/shard_map/ppermute | solution.py:37
  78.9 23.3 %collective-permute-start.24 = (bf16[512,512]{1,0:T(8,128)(2,1)}, bf16[512,512]{1,0:T(8,128)(2,1)S(1)}, u32[]{:S(2)}, u32[]{:S(2)}) collective-permute-start(bf16[512,512]{1,0:T(8,128)(2,1)} %collective-permute-done.17.refs_7_), channel_id=1, source_target_pairs={{0,8},{4,60},{8,16},{12,4},{16,24},{20,12},{24,32},{28,20},{32,40}... | collective-permute-start | bytes 1572872 | tf_op jit(solution)/shard_map/ppermute | solution.py:37
  90.3 12.0 %copy-start.7 = (bf16[256,1024]{1,0:T(8,128)(2,1)S(1)}, bf16[256,1024]{1,0:T(8,128)(2,1)}, u32[]{:S(2)}) copy-start(bf16[256,1024]{1,0:T(8,128)(2,1)} %copy-done.5) | copy-start | bytes 1572868
  90.3 12.0 %copy-start.12 = (bf16[256,1024]{1,0:T(8,128)(2,1)S(1)}, bf16[256,1024]{1,0:T(8,128)(2,1)}, u32[]{:S(2)}) copy-start(bf16[256,1024]{1,0:T(8,128)(2,1)} %copy-done.10) | copy-start | bytes 1572868
  102.2 27.8 %copy-start.16 = (f32[8,4]{0,1:T(4,128)S(1)}, f32[8,4]{0,1:T(4,128)}, u32[]{:S(2)}) copy-start(f32[8,4]{0,1:T(4,128)} %param.11) | copy-start | bytes 388
  108.9 33.0 %copy-start.15 = (f32[2048,128]{1,0:T(8,128)S(1)}, f32[2048,128]{1,0:T(8,128)}, u32[]{:S(2)}) copy-start(f32[2048,128]{1,0:T(8,128)} %field_ref.3) | copy-start | bytes 3145732
  122.8 13.8 %all-to-all-start.3 = ((f32[16,8,128]{2,1,0:T(8,128)}), f32[16,8,128]{2,1,0:T(8,128)S(1)}, u32[]{:S(2)}, u32[]{:S(2)}) async-start(f32[16,8,128]{2,1,0:T(8,128)} %broadcast_in_dim.14), calls=%async_computation.3 | async-start | bytes 131072 | tf_op jit(solution)/shard_map/all_to_all | solution.py:50
  (12 other events, 23.8 us)

commit v2 on v1

v2 whole, which is shorter than its diff:
```python
import functools

import jax
import jax.numpy as jnp
from jax import lax
from jax.experimental import pallas as pl
from jax.experimental.pallas import tpu as pltpu
from jax.sharding import PartitionSpec as P

LEN = 512
SEQS = 8
K = 8
TOP = 4
YS = 4
ZS = 8
XS = 4
CHIP = 128
WIDE = 512
GRAM = 16
DOTS = GRAM + K
SELF = DOTS + 1
PAIRS = [(k, l) for k in range(K) for l in range(k, K)]
HIGHEST = lax.Precision.HIGHEST
MB = 2**20


def toward(value, axis, sign):
    size = lax.axis_size(axis)
    axes = ("core", axis) if axis == "x" else (axis, "core")

    def place(i, core):
        return core * size + i if axis == "x" else i * 2 + core

    pairs = [
        (place(i, core), place((i + (sign if core == 0 else -sign)) % size, core))
        for i in range(size)
        for core in range(2)
    ]
    return lax.ppermute(value, axes, pairs)


def swap_core(value):
    return lax.ppermute(value, "core", [(0, 1), (1, 0)])


def together(*values):
    return lax.optimization_barrier(values)


def sum_over(value, axes):
    copies = jnp.broadcast_to(value[None], (lax.axis_size(axes),) + value.shape)
    return jnp.sum(lax.all_to_all(copies, axes, 0, 0), axis=0)


def sum_everywhere(value):
    return sum_over(sum_over(value, ("z", "core")), ("y", "x"))


def cells():
    shape = (8, 128)
    return (lax.broadcasted_iota(jnp.int32, shape, axis) for axis in range(2))


def total_of(value, axis=None):
    if axis is None:
        return total_of(total_of(value, 0), 1)
    return jnp.sum(value, axis=axis, keepdims=True)


def gram_kernel(basis_ref, field_ref, out_ref):
    count = len(PAIRS) + K + 1

    def step(at, totals):
        rows = pl.ds(pl.multiple_of(at * 16, 16), 16)
        stack = [basis_ref[k, rows, :].astype(jnp.float32) for k in range(K)]
        field = field_ref[rows, :]
        terms = [stack[k] * stack[l] for k, l in PAIRS] + [stack[k] * field for k in range(K)]
        terms.append(field * field)
        return tuple(t + (a[:8] + a[8:]) for t, a in zip(totals, terms))

    zero = jnp.zeros((8, 128), jnp.float32)
    totals = lax.fori_loop(0, field_ref.shape[0] // 16, step, (zero,) * count)
    totals = [total_of(total) for total in totals]
    row, lane = cells()
    out = jnp.where((row == 0) & (lane == SELF), totals[-1], 0.0)
    for (k, l), total in zip(PAIRS, totals):
        here = ((row == k) & (lane == GRAM + l)) | ((row == l) & (lane == GRAM + k))
        out = jnp.where(here, total, out)
    for k in range(K):
        out = jnp.where((row == k) & (lane == DOTS), totals[len(PAIRS) + k], out)
    out_ref[...] = out


def gram(basis, field):
    return pl.pallas_call(
        gram_kernel,
        out_shape=jax.ShapeDtypeStruct((8, 128), jnp.float32),
        in_specs=[pl.BlockSpec(memory_space=pltpu.VMEM)] * 2,
        out_specs=pl.BlockSpec(memory_space=pltpu.VMEM),
        compiler_params=pltpu.CompilerParams(vmem_limit_bytes=8 * MB),
        cost_estimate=pl.CostEstimate(flops=24 * MB, bytes_accessed=18 * MB, transcendentals=0),
        name="gram",
    )(basis, field)


def weigh(sums):
    row, lane = cells()
    overlaps = jnp.where((lane >= GRAM) & (lane < GRAM + K), sums, 0.0)

    def times(column):
        across = total_of(jnp.where(lane - GRAM == row, column, 0.0), 0)
        return total_of(overlaps * across, 1)

    first = total_of(jnp.where(lane == DOTS, sums, 0.0), 1)
    whole = total_of(jnp.where((lane == SELF) & (row == 0), sums, 0.0))
    weights = first + (first - times(first))
    squares = whole + total_of(weights * (times(weights) - (first + first)), 0)
    return weights, squares, whole


def spread(weights):
    return [jnp.broadcast_to(weights[k : k + 1], (16, 128)) for k in range(K)]


def take_off(weights, basis_ref, field_ref, rows):
    rest = field_ref[rows, :]
    for k in range(K):
        rest = rest - weights[k] * basis_ref[k, rows, :].astype(jnp.float32)
    return rest


def squares_kernel(sums_ref, basis_ref, field_ref, out_ref):
    weights = spread(weigh(sums_ref[...])[0])

    def step(at, total):
        rest = take_off(weights, basis_ref, field_ref, pl.ds(pl.multiple_of(at * 16, 16), 16))
        square = rest * rest
        return total + (square[:8] + square[8:])

    out_ref[...] = lax.fori_loop(
        0, field_ref.shape[0] // 16, step, jnp.zeros((8, 128), jnp.float32)
    )


def squared_length(sums, basis, field):
    vmem = pl.BlockSpec(memory_space=pltpu.VMEM)
    parts = pl.pallas_call(
        squares_kernel,
        out_shape=jax.ShapeDtypeStruct((8, 128), jnp.float32),
        in_specs=[vmem] * 3,
        out_specs=vmem,
        compiler_params=pltpu.CompilerParams(vmem_limit_bytes=8 * MB),
        name="squares",
    )(sums, basis, field)
    return jnp.sum(sum_everywhere(parts))


def finish_kernel(given, squares_ref, sums_ref, rotation_ref, basis_ref, field_ref, *out_refs):
    new_ref, hessenberg_ref, influence_ref, little_ref, spread_ref = out_refs

    @pl.when(pl.program_id(0) == 0)
    def _():
        sums = sums_ref[...]
        column, squares, whole = weigh(sums)
        little_ref[0] = (squares * 256.0 < whole).astype(jnp.int32)[0, 0]
        if given:
            squares = squares_ref[...]
        length = jnp.sqrt(squares + 1e-06)
        for k, weight in enumerate(spread(column)):
            spread_ref[k] = weight
        spread_ref[K] = jnp.broadcast_to(1.0 / length, (16, 128))
        row, lane = cells()
        across = total_of(jnp.where(lane == row, column, 0.0), 0)
        hessenberg_ref[...] = jnp.where(lane[:1] == K, length, across)[:, : K + 1]
        influence_ref[...] = lax.dot_general(
            rotation_ref[...],
            jnp.where(lane < K, sums, 0.0),
            (((1,), (1,)), ((), ())),
            precision=HIGHEST,
            preferred_element_type=jnp.float32,
        )[:TOP]

    weights = [spread_ref[k] for k in range(K)]
    scale = spread_ref[K]

    def step(at, carry):
        rows = pl.ds(pl.multiple_of(at * 16, 16), 16)
        rest = take_off(weights, basis_ref, field_ref, rows)
        new_ref[rows, :] = (rest * scale).astype(jnp.bfloat16)
        return carry

    lax.fori_loop(0, field_ref.shape[0] // 16, step, 0, unroll=4)


def finish(given, squares, sums, rotation, basis, field):
    vmem = pl.BlockSpec(memory_space=pltpu.VMEM)
    rows = field.shape[0] // 4
    block = pl.BlockSpec((rows, 128), lambda t: (t, 0))
    return pl.pallas_call(
        functools.partial(finish_kernel, given),
        out_shape=[
            jax.ShapeDtypeStruct(field.shape, jnp.bfloat16),
            jax.ShapeDtypeStruct((1, K + 1), jnp.float32),
            jax.ShapeDtypeStruct((TOP, SEQS), jnp.float32),
            jax.ShapeDtypeStruct((1,), jnp.int32),
        ],
        grid=(4,),
        in_specs=[vmem] * 3 + [pl.BlockSpec((K, rows, 128), lambda t: (0, t, 0)), block],
        out_specs=[block, vmem, vmem, pl.BlockSpec(memory_space=pltpu.SMEM)],
        scratch_shapes=[pltpu.VMEM((K + 1, 16, 128), jnp.float32)],
        compiler_params=pltpu.CompilerParams(vmem_limit_bytes=8 * MB),
        cost_estimate=pl.CostEstimate(flops=6 * MB, bytes_accessed=6 * MB, transcendentals=0),
        name="finish",
    )(squares, sums, rotation, basis, field)


def turn_basis_kernel(core_ref, own_ref, other_ref, left_ref, right_ref):
    for at, ref in enumerate((own_ref, other_ref)):
        turned = ref[0].T
        left_ref[0, at * 128 : (at + 1) * 128, :] = turned[:, :WIDE]
        right_ref[0, at * 128 : (at + 1) * 128, :] = turned[:, WIDE:]


def turn_basis(core, basis, other):
    half = other.shape[1] // 2
    return pl.pallas_call(
        turn_basis_kernel,
        out_shape=[jax.ShapeDtypeStruct((K, 256, WIDE), jnp.bfloat16)] * 2,
        grid_spec=pltpu.PrefetchScalarGridSpec(
            num_scalar_prefetch=1,
            grid=(K,),
            in_specs=[pl.BlockSpec((1, half, 128), lambda k, core: (k, core[0], 0))] * 2,
            out_specs=[pl.BlockSpec((1, 256, WIDE), lambda k, core: (k, 0, 0))] * 2,
        ),
        compiler_params=pltpu.CompilerParams(vmem_limit_bytes=8 * MB),
        cost_estimate=pl.CostEstimate(flops=0, bytes_accessed=8 * MB, transcendentals=0),
        name="turn_basis",
    )(core, basis, other)


def turn_inputs_kernel(core_ref, own_ref, other_ref, out_ref):
    for at, ref in enumerate((own_ref, other_ref)):
        parts = ref[...].reshape(-1, 2, CHIP // 2, 128)
        turned = jnp.concatenate([parts[:, 1:], parts[:, :1]], axis=1)
        parts = jnp.where(core_ref[0] == 1, turned, parts)
        out_ref[at * 128 : (at + 1) * 128, :] = parts.reshape(-1, 128).T


def turn_inputs(core, own, other):
    vmem = pl.BlockSpec(memory_space=pltpu.VMEM)
    return pl.pallas_call(
        turn_inputs_kernel,
        out_shape=jax.ShapeDtypeStruct((256, own.shape[0]), jnp.bfloat16),
        in_specs=[pl.BlockSpec(memory_space=pltpu.SMEM), vmem, vmem],
        out_specs=vmem,
        compiler_params=pltpu.CompilerParams(vmem_limit_bytes=8 * MB),
        cost_estimate=pl.CostEstimate(flops=0, bytes_accessed=MB, transcendentals=0),
        name="turn_inputs",
    )(core, own, other)


def keep_parts(parts_ref, slot, tile):
    high = tile.astype(jnp.bfloat16)
    parts_ref[2 * slot] = high
    parts_ref[2 * slot + 1] = (tile - high.astype(jnp.float32)).astype(jnp.bfloat16)


def products(parts_ref, count, basis_ref):
    cross = jnp.zeros((count * 64, 256), jnp.float32)
    for at in range(8):
        rows = slice(at * 32, (at + 1) * 32)
        tiles = parts_ref[: 2 * count, rows, :].reshape(count * 64, WIDE)
        basis = basis_ref[:, rows, :].reshape(256, WIDE)
        cross = cross + lax.dot_general(
            tiles, basis, (((1,), (1,)), ((), ())), preferred_element_type=jnp.float32
        )
    row = lax.broadcasted_iota(jnp.int32, cross.shape, 0)
    lane = lax.broadcasted_iota(jnp.int32, cross.shape, 1)
    cross = jnp.where(lax.rem(row, 32) == lax.rem(lane, 32), cross, 0.0)
    return jnp.sum(cross.reshape(count, 64, 256), axis=1)


def add_products(out_ref, sums, owners):
    owner = lax.broadcasted_iota(jnp.int32, (256, 128), 0) // 32
    pick = (owner == lax.broadcasted_iota(jnp.int32, (256, 128), 1)).astype(jnp.float32)
    sums = jnp.dot(sums, pick, precision=HIGHEST, preferred_element_type=jnp.float32)
    for at, owner in enumerate(owners):
        out_ref[pl.ds(owner, 1), :] += sums[at : at + 1]


class Place:
    def __init__(self, ref):
        self.y, self.z, self.x, self.sign = (ref[i] for i in range(4))

    def y_slot(self, y):
        return lax.rem(self.sign * (self.y - y) + 2 * YS, YS)

    def z_slot(self, z):
        return lax.rem(self.sign * (self.z - z) + 2 * ZS, ZS)

    def x_slot(self, x):
        return lax.rem(self.sign * (self.x - x) + 2 * XS, XS)

    def y_of(self, slot):
        return lax.rem(self.y - self.sign * slot + 2 * YS, YS)


def chip_rows(slot):
    return pl.ds(pl.multiple_of(slot * CHIP, CHIP), CHIP)


def example_tile(place, inputs_ref, y, part, block):
    grads = jnp.concatenate([block(place.z_slot(part * 4 + j)) for j in range(4)], axis=0)
    cols = pl.ds(pl.multiple_of(part * LEN, LEN), LEN)
    inputs = inputs_ref[place.x_slot(y), :, cols]
    return jnp.dot(inputs, grads, preferred_element_type=jnp.float32)


def rows_example(place, inputs_ref, parts_ref, at, slot_y, ref):
    y = place.y_of(slot_y)
    for part in range(2):
        tile = example_tile(place, inputs_ref, y, part, lambda d: ref[chip_rows(d), :])
        keep_parts(parts_ref, at + part, tile)
    return [y * 2, y * 2 + 1]


def fetch(pairs, sems):
    copies = [pltpu.make_async_copy(a, b, sems.at[at]) for at, (a, b) in enumerate(pairs)]
    for copy in copies:
        copy.start()
    return copies


def right_kernel(place_ref, far_basis_ref, before_ref, *refs):
    rights, out_ref, inputs_ref, parts_ref, basis_ref, right_ref, sems = refs[4:7], *refs[7:]
    pairs = [(ref, inputs_ref.at[slot]) for slot, ref in enumerate(refs[:4])]
    pairs += [(ref, right_ref.at[at]) for at, ref in enumerate(rights)]
    copies = fetch(pairs + [(far_basis_ref, basis_ref)], sems)
    inputs, copies, basis = copies[:4], copies[4:-1], copies[-1]
    place = Place(place_ref)
    out_ref[...] = before_ref[...]
    for copy in inputs:
        copy.wait()
    owners = []
    for at, slot_y in enumerate((0, 1, 3)):
        copies[at].wait()
        owners += rows_example(place, inputs_ref, parts_ref, 2 * at, slot_y, right_ref.at[at])
    basis.wait()
    add_products(out_ref, products(parts_ref, 6, basis_ref), owners)


def left_kernel(place_ref, far_basis_ref, before_ref, *refs):
    lefts, out_ref, inputs_ref, parts_ref, basis_ref, left_ref, sems = refs[4:11], *refs[11:]
    pairs = [(ref, inputs_ref.at[slot]) for slot, ref in enumerate(refs[:4])]
    pairs += [(ref, left_ref.at[slot]) for slot, ref in zip((0, 1, 2, 3, 5, 6, 7), lefts)]
    copies = fetch(pairs + [(far_basis_ref, basis_ref)], sems)
    place = Place(place_ref)
    out_ref[...] = before_ref[...]
    left_ref[4] = jnp.zeros_like(left_ref[4])
    for copy in copies[:-1]:
        copy.wait()
    for example in range(SEQS):
        y, part = example // 2, example % 2
        rows = chip_rows(place.y_slot(y))
        tile = example_tile(place, inputs_ref, y, part, lambda d: left_ref[d, rows, :])
        keep_parts(parts_ref, example, tile)
    copies[-1].wait()
    add_products(out_ref, products(parts_ref, SEQS, basis_ref), range(SEQS))


def far_kernel(place_ref, left_basis_ref, right_basis_ref, before_ref, *refs):
    left_ref, right_ref, out_ref, inputs_ref, parts_ref = refs[4:]
    place = Place(place_ref)
    out_ref[...] = before_ref[...]
    for slot in range(XS):
        inputs_ref[slot] = refs[slot][...]
    z = lax.rem(place.z + 4, ZS)
    owners = []
    for slot_y in range(YS):
        y = place.y_of(slot_y)
        tile = jnp.dot(
            inputs_ref[place.x_slot(y), :, chip_rows(z)],
            left_ref[slot_y * CHIP : (slot_y + 1) * CHIP, :],
            preferred_element_type=jnp.float32,
        )
        keep_parts(parts_ref, slot_y, tile)
        owners.append(y * 2 + z // 4)
    left = products(parts_ref, YS, left_basis_ref)
    owners += rows_example(place, inputs_ref, parts_ref, 0, 2, right_ref)
    right = products(parts_ref, 2, right_basis_ref)
    add_products(out_ref, jnp.concatenate([left, right]), owners)


def project(kernel, place, inputs, bases, before, grads, space, slots, scratch):
    vmem, large = pl.BlockSpec(memory_space=pltpu.VMEM), pl.BlockSpec(memory_space=space)
    return pl.pallas_call(
        kernel,
        out_shape=jax.ShapeDtypeStruct((8, 128), jnp.float32),
        in_specs=[pl.BlockSpec(memory_space=pltpu.SMEM)]
        + [large] * len(bases)
        + [vmem]
        + [large] * (len(inputs) + len(grads)),
        out_specs=vmem,
        scratch_shapes=[
            pltpu.VMEM((XS,) + inputs[0].shape, jnp.bfloat16),
            pltpu.VMEM((2 * slots, 256, WIDE), jnp.bfloat16),
        ]
        + scratch,
        compiler_params=pltpu.CompilerParams(vmem_limit_bytes=14 * MB),
        cost_estimate=pl.CostEstimate(
            flops=sum(512 * g.size for g in grads) + 512 * MB * slots,
            bytes_accessed=4 * MB,
            transcendentals=0,
        ),
        name=kernel.__name__,
    )(place, *bases, before, *inputs, *grads)


def on_device(krylov_basis, hessian_product, output_grads, layer_inputs, rotation):
    core = lax.axis_index("core")
    place = [lax.axis_index(axis) for axis in ("y", "z", "x")] + [1 - 2 * core]
    place = jnp.stack(place).astype(jnp.int32)
    core_id = core[None].astype(jnp.int32)
    half = krylov_basis.shape[1] // 2

    both = (output_grads, swap_core(output_grads))
    a, b = (
        jnp.concatenate(
            [lax.dynamic_slice_in_dim(g, core * half + at * WIDE, WIDE, 1) for g in both]
        )
        for at in range(2)
    )
    b1, b7 = toward(b, "z", 1), toward(b, "z", -1)
    a1, a3 = toward(a, "y", 1), toward(a, "y", -1)
    b1, b7, a1, a3, krylov, layer = together(b1, b7, a1, a3, krylov_basis, layer_inputs)
    x0 = turn_inputs(core_id, layer, swap_core(layer))
    x1, x3 = toward(x0, "x", 1), toward(x0, "x", -1)
    left_basis, right_basis = turn_basis(core_id, krylov, swap_core(krylov))
    b2, b6 = toward(b1, "z", 1), toward(b7, "z", -1)
    a2 = toward(a1, "y", 1)
    l0 = jnp.concatenate([a, a1, a2, a3])
    l0, field = together(l0, hessian_product)
    l1, l7 = toward(l0, "z", 1), toward(l0, "z", -1)
    b3, b5 = toward(b2, "z", 1), toward(b6, "z", -1)
    b4 = toward(b3, "z", 1)
    r0 = jnp.concatenate([b, b1, b2, b3, b4, b5, b6, b7])
    r1, r3 = toward(r0, "y", 1), toward(r0, "y", -1)
    sums = gram(krylov_basis, field)
    l1, l7, left_basis, right_basis = together(l1, l7, left_basis, right_basis)
    l2, l6 = toward(l1, "z", 1), toward(l7, "z", -1)
    x2 = toward(x1, "x", 1)
    l2, l6, sums = together(l2, l6, sums)
    l3, l5 = toward(l2, "z", 1), toward(l6, "z", -1)
    r2 = toward(r1, "y", 1)
    inputs = [x0, x1, x2, x3]
    sems = pltpu.SemaphoreType.DMA((12,))
    basis = pltpu.VMEM(left_basis.shape, jnp.bfloat16)
    held = [basis, pltpu.VMEM((3, ZS * CHIP, WIDE), jnp.bfloat16), sems]
    sums = project(
        right_kernel, place, inputs, [right_basis], sums, [r0, r1, r3], pl.ANY, 6, held
    )
    l3, l5, sums = together(l3, l5, sums)
    l4 = toward(l3, "z", 1)

    held = [basis, pltpu.VMEM((ZS, YS * CHIP, WIDE), jnp.bfloat16), sems]
    lefts = [l0, l1, l2, l3, l5, l6, l7]
    sums = project(left_kernel, place, inputs, [left_basis], sums, lefts, pl.ANY, SEQS, held)
    bases = [left_basis, right_basis]
    sums = project(far_kernel, place, inputs, bases, sums, [l4, r2], pltpu.VMEM, YS, [])
    rotation = jnp.pad(rotation.T, ((0, 8 - TOP), (0, 128 - K)))
    sums, rotation = together(sums, rotation)
    sums = sum_everywhere(sums)

    none = jnp.zeros((1, 1), jnp.float32)
    *results, little = finish(False, none, sums, rotation, krylov_basis, hessian_product)

    def measured(results):
        squares = squared_length(sums, krylov_basis, hessian_product)[None, None]
        return tuple(
            finish(True, squares, sums, rotation, krylov_basis, hessian_product)[:3]
        )

    new_vector, hessenberg, influence = lax.cond(
        little[0] == 1, measured, lambda results: tuple(results), results
    )
    return new_vector, hessenberg[0], influence.T


def solution(mesh):
    chips = jax.sharding.Mesh(mesh.devices.reshape(YS, ZS, 2, XS), ("y", "z", "core", "x"))
    col, tok = ("y", "z", "core"), "x"
    return jax.shard_map(
        on_device,
        mesh=chips,
        in_specs=(P(None, tok, col), P(tok, col), P(col, tok), P(tok, col), P()),
        out_specs=(P(tok, col), P(), P()),
        check_vma=False,
    )
```

time: 143 us -> 127 us (0.89)
  blocking collectives: 13.1 us -> 31.2 us
  waiting for transfers between devices: 34.1 us -> 22.8 us
  local copies, waits for them, and re-layouts: 14.9 us -> 5.45 us
  starting transfers between devices: 44.2 us -> 35.4 us
  Pallas kernels: 34.5 us -> 29.7 us
    all_to_all x1 -> x2, blocking collectives: 13.1 us -> 31.2 us  [sum_over(): return jnp.sum(lax.all_to_all(copies, axes, 0, 0), axis=0)]
    unnamed x46 -> x42, local copies, waits for them, and re-layouts: 14.2 us -> 5.41 us
    all_to_all x1 -> x0, starting transfers between devices: 7.26 us -> none  [sum_over(): return jnp.sum(lax.all_to_all(copies, axes, 0, 0), axis=0)]
    all_to_all x1 -> x0, waiting for transfers between devices: 6.42 us -> none  [sum_over(): return jnp.sum(lax.all_to_all(copies, axes, 0, 0), axis=0)]
    pallas_call x2 -> x3, Pallas kernels: 18.6 us -> 13.7 us  [project(): pl.pallas_call(kernel, out_shape=jax.ShapeDtypeStruct((8, 128), jnp.float...]
    ppermute x23, waiting for transfers between devices: 27.2 us -> 22.3 us  [toward(): return lax.ppermute(value, axes, pairs)]
    ppermute x3, starting transfers between devices: 5.25 us -> 3.42 us  [swap_core(): return lax.ppermute(value, 'core', [(0, 1), (1, 0)])]
  transfers between devices with their start and end apart: 27 -> 26, of which waited for: 9 -> 10; matrix products, arithmetic and copies ran while one was open for 1% -> 1% of each run, Pallas kernels for 16% -> 17%
where the time goes in v2:
time: 127 us
  starting transfers between devices  35.4 us (28%)
  blocking collectives  31.2 us (25%)
  Pallas kernels  29.7 us (23%)
  waiting for transfers between devices  22.8 us (18%)
  local copies, waits for them, and re-layouts  5.45 us (4%)
  between operations  1.81 us (1%)
    ppermute x23, starting transfers between devices, toward(): return lax.ppermute(value, axes, pairs)  32 us
    all_to_all x2, blocking collectives, sum_over(): return jnp.sum(lax.all_to_all(copies, axes, 0, 0), axis=0)  31.2 us
    ppermute x23, waiting for transfers between devices, toward(): return lax.ppermute(value, axes, pairs)  22.3 us
    pallas_call x3, Pallas kernels, project(): pl.pallas_call(kernel, out_shape=jax.ShapeDtypeStruct((8, 128), jnp.float...  13.7 us
    pallas_call x1, Pallas kernels, gram(): pl.pallas_call(gram_kernel, out_shape=jax.ShapeDtypeStruct((8, 128), jnp....  6.28 us
    unnamed x42, local copies, waits for them, and re-layouts  5.41 us
    pallas_call x1, Pallas kernels, turn_basis(): pl.pallas_call(turn_basis_kernel, out_shape=[jax.ShapeDtypeStruct((K, 256...  4.84 us
    pallas_call x1, Pallas kernels, finish(): pl.pallas_call(functools.partial(finish_kernel, given), out_shape=[jax.Sh...  4.73 us
  transfers between devices with their start and end apart: 26, of which 10 were waited for; matrix products, arithmetic and copies ran while one was open for 1% of the time, Pallas kernels for 17%

profile of v2, /device:TPU:1, one launch (start us, length us, event | category | flops | bytes accessed | tf_op | source)
XLA Modules:
  0.0 126.5 jit_solution(5716357822773268927)
XLA Ops:
  0.6 3.3 %collective-permute-start = (bf16[64,2048]{1,0:T(8,128)(2,1)}, bf16[64,2048]{1,0:T(8,128)(2,1)S(1)}, u32[]{:S(2)}, u32[]{:S(2)}) collective-permute-start(bf16[64,2048]{1,0:T(8,128)(2,1)} %param.9), channel_id=1, source_target_pairs={{0,4},{4,0},{1,5},{5,1},{2,6},{6,2},{3,7},{7,3},{8,12},{12,8},{9,1... | collective-permute-start | bytes 786440 | tf_op jit(solution)/shard_map/ppermute | solution.py:43
  5.4 1.1 collective-permute-start.3
  6.9 5.2 %collective-permute-start.1 = (bf16[128,512]{1,0:T(8,128)(2,1)S(1)}, bf16[128,512]{1,0:T(8,128)(2,1)S(1)}, u32[]{:S(2)}, u32[]{:S(2)}) collective-permute-start(bf16[128,512]{1,0:T(8,128)(2,1)S(1)} %pad_maximum_fusion), channel_id=1, source_target_pairs={{0,8},{4,60},{8,16},{12,4},{16,24},{20,12},{24,32},{28,20},{32,40}... | collective-permute-start | bytes 393224 | tf_op jit(solution)/shard_map/ppermute | solution.py:39
  12.8 1.2 collective-permute-done.1
  14.1 3.1 %collective-permute-done.2 = bf16[128,512]{1,0:T(8,128)(2,1)S(1)} collective-permute-done((bf16[128,512]{1,0:T(8,128)(2,1)S(1)}, bf16[128,512]{1,0:T(8,128)(2,1)S(1)}, u32[]{:S(2)}, u32[]{:S(2)}) %collective-permute-start.2) | collective-permute-done | bytes 131104 | tf_op jit(solution)/shard_map/ppermute | solution.py:39
  17.1 2.1 %collective-permute-start.17 = (bf16[128,512]{1,0:T(8,128)(2,1)S(1)}, bf16[128,512]{1,0:T(8,128)(2,1)S(1)}, u32[]{:S(2)}, u32[]{:S(2)}) collective-permute-start(bf16[128,512]{1,0:T(8,128)(2,1)S(1)} %collective-permute-done.1), channel_id=1, source_target_pairs={{0,8},{4,60},{8,16},{12,4},{16,24},{20,12},{24,32},{28,20},{32,40}... | collective-permute-start | bytes 393224 | tf_op jit(solution)/shard_map/ppermute | solution.py:39
  19.3 2.7 %collective-permute-start.5 = (bf16[128,512]{1,0:T(8,128)(2,1)S(1)}, bf16[128,512]{1,0:T(8,128)(2,1)S(1)}, u32[]{:S(2)}, u32[]{:S(2)}) collective-permute-start(bf16[128,512]{1,0:T(8,128)(2,1)S(1)} %collective-permute-done.3), channel_id=1, source_target_pairs={{0,64},{4,196},{64,128},{68,4},{128,192},{132,68},{192,0},{196,132... | collective-permute-start | bytes 393224 | tf_op jit(solution)/shard_map/ppermute | solution.py:39
  22.1 2.6 %collective-permute-start.18 = (bf16[128,512]{1,0:T(8,128)(2,1)S(1)}, bf16[128,512]{1,0:T(8,128)(2,1)S(1)}, u32[]{:S(2)}, u32[]{:S(2)}) collective-permute-start(bf16[128,512]{1,0:T(8,128)(2,1)S(1)} %collective-permute-done.17), channel_id=1, source_target_pairs={{0,8},{4,60},{8,16},{12,4},{16,24},{20,12},{24,32},{28,20},{32,40}... | collective-permute-start | bytes 393224 | tf_op jit(solution)/shard_map/ppermute | solution.py:39
  24.9 1.8 %collective-permute-done.18 = bf16[128,512]{1,0:T(8,128)(2,1)S(1)} collective-permute-done((bf16[128,512]{1,0:T(8,128)(2,1)S(1)}, bf16[128,512]{1,0:T(8,128)(2,1)S(1)}, u32[]{:S(2)}, u32[]{:S(2)}) %collective-permute-start.18) | collective-permute-done | bytes 131104 | tf_op jit(solution)/shard_map/ppermute | solution.py:39
  26.7 3.1 %collective-permute-start.19 = (bf16[128,512]{1,0:T(8,128)(2,1)S(1)}, bf16[128,512]{1,0:T(8,128)(2,1)S(1)}, u32[]{:S(2)}, u32[]{:S(2)}) collective-permute-start(bf16[128,512]{1,0:T(8,128)(2,1)S(1)} %collective-permute-done.18), channel_id=1, source_target_pairs={{0,8},{4,60},{8,16},{12,4},{16,24},{20,12},{24,32},{28,20},{32,40}... | collective-permute-start | bytes 393224 | tf_op jit(solution)/shard_map/ppermute | solution.py:39
  31.2 4.7 %collective-permute-done.19 = bf16[128,512]{1,0:T(8,128)(2,1)S(1)} collective-permute-done((bf16[128,512]{1,0:T(8,128)(2,1)S(1)}, bf16[128,512]{1,0:T(8,128)(2,1)S(1)}, u32[]{:S(2)}, u32[]{:S(2)}) %collective-permute-start.19) | collective-permute-done | bytes 131104 | tf_op jit(solution)/shard_map/ppermute | solution.py:39
  35.9 2.5 %collective-permute-start.14 = (bf16[256,1024]{1,0:T(8,128)(2,1)S(1)}, bf16[256,1024]{1,0:T(8,128)(2,1)}, u32[]{:S(2)}, u32[]{:S(2)}) collective-permute-start(bf16[256,1024]{1,0:T(8,128)(2,1)S(1)} %turn_inputs.1.refs_0_), channel_id=1, source_target_pairs={{0,1},{4,7},{1,2},{5,4},{2,3},{6,5},{3,0},{7,6},{8,9},{12,15},{9,1... | collective-permute-start | bytes 1572872 | tf_op jit(solution)/shard_map/ppermute | solution.py:39
  38.5 1.7 %collective-permute-start.22 = (bf16[1024,512]{1,0:T(8,128)(2,1)S(1)}, bf16[1024,512]{1,0:T(8,128)(2,1)S(1)}, u32[]{:S(2)}, u32[]{:S(2)}) collective-permute-start(bf16[1024,512]{1,0:T(8,128)(2,1)S(1)} %constant_dynamic-update-slice_fusion.5.refs_4_), channel_id=1, source_target_pairs={{0,64},{4,196},{64,128},{68,4},{128,192},{132,68},{192,0},{196,132... | collective-permute-start | bytes 3145736 | tf_op jit(solution)/shard_map/ppermute | solution.py:39
  40.2 4.8 %turn_basis.1 = (bf16[8,256,512]{2,1,0:T(8,128)(2,1)S(1)}, bf16[8,256,512]{2,1,0:T(8,128)(2,1)S(1)}) custom-call(s32[1]{0:T(128)} %bitcast.5.core_ref, bf16[8,2048,128]{2,1,0:T(8,128)(2,1)} %basis_ref.3, bf16[8,2048,128]{2,1,0:T(8,128)(2,1)S(1)} %collective-permute-done.8.other_ref), custom_call_target="tpu_custom_call" | custom-call | bytes 8388608 | tf_op jit(solution)/shard_map/turn_basis/pallas_call | solution.py:226
  45.3 2.6 %collective-permute-start.9 = (bf16[512,512]{1,0:T(8,128)(2,1)S(1)}, bf16[512,512]{1,0:T(8,128)(2,1)}, u32[]{:S(2)}, u32[]{:S(2)}) collective-permute-start(bf16[512,512]{1,0:T(8,128)(2,1)S(1)} %collective-permute-done.6.refs_5_), channel_id=1, source_target_pairs={{0,8},{4,60},{8,16},{12,4},{16,24},{20,12},{24,32},{28,20},{32,40}... | collective-permute-start | bytes 1572872 | tf_op jit(solution)/shard_map/ppermute | solution.py:39
  48.1 6.7 %collective-permute-done.10.refs_9_ = bf16[512,512]{1,0:T(8,128)(2,1)} collective-permute-done((bf16[512,512]{1,0:T(8,128)(2,1)S(1)}, bf16[512,512]{1,0:T(8,128)(2,1)}, u32[]{:S(2)}, u32[]{:S(2)}) %collective-permute-start.10) | collective-permute-done | bytes 524320 | tf_op jit(solution)/shard_map/ppermute | solution.py:39
  54.8 1.4 %collective-permute-start.15 = (bf16[256,1024]{1,0:T(8,128)(2,1)}, bf16[256,1024]{1,0:T(8,128)(2,1)}, u32[]{:S(2)}, u32[]{:S(2)}) collective-permute-start(bf16[256,1024]{1,0:T(8,128)(2,1)} %collective-permute-done.14.refs_1_), channel_id=1, source_target_pairs={{0,1},{4,7},{1,2},{5,4},{2,3},{6,5},{3,0},{7,6},{8,9},{12,15},{9,1... | collective-permute-start | bytes 1572872 | tf_op jit(solution)/shard_map/ppermute | solution.py:39
  56.2 6.3 %gram.1.before_ref = f32[8,128]{1,0:T(8,128)S(1)} custom-call(bf16[8,2048,128]{2,1,0:T(8,128)(2,1)S(1)} %copy-done.12, f32[2048,128]{1,0:T(8,128)S(1)} %copy-done.13), custom_call_target="tpu_custom_call" | custom-call | flops 25165824 | bytes 18874368 | tf_op jit(solution)/shard_map/gram/pallas_call | solution.py:95
  63.4 1.4 %collective-permute-start.12 = (bf16[512,512]{1,0:T(8,128)(2,1)}, bf16[512,512]{1,0:T(8,128)(2,1)}, u32[]{:S(2)}, u32[]{:S(2)}) collective-permute-start(bf16[512,512]{1,0:T(8,128)(2,1)} %collective-permute-done.10.refs_9_), channel_id=1, source_target_pairs={{0,56},{4,12},{8,0},{12,20},{16,8},{20,28},{24,16},{28,36},{32,24}... | collective-permute-start | bytes 1572872 | tf_op jit(solution)/shard_map/ppermute | solution.py:39
  64.9 1.9 %collective-permute-start.25 = (bf16[1024,512]{1,0:T(8,128)(2,1)S(1)}, bf16[1024,512]{1,0:T(8,128)(2,1)}, u32[]{:S(2)}, u32[]{:S(2)}) collective-permute-start(bf16[1024,512]{1,0:T(8,128)(2,1)S(1)} %collective-permute-done.22.refs_5_), channel_id=1, source_target_pairs={{0,64},{4,196},{64,128},{68,4},{128,192},{132,68},{192,0},{196,132... | collective-permute-start | bytes 3145736 | tf_op jit(solution)/shard_map/ppermute | solution.py:39
  66.9 1.0 collective-permute-done.15.refs_2_
  67.8 1.3 %collective-permute-done.23.refs_6_ = bf16[1024,512]{1,0:T(8,128)(2,1)} collective-permute-done((bf16[1024,512]{1,0:T(8,128)(2,1)S(1)}, bf16[1024,512]{1,0:T(8,128)(2,1)}, u32[]{:S(2)}, u32[]{:S(2)}) %collective-permute-start.23) | collective-permute-done | bytes 1048608 | tf_op jit(solution)/shard_map/ppermute | solution.py:39
  69.1 1.6 %copy-done.4 = bf16[8,256,512]{2,1,0:T(8,128)(2,1)S(1)} copy-done((bf16[8,256,512]{2,1,0:T(8,128)(2,1)S(1)}, bf16[8,256,512]{2,1,0:T(8,128)(2,1)}, u32[]{:S(2)}) %copy-start.4) | copy-done | bytes 2097176
  70.7 1.0 copy-done.10
  71.8 4.5 %right_kernel.1.before_ref = f32[8,128]{1,0:T(8,128)S(1)} custom-call(s32[4]{0:T(128)S(1)} %pad_add_fusion.place_ref, bf16[8,256,512]{2,1,0:T(8,128)(2,1)S(1)} %copy-done.4, f32[8,128]{1,0:T(8,128)S(1)} %gram.1.before_ref, bf16[256,1024]{1,0:T(8,128)(2,1)S(1)} %turn_inputs.1.refs_0_, bf16[256,1024]{1,0:T(8,128)(2,1)} %collective-permute-done.14.refs_1_, ...), custom_call_target="tpu_custom_call" | custom-call | flops 4026531840 | bytes 4194304 | tf_op jit(solution)/shard_map/right_kernel/pallas_call | solution.py:396
  76.3 2.4 %collective-permute-start.24 = (bf16[512,512]{1,0:T(8,128)(2,1)}, bf16[512,512]{1,0:T(8,128)(2,1)S(1)}, u32[]{:S(2)}, u32[]{:S(2)}) collective-permute-start(bf16[512,512]{1,0:T(8,128)(2,1)} %collective-permute-done.11.refs_7_), channel_id=1, source_target_pairs={{0,8},{4,60},{8,16},{12,4},{16,24},{20,12},{24,32},{28,20},{32,40}... | collective-permute-start | bytes 1572872 | tf_op jit(solution)/shard_map/ppermute | solution.py:39
  78.8 5.4 %left_kernel.1.before_ref = f32[8,128]{1,0:T(8,128)S(1)} custom-call(s32[4]{0:T(128)S(1)} %pad_add_fusion.place_ref, bf16[8,256,512]{2,1,0:T(8,128)(2,1)S(1)} %copy-done.2, f32[8,128]{1,0:T(8,128)S(1)} %right_kernel.1.before_ref, bf16[256,1024]{1,0:T(8,128)(2,1)S(1)} %turn_inputs.1.refs_0_, bf16[256,1024]{1,0:T(8,128)(2,1)} %collective-permute-done.14.refs_1_, ...), custom_call_target="tpu_custom_call" | custom-call | flops 5234491392 | bytes 4194304 | tf_op jit(solution)/shard_map/left_kernel/pallas_call | solution.py:396
  84.2 1.8 %collective-permute-done.24.refs_4_ = bf16[512,512]{1,0:T(8,128)(2,1)S(1)} collective-permute-done((bf16[512,512]{1,0:T(8,128)(2,1)}, bf16[512,512]{1,0:T(8,128)(2,1)S(1)}, u32[]{:S(2)}, u32[]{:S(2)}) %collective-permute-start.24) | collective-permute-done | bytes 524320 | tf_op jit(solution)/shard_map/ppermute | solution.py:39
  85.9 3.8 %far_kernel.1 = f32[8,128]{1,0:T(8,128)S(1)} custom-call(s32[4]{0:T(128)S(1)} %pad_add_fusion.place_ref, bf16[8,256,512]{2,1,0:T(8,128)(2,1)S(1)} %copy-done.2, bf16[8,256,512]{2,1,0:T(8,128)(2,1)S(1)} %copy-done.4, f32[8,128]{1,0:T(8,128)S(1)} %left_kernel.1.before_ref, bf16[256,1024]{1,0:T(8,128)(2,1)S(1)} %turn_inputs.1.refs_0_, ...), custom_call_target="tpu_custom_call" | custom-call | flops 2550136832 | bytes 4194304 | tf_op jit(solution)/shard_map/far_kernel/pallas_call | solution.py:396
  89.7 18.2 %all_to_all.20 = f32[16,8,128]{2,1,0:T(8,128)S(1)} all-to-all(f32[16,8,128]{2,1,0:T(8,128)S(1)} %broadcast_in_dim.13), channel_id=1, replica_groups=mesh['y'=4,'z'=8,'core'=2,'x'=4] {'z','core'}, dimensions={0} | all-to-all | bytes 131072 | tf_op jit(solution)/shard_map/all_to_all | solution.py:52
  108.0 13.0 %all_to_all.21 = f32[16,8,128]{2,1,0:T(8,128)S(1)} all-to-all(f32[16,8,128]{2,1,0:T(8,128)S(1)} %broadcast_in_dim.14), channel_id=1, replica_groups=mesh['y'=4,'z'=8,'core'=2,'x'=4] {'y','x'}, dimensions={0} | all-to-all | bytes 131072 | tf_op jit(solution)/shard_map/all_to_all | solution.py:52
  121.0 4.7 %finish.3 = (bf16[2048,128]{1,0:T(8,128)(2,1)}, f32[1,9]{1,0:T(1,128)}, f32[4,8]{1,0:T(4,128)}, s32[1]{0:T(128)}) custom-call(f32[1,1]{1,0:T(1,128)} %constant.11.clone.1.squares_ref, f32[8,128]{1,0:T(8,128)S(1)} %reduce_sum.41.sums_ref, f32[8,128]{1,0:T(8,128)S(1)} %pad.4.rotation_ref, bf16[8,2048,128]{2,1,0:T(8,128)(2,1)} %basis_ref.3, ...), custom_call_target="tpu_custom_call" | custom-call | flops 6291456 | bytes 6291456 | tf_op jit(solution)/shard_map/finish/pallas_call | solution.py:199
  (82 shorter events, 5.7 us)
Async XLA Ops:
  0.6 4.7 %collective-permute-start = (bf16[64,2048]{1,0:T(8,128)(2,1)}, bf16[64,2048]{1,0:T(8,128)(2,1)S(1)}, u32[]{:S(2)}, u32[]{:S(2)}) collective-permute-start(bf16[64,2048]{1,0:T(8,128)(2,1)} %param.9), channel_id=1, source_target_pairs={{0,4},{4,0},{1,5},{5,1},{2,6},{6,2},{3,7},{7,3},{8,12},{12,8},{9,1... | collective-permute-start | bytes 786440 | tf_op jit(solution)/shard_map/ppermute | solution.py:43
  5.4 6.8 %collective-permute-start.3 = (bf16[128,512]{1,0:T(8,128)(2,1)S(1)}, bf16[128,512]{1,0:T(8,128)(2,1)S(1)}, u32[]{:S(2)}, u32[]{:S(2)}) collective-permute-start(bf16[128,512]{1,0:T(8,128)(2,1)S(1)} %pad_maximum_fusion.1), channel_id=1, source_target_pairs={{0,64},{4,196},{64,128},{68,4},{128,192},{132,68},{192,0},{196,132... | collective-permute-start | bytes 393224 | tf_op jit(solution)/shard_map/ppermute | solution.py:39
  6.4 6.4 %collective-permute-start.4 = (bf16[128,512]{1,0:T(8,128)(2,1)S(1)}, bf16[128,512]{1,0:T(8,128)(2,1)S(1)}, u32[]{:S(2)}, u32[]{:S(2)}) collective-permute-start(bf16[128,512]{1,0:T(8,128)(2,1)S(1)} %pad_maximum_fusion.1), channel_id=1, source_target_pairs={{0,192},{4,68},{64,0},{68,132},{128,64},{132,196},{192,128},{196,4... | collective-permute-start | bytes 393224 | tf_op jit(solution)/shard_map/ppermute | solution.py:39
  6.9 7.1 %collective-permute-start.1 = (bf16[128,512]{1,0:T(8,128)(2,1)S(1)}, bf16[128,512]{1,0:T(8,128)(2,1)S(1)}, u32[]{:S(2)}, u32[]{:S(2)}) collective-permute-start(bf16[128,512]{1,0:T(8,128)(2,1)S(1)} %pad_maximum_fusion), channel_id=1, source_target_pairs={{0,8},{4,60},{8,16},{12,4},{16,24},{20,12},{24,32},{28,20},{32,40}... | collective-permute-start | bytes 393224 | tf_op jit(solution)/shard_map/ppermute | solution.py:39
  12.1 5.0 %collective-permute-start.2 = (bf16[128,512]{1,0:T(8,128)(2,1)S(1)}, bf16[128,512]{1,0:T(8,128)(2,1)S(1)}, u32[]{:S(2)}, u32[]{:S(2)}) collective-permute-start(bf16[128,512]{1,0:T(8,128)(2,1)S(1)} %pad_maximum_fusion), channel_id=1, source_target_pairs={{0,56},{4,12},{8,0},{12,20},{16,8},{20,28},{24,16},{28,36},{32,24}... | collective-permute-start | bytes 393224 | tf_op jit(solution)/shard_map/ppermute | solution.py:39
  17.1 23.1 %collective-permute-start.8 = (bf16[8,2048,128]{2,1,0:T(8,128)(2,1)}, bf16[8,2048,128]{2,1,0:T(8,128)(2,1)S(1)}, u32[]{:S(2)}, u32[]{:S(2)}) collective-permute-start(bf16[8,2048,128]{2,1,0:T(8,128)(2,1)} %basis_ref.3), channel_id=1, source_target_pairs={{0,4},{4,0},{1,5},{5,1},{2,6},{6,2},{3,7},{7,3},{8,12},{12,8},{9,1... | collective-permute-start | bytes 12582920 | tf_op jit(solution)/shard_map/ppermute | solution.py:43
  17.1 5.0 %collective-permute-start.17 = (bf16[128,512]{1,0:T(8,128)(2,1)S(1)}, bf16[128,512]{1,0:T(8,128)(2,1)S(1)}, u32[]{:S(2)}, u32[]{:S(2)}) collective-permute-start(bf16[128,512]{1,0:T(8,128)(2,1)S(1)} %collective-permute-done.1), channel_id=1, source_target_pairs={{0,8},{4,60},{8,16},{12,4},{16,24},{20,12},{24,32},{28,20},{32,40}... | collective-permute-start | bytes 393224 | tf_op jit(solution)/shard_map/ppermute | solution.py:39
  19.3 5.5 %collective-permute-start.5 = (bf16[128,512]{1,0:T(8,128)(2,1)S(1)}, bf16[128,512]{1,0:T(8,128)(2,1)S(1)}, u32[]{:S(2)}, u32[]{:S(2)}) collective-permute-start(bf16[128,512]{1,0:T(8,128)(2,1)S(1)} %collective-permute-done.3), channel_id=1, source_target_pairs={{0,64},{4,196},{64,128},{68,4},{128,192},{132,68},{192,0},{196,132... | collective-permute-start | bytes 393224 | tf_op jit(solution)/shard_map/ppermute | solution.py:39
  21.9 7.9 %collective-permute-start.20 = (bf16[128,512]{1,0:T(8,128)(2,1)S(1)}, bf16[128,512]{1,0:T(8,128)(2,1)S(1)}, u32[]{:S(2)}, u32[]{:S(2)}) collective-permute-start(bf16[128,512]{1,0:T(8,128)(2,1)S(1)} %collective-permute-done.2), channel_id=1, source_target_pairs={{0,56},{4,12},{8,0},{12,20},{16,8},{20,28},{24,16},{28,36},{32,24}... | collective-permute-start | bytes 393224 | tf_op jit(solution)/shard_map/ppermute | solution.py:39
  22.0 7.9 %collective-permute-start.13 = (bf16[1024,128]{1,0:T(8,128)(2,1)}, bf16[1024,128]{1,0:T(8,128)(2,1)S(1)}, u32[]{:S(2)}, u32[]{:S(2)}) collective-permute-start(bf16[1024,128]{1,0:T(8,128)(2,1)} %own_ref.1), channel_id=1, source_target_pairs={{0,4},{4,0},{1,5},{5,1},{2,6},{6,2},{3,7},{7,3},{8,12},{12,8},{9,1... | collective-permute-start | bytes 786440 | tf_op jit(solution)/shard_map/ppermute | solution.py:43
  22.1 4.6 %collective-permute-start.18 = (bf16[128,512]{1,0:T(8,128)(2,1)S(1)}, bf16[128,512]{1,0:T(8,128)(2,1)S(1)}, u32[]{:S(2)}, u32[]{:S(2)}) collective-permute-start(bf16[128,512]{1,0:T(8,128)(2,1)S(1)} %collective-permute-done.17), channel_id=1, source_target_pairs={{0,8},{4,60},{8,16},{12,4},{16,24},{20,12},{24,32},{28,20},{32,40}... | collective-permute-start | bytes 393224 | tf_op jit(solution)/shard_map/ppermute | solution.py:39
  24.8 20.3 %collective-permute-start.6 = (bf16[512,512]{1,0:T(8,128)(2,1)S(1)}, bf16[512,512]{1,0:T(8,128)(2,1)S(1)}, u32[]{:S(2)}, u32[]{:S(2)}) collective-permute-start(bf16[512,512]{1,0:T(8,128)(2,1)S(1)} %constant_dynamic-update-slice_fusion.refs_4_), channel_id=1, source_target_pairs={{0,8},{4,60},{8,16},{12,4},{16,24},{20,12},{24,32},{28,20},{32,40}... | collective-permute-start | bytes 1572872 | tf_op jit(solution)/shard_map/ppermute | solution.py:39
  26.7 9.2 %collective-permute-start.19 = (bf16[128,512]{1,0:T(8,128)(2,1)S(1)}, bf16[128,512]{1,0:T(8,128)(2,1)S(1)}, u32[]{:S(2)}, u32[]{:S(2)}) collective-permute-start(bf16[128,512]{1,0:T(8,128)(2,1)S(1)} %collective-permute-done.18), channel_id=1, source_target_pairs={{0,8},{4,60},{8,16},{12,4},{16,24},{20,12},{24,32},{28,20},{32,40}... | collective-permute-start | bytes 393224 | tf_op jit(solution)/shard_map/ppermute | solution.py:39
  29.8 8.6 %collective-permute-start.21 = (bf16[128,512]{1,0:T(8,128)(2,1)S(1)}, bf16[128,512]{1,0:T(8,128)(2,1)S(1)}, u32[]{:S(2)}, u32[]{:S(2)}) collective-permute-start(bf16[128,512]{1,0:T(8,128)(2,1)S(1)} %collective-permute-done.20), channel_id=1, source_target_pairs={{0,56},{4,12},{8,0},{12,20},{16,8},{20,28},{24,16},{28,36},{32,24}... | collective-permute-start | bytes 393224 | tf_op jit(solution)/shard_map/ppermute | solution.py:39
  30.0 15.2 %collective-permute-start.7 = (bf16[512,512]{1,0:T(8,128)(2,1)S(1)}, bf16[512,512]{1,0:T(8,128)(2,1)S(1)}, u32[]{:S(2)}, u32[]{:S(2)}) collective-permute-start(bf16[512,512]{1,0:T(8,128)(2,1)S(1)} %constant_dynamic-update-slice_fusion.refs_4_), channel_id=1, source_target_pairs={{0,56},{4,12},{8,0},{12,20},{16,8},{20,28},{24,16},{28,36},{32,24}... | collective-permute-start | bytes 1572872 | tf_op jit(solution)/shard_map/ppermute | solution.py:39
  35.9 12.0 %collective-permute-start.14 = (bf16[256,1024]{1,0:T(8,128)(2,1)S(1)}, bf16[256,1024]{1,0:T(8,128)(2,1)}, u32[]{:S(2)}, u32[]{:S(2)}) collective-permute-start(bf16[256,1024]{1,0:T(8,128)(2,1)S(1)} %turn_inputs.1.refs_0_), channel_id=1, source_target_pairs={{0,1},{4,7},{1,2},{5,4},{2,3},{6,5},{3,0},{7,6},{8,9},{12,15},{9,1... | collective-permute-start | bytes 1572872 | tf_op jit(solution)/shard_map/ppermute | solution.py:39
  38.5 17.7 %copy-start.12 = (bf16[8,2048,128]{2,1,0:T(8,128)(2,1)S(1)}, bf16[8,2048,128]{2,1,0:T(8,128)(2,1)}, u32[]{:S(2)}) copy-start(bf16[8,2048,128]{2,1,0:T(8,128)(2,1)} %basis_ref.3) | copy-start | bytes 12582916
  38.5 26.4 %collective-permute-start.22 = (bf16[1024,512]{1,0:T(8,128)(2,1)S(1)}, bf16[1024,512]{1,0:T(8,128)(2,1)S(1)}, u32[]{:S(2)}, u32[]{:S(2)}) collective-permute-start(bf16[1024,512]{1,0:T(8,128)(2,1)S(1)} %constant_dynamic-update-slice_fusion.5.refs_4_), channel_id=1, source_target_pairs={{0,64},{4,196},{64,128},{68,4},{128,192},{132,68},{192,0},{196,132... | collective-permute-start | bytes 3145736 | tf_op jit(solution)/shard_map/ppermute | solution.py:39
  45.1 19.8 %copy-start.1 = (bf16[8,256,512]{2,1,0:T(8,128)(2,1)}, bf16[8,256,512]{2,1,0:T(8,128)(2,1)S(1)}, u32[]{:S(2)}) copy-start(bf16[8,256,512]{2,1,0:T(8,128)(2,1)S(1)} %get-tuple-element.66.far_basis_ref.left_basis_ref) | copy-start | bytes 6291460
  45.1 19.8 %copy-start.3 = (bf16[8,256,512]{2,1,0:T(8,128)(2,1)}, bf16[8,256,512]{2,1,0:T(8,128)(2,1)S(1)}, u32[]{:S(2)}) copy-start(bf16[8,256,512]{2,1,0:T(8,128)(2,1)S(1)} %get-tuple-element.67.far_basis_ref.right_basis_ref) | copy-start | bytes 6291460
  45.1 19.8 %copy-start.5 = (bf16[512,512]{1,0:T(8,128)(2,1)}, bf16[512,512]{1,0:T(8,128)(2,1)S(1)}, u32[]{:S(2)}) copy-start(bf16[512,512]{1,0:T(8,128)(2,1)S(1)} %collective-permute-done.6.refs_5_) | copy-start | bytes 1572868
  45.1 19.7 %copy-start.7 = (bf16[512,512]{1,0:T(8,128)(2,1)}, bf16[512,512]{1,0:T(8,128)(2,1)S(1)}, u32[]{:S(2)}) copy-start(bf16[512,512]{1,0:T(8,128)(2,1)S(1)} %collective-permute-done.7.refs_10_) | copy-start | bytes 1572868
  45.1 9.6 %collective-permute-start.10 = (bf16[512,512]{1,0:T(8,128)(2,1)S(1)}, bf16[512,512]{1,0:T(8,128)(2,1)}, u32[]{:S(2)}, u32[]{:S(2)}) collective-permute-start(bf16[512,512]{1,0:T(8,128)(2,1)S(1)} %collective-permute-done.7.refs_10_), channel_id=1, source_target_pairs={{0,56},{4,12},{8,0},{12,20},{16,8},{20,28},{24,16},{28,36},{32,24}... | collective-permute-start | bytes 1572872 | tf_op jit(solution)/shard_map/ppermute | solution.py:39
  45.2 23.9 %collective-permute-start.23 = (bf16[1024,512]{1,0:T(8,128)(2,1)S(1)}, bf16[1024,512]{1,0:T(8,128)(2,1)}, u32[]{:S(2)}, u32[]{:S(2)}) collective-permute-start(bf16[1024,512]{1,0:T(8,128)(2,1)S(1)} %constant_dynamic-update-slice_fusion.5.refs_4_), channel_id=1, source_target_pairs={{0,192},{4,68},{64,0},{68,132},{128,64},{132,196},{192,128},{196,4... | collective-permute-start | bytes 3145736 | tf_op jit(solution)/shard_map/ppermute | solution.py:39
  45.3 17.2 %collective-permute-start.9 = (bf16[512,512]{1,0:T(8,128)(2,1)S(1)}, bf16[512,512]{1,0:T(8,128)(2,1)}, u32[]{:S(2)}, u32[]{:S(2)}) collective-permute-start(bf16[512,512]{1,0:T(8,128)(2,1)S(1)} %collective-permute-done.6.refs_5_), channel_id=1, source_target_pairs={{0,8},{4,60},{8,16},{12,4},{16,24},{20,12},{24,32},{28,20},{32,40}... | collective-permute-start | bytes 1572872 | tf_op jit(solution)/shard_map/ppermute | solution.py:39
  47.9 14.7 %collective-permute-start.16 = (bf16[256,1024]{1,0:T(8,128)(2,1)S(1)}, bf16[256,1024]{1,0:T(8,128)(2,1)S(1)}, u32[]{:S(2)}, u32[]{:S(2)}) collective-permute-start(bf16[256,1024]{1,0:T(8,128)(2,1)S(1)} %turn_inputs.1.refs_0_), channel_id=1, source_target_pairs={{0,3},{4,5},{1,0},{5,6},{2,1},{6,7},{3,2},{7,4},{8,11},{12,13},{9,... | collective-permute-start | bytes 1572872 | tf_op jit(solution)/shard_map/ppermute | solution.py:39
  54.8 13.1 %collective-permute-start.15 = (bf16[256,1024]{1,0:T(8,128)(2,1)}, bf16[256,1024]{1,0:T(8,128)(2,1)}, u32[]{:S(2)}, u32[]{:S(2)}) collective-permute-start(bf16[256,1024]{1,0:T(8,128)(2,1)} %collective-permute-done.14.refs_1_), channel_id=1, source_target_pairs={{0,1},{4,7},{1,2},{5,4},{2,3},{6,5},{3,0},{7,6},{8,9},{12,15},{9,1... | collective-permute-start | bytes 1572872 | tf_op jit(solution)/shard_map/ppermute | solution.py:39
  62.5 13.8 %collective-permute-start.11 = (bf16[512,512]{1,0:T(8,128)(2,1)}, bf16[512,512]{1,0:T(8,128)(2,1)}, u32[]{:S(2)}, u32[]{:S(2)}) collective-permute-start(bf16[512,512]{1,0:T(8,128)(2,1)} %collective-permute-done.9.refs_6_), channel_id=1, source_target_pairs={{0,8},{4,60},{8,16},{12,4},{16,24},{20,12},{24,32},{28,20},{32,40}... | collective-permute-start | bytes 1572872 | tf_op jit(solution)/shard_map/ppermute | solution.py:39
  63.4 12.9 %collective-permute-start.12 = (bf16[512,512]{1,0:T(8,128)(2,1)}, bf16[512,512]{1,0:T(8,128)(2,1)}, u32[]{:S(2)}, u32[]{:S(2)}) collective-permute-start(bf16[512,512]{1,0:T(8,128)(2,1)} %collective-permute-done.10.refs_9_), channel_id=1, source_target_pairs={{0,56},{4,12},{8,0},{12,20},{16,8},{20,28},{24,16},{28,36},{32,24}... | collective-permute-start | bytes 1572872 | tf_op jit(solution)/shard_map/ppermute | solution.py:39
  64.9 19.3 %collective-permute-start.25 = (bf16[1024,512]{1,0:T(8,128)(2,1)S(1)}, bf16[1024,512]{1,0:T(8,128)(2,1)}, u32[]{:S(2)}, u32[]{:S(2)}) collective-permute-start(bf16[1024,512]{1,0:T(8,128)(2,1)S(1)} %collective-permute-done.22.refs_5_), channel_id=1, source_target_pairs={{0,64},{4,196},{64,128},{68,4},{128,192},{132,68},{192,0},{196,132... | collective-permute-start | bytes 3145736 | tf_op jit(solution)/shard_map/ppermute | solution.py:39
  76.3 9.6 %collective-permute-start.24 = (bf16[512,512]{1,0:T(8,128)(2,1)}, bf16[512,512]{1,0:T(8,128)(2,1)S(1)}, u32[]{:S(2)}, u32[]{:S(2)}) collective-permute-start(bf16[512,512]{1,0:T(8,128)(2,1)} %collective-permute-done.11.refs_7_), channel_id=1, source_target_pairs={{0,8},{4,60},{8,16},{12,4},{16,24},{20,12},{24,32},{28,20},{32,40}... | collective-permute-start | bytes 1572872 | tf_op jit(solution)/shard_map/ppermute | solution.py:39
  84.2 36.9 %copy-start.14 = (f32[2048,128]{1,0:T(8,128)S(1)}, f32[2048,128]{1,0:T(8,128)}, u32[]{:S(2)}) copy-start(f32[2048,128]{1,0:T(8,128)} %field_ref.2) | copy-start | bytes 3145732
  (10 other events, 66.9 us)

commit v3 on v2

--- a/solution.py
+++ b/solution.py
@@ -19,7 +19,6 @@
 GRAM = 16
 DOTS = GRAM + K
 SELF = DOTS + 1
-PAIRS = [(k, l) for k in range(K) for l in range(k, K)]
 HIGHEST = lax.Precision.HIGHEST
 MB = 2**20
 
@@ -67,40 +66,72 @@
     return jnp.sum(value, axis=axis, keepdims=True)
 
 
-def gram_kernel(basis_ref, field_ref, out_ref):
-    count = len(PAIRS) + K + 1
-
-    def step(at, totals):
-        rows = pl.ds(pl.multiple_of(at * 16, 16), 16)
-        stack = [basis_ref[k, rows, :].astype(jnp.float32) for k in range(K)]
-        field = field_ref[rows, :]
-        terms = [stack[k] * stack[l] for k, l in PAIRS] + [stack[k] * field for k in range(K)]
-        terms.append(field * field)
-        return tuple(t + (a[:8] + a[8:]) for t, a in zip(totals, terms))
-
-    zero = jnp.zeros((8, 128), jnp.float32)
-    totals = lax.fori_loop(0, field_ref.shape[0] // 16, step, (zero,) * count)
-    totals = [total_of(total) for total in totals]
-    row, lane = cells()
-    out = jnp.where((row == 0) & (lane == SELF), totals[-1], 0.0)
-    for (k, l), total in zip(PAIRS, totals):
-        here = ((row == k) & (lane == GRAM + l)) | ((row == l) & (lane == GRAM + k))
-        out = jnp.where(here, total, out)
-    for k in range(K):
-        out = jnp.where((row == k) & (lane == DOTS), totals[len(PAIRS) + k], out)
-    out_ref[...] = out
+def gram_kernel(basis_ref, field_ref, out_ref, cross_ref, dots_ref):
+    at_step = pl.program_id(0)
+
+    @pl.when(at_step == 0)
+    def _():
+        cross_ref[...] = jnp.zeros_like(cross_ref)
+        dots_ref[...] = jnp.zeros_like(dots_ref)
+
+    cross, dots = cross_ref[...], [dots_ref[k] for k in range(K + 1)]
+    for at in range(0, field_ref.shape[0], 64):
+        halves = [slice(at, at + 32), slice(at + 32, at + 64)]
+        tile = jnp.concatenate([basis_ref[:, r, :].reshape(256, 128) for r in halves], axis=1)
+        cross = cross + lax.dot_general(
+            tile, tile, (((1,), (1,)), ((), ())), preferred_element_type=jnp.float32
+        )
+        for r in halves:
+            field = field_ref[r, :]
+            terms = [basis_ref[k, r, :].astype(jnp.float32) * field for k in range(K)]
+            terms.append(field * field)
+            dots = [d + (t[:8] + t[8:16]) + (t[16:24] + t[24:]) for d, t in zip(dots, terms)]
+    cross_ref[...] = cross
+    for k in range(K + 1):
+        dots_ref[k] = dots[k]
+
+    @pl.when(at_step == pl.num_programs(0) - 1)
+    def _():
+        out = matched(cross_ref[...], 8, GRAM)
+        row, lane = cells()
+        for k in range(K):
+            out = jnp.where((row == k) & (lane == DOTS), total_of(dots_ref[k]), out)
+        out_ref[...] = jnp.where((row == 0) & (lane == SELF), total_of(dots_ref[K]), out)
 
 
 def gram(basis, field):
+    rows = field.shape[0] // 4
     return pl.pallas_call(
         gram_kernel,
         out_shape=jax.ShapeDtypeStruct((8, 128), jnp.float32),
-        in_specs=[pl.BlockSpec(memory_space=pltpu.VMEM)] * 2,
+        grid=(4,),
+        in_specs=[
+            pl.BlockSpec((K, rows, 128), lambda t: (0, t, 0)),
+            pl.BlockSpec((rows, 128), lambda t: (t, 0)),
+        ],
         out_specs=pl.BlockSpec(memory_space=pltpu.VMEM),
+        scratch_shapes=[
+            pltpu.VMEM((256, 256), jnp.float32),
+            pltpu.VMEM((K + 1, 8, 128), jnp.float32),
+        ],
         compiler_params=pltpu.CompilerParams(vmem_limit_bytes=8 * MB),
         cost_estimate=pl.CostEstimate(flops=24 * MB, bytes_accessed=18 * MB, transcendentals=0),
         name="gram",
     )(basis, field)
+
+
+def matched(cross, slots, lane):
+    r = lax.broadcasted_iota(jnp.int32, cross.shape, 0)
+    q = lax.broadcasted_iota(jnp.int32, cross.shape, 1)
+    cross = jnp.where(lax.rem(r, 32) == lax.rem(q, 32), cross, 0.0)
+    sums = jnp.sum(cross.reshape(slots, -1, 256), axis=1)
+    return pick_lanes(sums, lane)
+
+
+def pick_lanes(sums, lane):
+    owner = lax.broadcasted_iota(jnp.int32, (256, 128), 0) // 32 + lane
+    pick = (owner == lax.broadcasted_iota(jnp.int32, (256, 128), 1)).astype(jnp.float32)
+    return jnp.dot(sums, pick, precision=HIGHEST, preferred_element_type=jnp.float32)
 
 
 def weigh(sums):
@@ -215,10 +246,11 @@
 
 
 def turn_basis_kernel(core_ref, own_ref, other_ref, left_ref, right_ref):
-    for at, ref in enumerate((own_ref, other_ref)):
-        turned = ref[0].T
-        left_ref[0, at * 128 : (at + 1) * 128, :] = turned[:, :WIDE]
-        right_ref[0, at * 128 : (at + 1) * 128, :] = turned[:, WIDE:]
+    for k in range(2):
+        for at, ref in enumerate((own_ref, other_ref)):
+            turned = ref[k].T
+            left_ref[k, at * 128 : (at + 1) * 128, :] = turned[:, :WIDE]
+            right_ref[k, at * 128 : (at + 1) * 128, :] = turned[:, WIDE:]
 
 
 def turn_basis(core, basis, other):
@@ -228,9 +260,9 @@
         out_shape=[jax.ShapeDtypeStruct((K, 256, WIDE), jnp.bfloat16)] * 2,
         grid_spec=pltpu.PrefetchScalarGridSpec(
             num_scalar_prefetch=1,
-            grid=(K,),
-            in_specs=[pl.BlockSpec((1, half, 128), lambda k, core: (k, core[0], 0))] * 2,
-            out_specs=[pl.BlockSpec((1, 256, WIDE), lambda k, core: (k, 0, 0))] * 2,
+            grid=(K // 2,),
+            in_specs=[pl.BlockSpec((2, half, 128), lambda k, core: (k, core[0], 0))] * 2,
+            out_specs=[pl.BlockSpec((2, 256, WIDE), lambda k, core: (k, 0, 0))] * 2,
         ),
         compiler_params=pltpu.CompilerParams(vmem_limit_bytes=8 * MB),
         cost_estimate=pl.CostEstimate(flops=0, bytes_accessed=8 * MB, transcendentals=0),
@@ -281,9 +313,7 @@
 
 
 def add_products(out_ref, sums, owners):
-    owner = lax.broadcasted_iota(jnp.int32, (256, 128), 0) // 32
-    pick = (owner == lax.broadcasted_iota(jnp.int32, (256, 128), 1)).astype(jnp.float32)
-    sums = jnp.dot(sums, pick, precision=HIGHEST, preferred_element_type=jnp.float32)
+    sums = pick_lanes(sums, 0)
     for at, owner in enumerate(owners):
         out_ref[pl.ds(owner, 1), :] += sums[at : at + 1]
 
@@ -443,10 +473,11 @@
     l1, l7 = toward(l0, "z", 1), toward(l0, "z", -1)
     b3, b5 = toward(b2, "z", 1), toward(b6, "z", -1)
     b4 = toward(b3, "z", 1)
+    b4, left_basis, right_basis = together(b4, left_basis, right_basis)
     r0 = jnp.concatenate([b, b1, b2, b3, b4, b5, b6, b7])
     r1, r3 = toward(r0, "y", 1), toward(r0, "y", -1)
     sums = gram(krylov_basis, field)
-    l1, l7, left_basis, right_basis = together(l1, l7, left_basis, right_basis)
+    l1, l7 = together(l1, l7)
     l2, l6 = toward(l1, "z", 1), toward(l7, "z", -1)
     x2 = toward(x1, "x", 1)
     l2, l6, sums = together(l2, l6, sums)

time: 127 us -> 122 us (0.961)
  Pallas kernels: 29.7 us -> 24.4 us
  blocking collectives: 31.2 us -> 26.8 us
  local copies, waits for them, and re-layouts: 5.45 us -> 8.14 us
    all_to_all x2, blocking collectives: 31.2 us -> 26.8 us  [sum_over(): return jnp.sum(lax.all_to_all(copies, axes, 0, 0), axis=0)]
    pallas_call x1, Pallas kernels: 6.28 us -> 2.55 us  [gram(): pl.pallas_call(gram_kernel, out_shape=jax.ShapeDtypeStruct((8, 128), jnp....]
    unnamed x42, local copies, waits for them, and re-layouts: 5.41 us -> 8.1 us
    pallas_call x1, Pallas kernels: 4.84 us -> 3.18 us  [turn_basis(): pl.pallas_call(turn_basis_kernel, out_shape=[jax.ShapeDtypeStruct((K, 256...]
  transfers between devices with their start and end apart: 26 -> 26, of which waited for: 10 -> 10; matrix products, arithmetic and copies ran while one was open for 1% -> 1% of each run, Pallas kernels for 17% -> 13%
where the time goes in v3:
time: 122 us
  starting transfers between devices  36.5 us (30%)
  blocking collectives  26.8 us (22%)
  Pallas kernels  24.4 us (20%)
  waiting for transfers between devices  23.9 us (20%)
  local copies, waits for them, and re-layouts  8.14 us (7%)
  between operations  1.74 us (1%)
    ppermute x23, starting transfers between devices, toward(): return lax.ppermute(value, axes, pairs)  33.1 us
    all_to_all x2, blocking collectives, sum_over(): return jnp.sum(lax.all_to_all(copies, axes, 0, 0), axis=0)  26.8 us
    ppermute x23, waiting for transfers between devices, toward(): return lax.ppermute(value, axes, pairs)  23.4 us
    pallas_call x3, Pallas kernels, project(): pl.pallas_call(kernel, out_shape=jax.ShapeDtypeStruct((8, 128), jnp.float...  13.7 us
    unnamed x42, local copies, waits for them, and re-layouts  8.1 us
    pallas_call x1, Pallas kernels, finish(): pl.pallas_call(functools.partial(finish_kernel, given), out_shape=[jax.Sh...  4.83 us
    ppermute x3, starting transfers between devices, swap_core(): return lax.ppermute(value, 'core', [(0, 1), (1, 0)])  3.42 us
    pallas_call x1, Pallas kernels, turn_basis(): pl.pallas_call(turn_basis_kernel, out_shape=[jax.ShapeDtypeStruct((K, 256...  3.18 us
  transfers between devices with their start and end apart: 26, of which 10 were waited for; matrix products, arithmetic and copies ran while one was open for 1% of the time, Pallas kernels for 13%

profile of v3, /device:TPU:1, one launch (start us, length us, event | category | flops | bytes accessed | tf_op | source)
XLA Modules:
  0.0 121.7 jit_solution(16036609798402555354)
XLA Ops:
  0.6 3.3 %collective-permute-start = (bf16[64,2048]{1,0:T(8,128)(2,1)}, bf16[64,2048]{1,0:T(8,128)(2,1)S(1)}, u32[]{:S(2)}, u32[]{:S(2)}) collective-permute-start(bf16[64,2048]{1,0:T(8,128)(2,1)} %param.9), channel_id=1, source_target_pairs={{0,4},{4,0},{1,5},{5,1},{2,6},{6,2},{3,7},{7,3},{8,12},{12,8},{9,1... | collective-permute-start | bytes 786440 | tf_op jit(solution)/shard_map/ppermute | solution.py:42
  5.4 1.1 collective-permute-start.3
  6.9 5.2 %collective-permute-start.1 = (bf16[128,512]{1,0:T(8,128)(2,1)S(1)}, bf16[128,512]{1,0:T(8,128)(2,1)S(1)}, u32[]{:S(2)}, u32[]{:S(2)}) collective-permute-start(bf16[128,512]{1,0:T(8,128)(2,1)S(1)} %pad_maximum_fusion), channel_id=1, source_target_pairs={{0,8},{4,60},{8,16},{12,4},{16,24},{20,12},{24,32},{28,20},{32,40}... | collective-permute-start | bytes 393224 | tf_op jit(solution)/shard_map/ppermute | solution.py:38
  12.8 1.2 %collective-permute-done.1 = bf16[128,512]{1,0:T(8,128)(2,1)S(1)} collective-permute-done((bf16[128,512]{1,0:T(8,128)(2,1)S(1)}, bf16[128,512]{1,0:T(8,128)(2,1)S(1)}, u32[]{:S(2)}, u32[]{:S(2)}) %collective-permute-start.1) | collective-permute-done | bytes 131104 | tf_op jit(solution)/shard_map/ppermute | solution.py:38
  14.1 3.1 %collective-permute-done.2 = bf16[128,512]{1,0:T(8,128)(2,1)S(1)} collective-permute-done((bf16[128,512]{1,0:T(8,128)(2,1)S(1)}, bf16[128,512]{1,0:T(8,128)(2,1)S(1)}, u32[]{:S(2)}, u32[]{:S(2)}) %collective-permute-start.2) | collective-permute-done | bytes 131104 | tf_op jit(solution)/shard_map/ppermute | solution.py:38
  17.1 2.1 %collective-permute-start.5 = (bf16[128,512]{1,0:T(8,128)(2,1)S(1)}, bf16[128,512]{1,0:T(8,128)(2,1)S(1)}, u32[]{:S(2)}, u32[]{:S(2)}) collective-permute-start(bf16[128,512]{1,0:T(8,128)(2,1)S(1)} %collective-permute-done.1), channel_id=1, source_target_pairs={{0,8},{4,60},{8,16},{12,4},{16,24},{20,12},{24,32},{28,20},{32,40}... | collective-permute-start | bytes 393224 | tf_op jit(solution)/shard_map/ppermute | solution.py:38
  19.3 2.7 %collective-permute-start.9 = (bf16[128,512]{1,0:T(8,128)(2,1)S(1)}, bf16[128,512]{1,0:T(8,128)(2,1)S(1)}, u32[]{:S(2)}, u32[]{:S(2)}) collective-permute-start(bf16[128,512]{1,0:T(8,128)(2,1)S(1)} %collective-permute-done.3), channel_id=1, source_target_pairs={{0,64},{4,196},{64,128},{68,4},{128,192},{132,68},{192,0},{196,132... | collective-permute-start | bytes 393224 | tf_op jit(solution)/shard_map/ppermute | solution.py:38
  22.1 2.6 %collective-permute-start.6 = (bf16[128,512]{1,0:T(8,128)(2,1)S(1)}, bf16[128,512]{1,0:T(8,128)(2,1)S(1)}, u32[]{:S(2)}, u32[]{:S(2)}) collective-permute-start(bf16[128,512]{1,0:T(8,128)(2,1)S(1)} %collective-permute-done.5), channel_id=1, source_target_pairs={{0,8},{4,60},{8,16},{12,4},{16,24},{20,12},{24,32},{28,20},{32,40}... | collective-permute-start | bytes 393224 | tf_op jit(solution)/shard_map/ppermute | solution.py:38
  24.9 1.8 %collective-permute-done.6 = bf16[128,512]{1,0:T(8,128)(2,1)S(1)} collective-permute-done((bf16[128,512]{1,0:T(8,128)(2,1)S(1)}, bf16[128,512]{1,0:T(8,128)(2,1)S(1)}, u32[]{:S(2)}, u32[]{:S(2)}) %collective-permute-start.6) | collective-permute-done | bytes 131104 | tf_op jit(solution)/shard_map/ppermute | solution.py:38
  26.7 3.1 %collective-permute-start.7 = (bf16[128,512]{1,0:T(8,128)(2,1)S(1)}, bf16[128,512]{1,0:T(8,128)(2,1)S(1)}, u32[]{:S(2)}, u32[]{:S(2)}) collective-permute-start(bf16[128,512]{1,0:T(8,128)(2,1)S(1)} %collective-permute-done.6), channel_id=1, source_target_pairs={{0,8},{4,60},{8,16},{12,4},{16,24},{20,12},{24,32},{28,20},{32,40}... | collective-permute-start | bytes 393224 | tf_op jit(solution)/shard_map/ppermute | solution.py:38
  30.1 0.9 copy-done
  31.2 2.7 %collective-permute-start.17 = (bf16[256,1024]{1,0:T(8,128)(2,1)S(1)}, bf16[256,1024]{1,0:T(8,128)(2,1)}, u32[]{:S(2)}, u32[]{:S(2)}) collective-permute-start(bf16[256,1024]{1,0:T(8,128)(2,1)S(1)} %turn_inputs.1.refs_0_), channel_id=1, source_target_pairs={{0,1},{4,7},{1,2},{5,4},{2,3},{6,5},{3,0},{7,6},{8,9},{12,15},{9,1... | collective-permute-start | bytes 1572872 | tf_op jit(solution)/shard_map/ppermute | solution.py:38
  34.0 3.2 %turn_basis.1 = (bf16[8,256,512]{2,1,0:T(8,128)(2,1)S(1)}, bf16[8,256,512]{2,1,0:T(8,128)(2,1)S(1)}) custom-call(s32[1]{0:T(128)} %bitcast.5.core_ref, bf16[8,2048,128]{2,1,0:T(8,128)(2,1)} %basis_ref.3, bf16[8,2048,128]{2,1,0:T(8,128)(2,1)S(1)} %collective-permute-done.8.other_ref), custom_call_target="tpu_custom_call" | custom-call | bytes 8388608 | tf_op jit(solution)/shard_map/turn_basis/pallas_call | solution.py:258
  37.2 1.4 %copy-done.1 = bf16[8,256,512]{2,1,0:T(8,128)(2,1)} copy-done((bf16[8,256,512]{2,1,0:T(8,128)(2,1)}, bf16[8,256,512]{2,1,0:T(8,128)(2,1)S(1)}, u32[]{:S(2)}) %copy-start.1) | copy-done | bytes 2097176
  38.5 1.3 %copy-done.3 = bf16[8,256,512]{2,1,0:T(8,128)(2,1)} copy-done((bf16[8,256,512]{2,1,0:T(8,128)(2,1)}, bf16[8,256,512]{2,1,0:T(8,128)(2,1)S(1)}, u32[]{:S(2)}) %copy-start.3) | copy-done | bytes 2097176
  39.9 2.2 %collective-permute-start.22 = (bf16[1024,512]{1,0:T(8,128)(2,1)S(1)}, bf16[1024,512]{1,0:T(8,128)(2,1)S(1)}, u32[]{:S(2)}, u32[]{:S(2)}) collective-permute-start(bf16[1024,512]{1,0:T(8,128)(2,1)S(1)} %constant_dynamic-update-slice_fusion.5.refs_4_), channel_id=1, source_target_pairs={{0,64},{4,196},{64,128},{68,4},{128,192},{132,68},{192,0},{196,132... | collective-permute-start | bytes 3145736 | tf_op jit(solution)/shard_map/ppermute | solution.py:38
  42.2 1.6 %collective-permute-done.11.refs_10_ = bf16[512,512]{1,0:T(8,128)(2,1)S(1)} collective-permute-done((bf16[512,512]{1,0:T(8,128)(2,1)S(1)}, bf16[512,512]{1,0:T(8,128)(2,1)S(1)}, u32[]{:S(2)}, u32[]{:S(2)}) %collective-permute-start.11) | collective-permute-done | bytes 524320 | tf_op jit(solution)/shard_map/ppermute | solution.py:38
  43.8 1.2 collective-permute-start.12
  46.1 7.2 %collective-permute-done.12.refs_6_ = bf16[512,512]{1,0:T(8,128)(2,1)} collective-permute-done((bf16[512,512]{1,0:T(8,128)(2,1)S(1)}, bf16[512,512]{1,0:T(8,128)(2,1)}, u32[]{:S(2)}, u32[]{:S(2)}) %collective-permute-start.12) | collective-permute-done | bytes 524320 | tf_op jit(solution)/shard_map/ppermute | solution.py:38
  53.3 2.3 %collective-permute-start.18 = (bf16[256,1024]{1,0:T(8,128)(2,1)}, bf16[256,1024]{1,0:T(8,128)(2,1)}, u32[]{:S(2)}, u32[]{:S(2)}) collective-permute-start(bf16[256,1024]{1,0:T(8,128)(2,1)} %collective-permute-done.17.refs_1_), channel_id=1, source_target_pairs={{0,1},{4,7},{1,2},{5,4},{2,3},{6,5},{3,0},{7,6},{8,9},{12,15},{9,1... | collective-permute-start | bytes 1572872 | tf_op jit(solution)/shard_map/ppermute | solution.py:38
  55.6 2.6 %gram.1.before_ref = f32[8,128]{1,0:T(8,128)S(1)} custom-call(bf16[8,2048,128]{2,1,0:T(8,128)(2,1)S(1)} %copy-done.12, f32[2048,128]{1,0:T(8,128)S(1)} %copy-done.13), custom_call_target="tpu_custom_call" | custom-call | flops 25165824 | bytes 18874368 | tf_op jit(solution)/shard_map/gram/pallas_call | solution.py:104
  60.7 4.2 %collective-permute-start.25 = (bf16[1024,512]{1,0:T(8,128)(2,1)S(1)}, bf16[1024,512]{1,0:T(8,128)(2,1)}, u32[]{:S(2)}, u32[]{:S(2)}) collective-permute-start(bf16[1024,512]{1,0:T(8,128)(2,1)S(1)} %collective-permute-done.22.refs_5_), channel_id=1, source_target_pairs={{0,64},{4,196},{64,128},{68,4},{128,192},{132,68},{192,0},{196,132... | collective-permute-start | bytes 3145736 | tf_op jit(solution)/shard_map/ppermute | solution.py:38
  65.0 4.4 %collective-permute-done.23.refs_6_ = bf16[1024,512]{1,0:T(8,128)(2,1)} collective-permute-done((bf16[1024,512]{1,0:T(8,128)(2,1)S(1)}, bf16[1024,512]{1,0:T(8,128)(2,1)}, u32[]{:S(2)}, u32[]{:S(2)}) %collective-permute-start.23) | collective-permute-done | bytes 1048608 | tf_op jit(solution)/shard_map/ppermute | solution.py:38
  69.4 1.6 %copy-done.4 = bf16[8,256,512]{2,1,0:T(8,128)(2,1)S(1)} copy-done((bf16[8,256,512]{2,1,0:T(8,128)(2,1)S(1)}, bf16[8,256,512]{2,1,0:T(8,128)(2,1)}, u32[]{:S(2)}) %copy-start.4) | copy-done | bytes 2097176
  71.0 1.0 copy-done.10
  72.0 4.5 %right_kernel.1.before_ref = f32[8,128]{1,0:T(8,128)S(1)} custom-call(s32[4]{0:T(128)S(1)} %pad_add_fusion.place_ref, bf16[8,256,512]{2,1,0:T(8,128)(2,1)S(1)} %copy-done.4, f32[8,128]{1,0:T(8,128)S(1)} %gram.1.before_ref, bf16[256,1024]{1,0:T(8,128)(2,1)S(1)} %turn_inputs.1.refs_0_, bf16[256,1024]{1,0:T(8,128)(2,1)} %collective-permute-done.17.refs_1_, ...), custom_call_target="tpu_custom_call" | custom-call | flops 4026531840 | bytes 4194304 | tf_op jit(solution)/shard_map/right_kernel/pallas_call | solution.py:426
  77.0 5.4 %left_kernel.1.before_ref = f32[8,128]{1,0:T(8,128)S(1)} custom-call(s32[4]{0:T(128)S(1)} %pad_add_fusion.place_ref, bf16[8,256,512]{2,1,0:T(8,128)(2,1)S(1)} %copy-done.2, f32[8,128]{1,0:T(8,128)S(1)} %right_kernel.1.before_ref, bf16[256,1024]{1,0:T(8,128)(2,1)S(1)} %turn_inputs.1.refs_0_, bf16[256,1024]{1,0:T(8,128)(2,1)} %collective-permute-done.17.refs_1_, ...), custom_call_target="tpu_custom_call" | custom-call | flops 5234491392 | bytes 4194304 | tf_op jit(solution)/shard_map/left_kernel/pallas_call | solution.py:426
  82.3 3.1 %collective-permute-done.24.refs_4_ = bf16[512,512]{1,0:T(8,128)(2,1)S(1)} collective-permute-done((bf16[512,512]{1,0:T(8,128)(2,1)}, bf16[512,512]{1,0:T(8,128)(2,1)S(1)}, u32[]{:S(2)}, u32[]{:S(2)}) %collective-permute-start.24) | collective-permute-done | bytes 524320 | tf_op jit(solution)/shard_map/ppermute | solution.py:38
  85.4 3.8 %far_kernel.1 = f32[8,128]{1,0:T(8,128)S(1)} custom-call(s32[4]{0:T(128)S(1)} %pad_add_fusion.place_ref, bf16[8,256,512]{2,1,0:T(8,128)(2,1)S(1)} %copy-done.2, bf16[8,256,512]{2,1,0:T(8,128)(2,1)S(1)} %copy-done.4, f32[8,128]{1,0:T(8,128)S(1)} %left_kernel.1.before_ref, bf16[256,1024]{1,0:T(8,128)(2,1)S(1)} %turn_inputs.1.refs_0_, ...), custom_call_target="tpu_custom_call" | custom-call | flops 2550136832 | bytes 4194304 | tf_op jit(solution)/shard_map/far_kernel/pallas_call | solution.py:426
  89.2 14.6 %all_to_all.20 = f32[16,8,128]{2,1,0:T(8,128)S(1)} all-to-all(f32[16,8,128]{2,1,0:T(8,128)S(1)} %broadcast_in_dim.13), channel_id=1, replica_groups=mesh['y'=4,'z'=8,'core'=2,'x'=4] {'z','core'}, dimensions={0} | all-to-all | bytes 131072 | tf_op jit(solution)/shard_map/all_to_all | solution.py:51
  103.9 12.2 %all_to_all.21 = f32[16,8,128]{2,1,0:T(8,128)S(1)} all-to-all(f32[16,8,128]{2,1,0:T(8,128)S(1)} %broadcast_in_dim.14), channel_id=1, replica_groups=mesh['y'=4,'z'=8,'core'=2,'x'=4] {'y','x'}, dimensions={0} | all-to-all | bytes 131072 | tf_op jit(solution)/shard_map/all_to_all | solution.py:51
  116.1 4.8 %finish.3 = (bf16[2048,128]{1,0:T(8,128)(2,1)}, f32[1,9]{1,0:T(1,128)}, f32[4,8]{1,0:T(4,128)}, s32[1]{0:T(128)}) custom-call(f32[1,1]{1,0:T(1,128)} %constant.11.clone.1.squares_ref, f32[8,128]{1,0:T(8,128)S(1)} %reduce_sum.41.sums_ref, f32[8,128]{1,0:T(8,128)S(1)} %pad.4.rotation_ref, bf16[8,2048,128]{2,1,0:T(8,128)(2,1)} %basis_ref.3, f32[2048,128]{1,0:T(8,128)} %field_ref.2), custom_call_target="tpu_custom_call" | custom-call | flops 6291456 | bytes 6291456 | tf_op jit(solution)/shard_map/finish/pallas_call | solution.py:230
  (82 shorter events, 7.6 us)
Async XLA Ops:
  0.6 4.7 %collective-permute-start = (bf16[64,2048]{1,0:T(8,128)(2,1)}, bf16[64,2048]{1,0:T(8,128)(2,1)S(1)}, u32[]{:S(2)}, u32[]{:S(2)}) collective-permute-start(bf16[64,2048]{1,0:T(8,128)(2,1)} %param.9), channel_id=1, source_target_pairs={{0,4},{4,0},{1,5},{5,1},{2,6},{6,2},{3,7},{7,3},{8,12},{12,8},{9,1... | collective-permute-start | bytes 786440 | tf_op jit(solution)/shard_map/ppermute | solution.py:42
  5.4 6.8 %collective-permute-start.3 = (bf16[128,512]{1,0:T(8,128)(2,1)S(1)}, bf16[128,512]{1,0:T(8,128)(2,1)S(1)}, u32[]{:S(2)}, u32[]{:S(2)}) collective-permute-start(bf16[128,512]{1,0:T(8,128)(2,1)S(1)} %pad_maximum_fusion.1), channel_id=1, source_target_pairs={{0,64},{4,196},{64,128},{68,4},{128,192},{132,68},{192,0},{196,132... | collective-permute-start | bytes 393224 | tf_op jit(solution)/shard_map/ppermute | solution.py:38
  6.4 6.4 %collective-permute-start.4 = (bf16[128,512]{1,0:T(8,128)(2,1)S(1)}, bf16[128,512]{1,0:T(8,128)(2,1)S(1)}, u32[]{:S(2)}, u32[]{:S(2)}) collective-permute-start(bf16[128,512]{1,0:T(8,128)(2,1)S(1)} %pad_maximum_fusion.1), channel_id=1, source_target_pairs={{0,192},{4,68},{64,0},{68,132},{128,64},{132,196},{192,128},{196,4... | collective-permute-start | bytes 393224 | tf_op jit(solution)/shard_map/ppermute | solution.py:38
  6.9 7.1 %collective-permute-start.1 = (bf16[128,512]{1,0:T(8,128)(2,1)S(1)}, bf16[128,512]{1,0:T(8,128)(2,1)S(1)}, u32[]{:S(2)}, u32[]{:S(2)}) collective-permute-start(bf16[128,512]{1,0:T(8,128)(2,1)S(1)} %pad_maximum_fusion), channel_id=1, source_target_pairs={{0,8},{4,60},{8,16},{12,4},{16,24},{20,12},{24,32},{28,20},{32,40}... | collective-permute-start | bytes 393224 | tf_op jit(solution)/shard_map/ppermute | solution.py:38
  12.1 5.0 %collective-permute-start.2 = (bf16[128,512]{1,0:T(8,128)(2,1)S(1)}, bf16[128,512]{1,0:T(8,128)(2,1)S(1)}, u32[]{:S(2)}, u32[]{:S(2)}) collective-permute-start(bf16[128,512]{1,0:T(8,128)(2,1)S(1)} %pad_maximum_fusion), channel_id=1, source_target_pairs={{0,56},{4,12},{8,0},{12,20},{16,8},{20,28},{24,16},{28,36},{32,24}... | collective-permute-start | bytes 393224 | tf_op jit(solution)/shard_map/ppermute | solution.py:38
  17.1 14.1 %collective-permute-start.8 = (bf16[8,2048,128]{2,1,0:T(8,128)(2,1)}, bf16[8,2048,128]{2,1,0:T(8,128)(2,1)S(1)}, u32[]{:S(2)}, u32[]{:S(2)}) collective-permute-start(bf16[8,2048,128]{2,1,0:T(8,128)(2,1)} %basis_ref.3), channel_id=1, source_target_pairs={{0,4},{4,0},{1,5},{5,1},{2,6},{6,2},{3,7},{7,3},{8,12},{12,8},{9,1... | collective-permute-start | bytes 12582920 | tf_op jit(solution)/shard_map/ppermute | solution.py:42
  17.1 5.0 %collective-permute-start.5 = (bf16[128,512]{1,0:T(8,128)(2,1)S(1)}, bf16[128,512]{1,0:T(8,128)(2,1)S(1)}, u32[]{:S(2)}, u32[]{:S(2)}) collective-permute-start(bf16[128,512]{1,0:T(8,128)(2,1)S(1)} %collective-permute-done.1), channel_id=1, source_target_pairs={{0,8},{4,60},{8,16},{12,4},{16,24},{20,12},{24,32},{28,20},{32,40}... | collective-permute-start | bytes 393224 | tf_op jit(solution)/shard_map/ppermute | solution.py:38
  19.3 5.5 %collective-permute-start.9 = (bf16[128,512]{1,0:T(8,128)(2,1)S(1)}, bf16[128,512]{1,0:T(8,128)(2,1)S(1)}, u32[]{:S(2)}, u32[]{:S(2)}) collective-permute-start(bf16[128,512]{1,0:T(8,128)(2,1)S(1)} %collective-permute-done.3), channel_id=1, source_target_pairs={{0,64},{4,196},{64,128},{68,4},{128,192},{132,68},{192,0},{196,132... | collective-permute-start | bytes 393224 | tf_op jit(solution)/shard_map/ppermute | solution.py:38
  21.9 7.9 %collective-permute-start.20 = (bf16[128,512]{1,0:T(8,128)(2,1)S(1)}, bf16[128,512]{1,0:T(8,128)(2,1)S(1)}, u32[]{:S(2)}, u32[]{:S(2)}) collective-permute-start(bf16[128,512]{1,0:T(8,128)(2,1)S(1)} %collective-permute-done.2), channel_id=1, source_target_pairs={{0,56},{4,12},{8,0},{12,20},{16,8},{20,28},{24,16},{28,36},{32,24}... | collective-permute-start | bytes 393224 | tf_op jit(solution)/shard_map/ppermute | solution.py:38
  22.0 7.9 %collective-permute-start.16 = (bf16[1024,128]{1,0:T(8,128)(2,1)}, bf16[1024,128]{1,0:T(8,128)(2,1)S(1)}, u32[]{:S(2)}, u32[]{:S(2)}) collective-permute-start(bf16[1024,128]{1,0:T(8,128)(2,1)} %own_ref.1), channel_id=1, source_target_pairs={{0,4},{4,0},{1,5},{5,1},{2,6},{6,2},{3,7},{7,3},{8,12},{12,8},{9,1... | collective-permute-start | bytes 786440 | tf_op jit(solution)/shard_map/ppermute | solution.py:42
  22.1 4.6 %collective-permute-start.6 = (bf16[128,512]{1,0:T(8,128)(2,1)S(1)}, bf16[128,512]{1,0:T(8,128)(2,1)S(1)}, u32[]{:S(2)}, u32[]{:S(2)}) collective-permute-start(bf16[128,512]{1,0:T(8,128)(2,1)S(1)} %collective-permute-done.5), channel_id=1, source_target_pairs={{0,8},{4,60},{8,16},{12,4},{16,24},{20,12},{24,32},{28,20},{32,40}... | collective-permute-start | bytes 393224 | tf_op jit(solution)/shard_map/ppermute | solution.py:38
  24.8 17.4 %collective-permute-start.10 = (bf16[512,512]{1,0:T(8,128)(2,1)S(1)}, bf16[512,512]{1,0:T(8,128)(2,1)S(1)}, u32[]{:S(2)}, u32[]{:S(2)}) collective-permute-start(bf16[512,512]{1,0:T(8,128)(2,1)S(1)} %constant_dynamic-update-slice_fusion.refs_4_), channel_id=1, source_target_pairs={{0,8},{4,60},{8,16},{12,4},{16,24},{20,12},{24,32},{28,20},{32,40}... | collective-permute-start | bytes 1572872 | tf_op jit(solution)/shard_map/ppermute | solution.py:38
  26.7 13.1 %collective-permute-start.7 = (bf16[128,512]{1,0:T(8,128)(2,1)S(1)}, bf16[128,512]{1,0:T(8,128)(2,1)S(1)}, u32[]{:S(2)}, u32[]{:S(2)}) collective-permute-start(bf16[128,512]{1,0:T(8,128)(2,1)S(1)} %collective-permute-done.6), channel_id=1, source_target_pairs={{0,8},{4,60},{8,16},{12,4},{16,24},{20,12},{24,32},{28,20},{32,40}... | collective-permute-start | bytes 393224 | tf_op jit(solution)/shard_map/ppermute | solution.py:38
  29.8 10.0 %collective-permute-start.21 = (bf16[128,512]{1,0:T(8,128)(2,1)S(1)}, bf16[128,512]{1,0:T(8,128)(2,1)S(1)}, u32[]{:S(2)}, u32[]{:S(2)}) collective-permute-start(bf16[128,512]{1,0:T(8,128)(2,1)S(1)} %collective-permute-done.20), channel_id=1, source_target_pairs={{0,56},{4,12},{8,0},{12,20},{16,8},{20,28},{24,16},{28,36},{32,24}... | collective-permute-start | bytes 393224 | tf_op jit(solution)/shard_map/ppermute | solution.py:38
  30.0 13.8 %collective-permute-start.11 = (bf16[512,512]{1,0:T(8,128)(2,1)S(1)}, bf16[512,512]{1,0:T(8,128)(2,1)S(1)}, u32[]{:S(2)}, u32[]{:S(2)}) collective-permute-start(bf16[512,512]{1,0:T(8,128)(2,1)S(1)} %constant_dynamic-update-slice_fusion.refs_4_), channel_id=1, source_target_pairs={{0,56},{4,12},{8,0},{12,20},{16,8},{20,28},{24,16},{28,36},{32,24}... | collective-permute-start | bytes 1572872 | tf_op jit(solution)/shard_map/ppermute | solution.py:38
  31.2 24.4 %copy-start.12 = (bf16[8,2048,128]{2,1,0:T(8,128)(2,1)S(1)}, bf16[8,2048,128]{2,1,0:T(8,128)(2,1)}, u32[]{:S(2)}) copy-start(bf16[8,2048,128]{2,1,0:T(8,128)(2,1)} %basis_ref.3) | copy-start | bytes 12582916
  31.2 24.4 %copy-start.13 = (f32[2048,128]{1,0:T(8,128)S(1)}, f32[2048,128]{1,0:T(8,128)}, u32[]{:S(2)}) copy-start(f32[2048,128]{1,0:T(8,128)} %field_ref.2) | copy-start | bytes 3145732
  31.2 14.0 %collective-permute-start.17 = (bf16[256,1024]{1,0:T(8,128)(2,1)S(1)}, bf16[256,1024]{1,0:T(8,128)(2,1)}, u32[]{:S(2)}, u32[]{:S(2)}) collective-permute-start(bf16[256,1024]{1,0:T(8,128)(2,1)S(1)} %turn_inputs.1.refs_0_), channel_id=1, source_target_pairs={{0,1},{4,7},{1,2},{5,4},{2,3},{6,5},{3,0},{7,6},{8,9},{12,15},{9,1... | collective-permute-start | bytes 1572872 | tf_op jit(solution)/shard_map/ppermute | solution.py:38
  39.9 20.8 %collective-permute-start.22 = (bf16[1024,512]{1,0:T(8,128)(2,1)S(1)}, bf16[1024,512]{1,0:T(8,128)(2,1)S(1)}, u32[]{:S(2)}, u32[]{:S(2)}) collective-permute-start(bf16[1024,512]{1,0:T(8,128)(2,1)S(1)} %constant_dynamic-update-slice_fusion.5.refs_4_), channel_id=1, source_target_pairs={{0,64},{4,196},{64,128},{68,4},{128,192},{132,68},{192,0},{196,132... | collective-permute-start | bytes 3145736 | tf_op jit(solution)/shard_map/ppermute | solution.py:38
  42.2 18.6 %copy-start.5 = (bf16[512,512]{1,0:T(8,128)(2,1)}, bf16[512,512]{1,0:T(8,128)(2,1)S(1)}, u32[]{:S(2)}) copy-start(bf16[512,512]{1,0:T(8,128)(2,1)S(1)} %collective-permute-done.10.refs_5_) | copy-start | bytes 1572868
  43.8 17.0 %copy-start.7 = (bf16[512,512]{1,0:T(8,128)(2,1)}, bf16[512,512]{1,0:T(8,128)(2,1)S(1)}, u32[]{:S(2)}) copy-start(bf16[512,512]{1,0:T(8,128)(2,1)S(1)} %collective-permute-done.11.refs_10_) | copy-start | bytes 1572868
  43.8 9.5 %collective-permute-start.12 = (bf16[512,512]{1,0:T(8,128)(2,1)S(1)}, bf16[512,512]{1,0:T(8,128)(2,1)}, u32[]{:S(2)}, u32[]{:S(2)}) collective-permute-start(bf16[512,512]{1,0:T(8,128)(2,1)S(1)} %collective-permute-done.10.refs_5_), channel_id=1, source_target_pairs={{0,8},{4,60},{8,16},{12,4},{16,24},{20,12},{24,32},{28,20},{32,40}... | collective-permute-start | bytes 1572872 | tf_op jit(solution)/shard_map/ppermute | solution.py:38
  44.9 24.5 %collective-permute-start.23 = (bf16[1024,512]{1,0:T(8,128)(2,1)S(1)}, bf16[1024,512]{1,0:T(8,128)(2,1)}, u32[]{:S(2)}, u32[]{:S(2)}) collective-permute-start(bf16[1024,512]{1,0:T(8,128)(2,1)S(1)} %constant_dynamic-update-slice_fusion.5.refs_4_), channel_id=1, source_target_pairs={{0,192},{4,68},{64,0},{68,132},{128,64},{132,196},{192,128},{196,4... | collective-permute-start | bytes 3145736 | tf_op jit(solution)/shard_map/ppermute | solution.py:38
  44.9 13.5 %collective-permute-start.13 = (bf16[512,512]{1,0:T(8,128)(2,1)S(1)}, bf16[512,512]{1,0:T(8,128)(2,1)}, u32[]{:S(2)}, u32[]{:S(2)}) collective-permute-start(bf16[512,512]{1,0:T(8,128)(2,1)S(1)} %collective-permute-done.11.refs_10_), channel_id=1, source_target_pairs={{0,56},{4,12},{8,0},{12,20},{16,8},{20,28},{24,16},{28,36},{32,24}... | collective-permute-start | bytes 1572872 | tf_op jit(solution)/shard_map/ppermute | solution.py:38
  45.3 14.1 %collective-permute-start.19 = (bf16[256,1024]{1,0:T(8,128)(2,1)S(1)}, bf16[256,1024]{1,0:T(8,128)(2,1)S(1)}, u32[]{:S(2)}, u32[]{:S(2)}) collective-permute-start(bf16[256,1024]{1,0:T(8,128)(2,1)S(1)} %turn_inputs.1.refs_0_), channel_id=1, source_target_pairs={{0,3},{4,5},{1,0},{5,6},{2,1},{6,7},{3,2},{7,4},{8,11},{12,13},{9,... | collective-permute-start | bytes 1572872 | tf_op jit(solution)/shard_map/ppermute | solution.py:38
  53.3 11.8 %collective-permute-start.18 = (bf16[256,1024]{1,0:T(8,128)(2,1)}, bf16[256,1024]{1,0:T(8,128)(2,1)}, u32[]{:S(2)}, u32[]{:S(2)}) collective-permute-start(bf16[256,1024]{1,0:T(8,128)(2,1)} %collective-permute-done.17.refs_1_), channel_id=1, source_target_pairs={{0,1},{4,7},{1,2},{5,4},{2,3},{6,5},{3,0},{7,6},{8,9},{12,15},{9,1... | collective-permute-start | bytes 1572872 | tf_op jit(solution)/shard_map/ppermute | solution.py:38
  58.5 18.1 %collective-permute-start.14 = (bf16[512,512]{1,0:T(8,128)(2,1)}, bf16[512,512]{1,0:T(8,128)(2,1)}, u32[]{:S(2)}, u32[]{:S(2)}) collective-permute-start(bf16[512,512]{1,0:T(8,128)(2,1)} %collective-permute-done.12.refs_6_), channel_id=1, source_target_pairs={{0,8},{4,60},{8,16},{12,4},{16,24},{20,12},{24,32},{28,20},{32,40}... | collective-permute-start | bytes 1572872 | tf_op jit(solution)/shard_map/ppermute | solution.py:38
  60.2 16.4 %collective-permute-start.15 = (bf16[512,512]{1,0:T(8,128)(2,1)}, bf16[512,512]{1,0:T(8,128)(2,1)}, u32[]{:S(2)}, u32[]{:S(2)}) collective-permute-start(bf16[512,512]{1,0:T(8,128)(2,1)} %collective-permute-done.13.refs_9_), channel_id=1, source_target_pairs={{0,56},{4,12},{8,0},{12,20},{16,8},{20,28},{24,16},{28,36},{32,24}... | collective-permute-start | bytes 1572872 | tf_op jit(solution)/shard_map/ppermute | solution.py:38
  60.7 24.7 %collective-permute-start.25 = (bf16[1024,512]{1,0:T(8,128)(2,1)S(1)}, bf16[1024,512]{1,0:T(8,128)(2,1)}, u32[]{:S(2)}, u32[]{:S(2)}) collective-permute-start(bf16[1024,512]{1,0:T(8,128)(2,1)S(1)} %collective-permute-done.22.refs_5_), channel_id=1, source_target_pairs={{0,64},{4,196},{64,128},{68,4},{128,192},{132,68},{192,0},{196,132... | collective-permute-start | bytes 3145736 | tf_op jit(solution)/shard_map/ppermute | solution.py:38
  64.9 12.0 %copy-start.15 = (f32[8,4]{0,1:T(4,128)S(1)}, f32[8,4]{0,1:T(4,128)}, u32[]{:S(2)}) copy-start(f32[8,4]{0,1:T(4,128)} %param.11) | copy-start | bytes 388
  76.6 8.8 %collective-permute-start.24 = (bf16[512,512]{1,0:T(8,128)(2,1)}, bf16[512,512]{1,0:T(8,128)(2,1)S(1)}, u32[]{:S(2)}, u32[]{:S(2)}) collective-permute-start(bf16[512,512]{1,0:T(8,128)(2,1)} %collective-permute-done.14.refs_7_), channel_id=1, source_target_pairs={{0,8},{4,60},{8,16},{12,4},{16,24},{20,12},{24,32},{28,20},{32,40}... | collective-permute-start | bytes 1572872 | tf_op jit(solution)/shard_map/ppermute | solution.py:38
  89.2 32.3 %copy-start.14 = (f32[2048,128]{1,0:T(8,128)S(1)}, f32[2048,128]{1,0:T(8,128)}, u32[]{:S(2)}) copy-start(f32[2048,128]{1,0:T(8,128)} %field_ref.2) | copy-start | bytes 3145732
  (10 other events, 33.7 us)

commit v4 on v3

--- a/solution.py
+++ b/solution.py
@@ -66,7 +66,7 @@
     return jnp.sum(value, axis=axis, keepdims=True)
 
 
-def gram_kernel(basis_ref, field_ref, out_ref, cross_ref, dots_ref):
+def gram_kernel(before_ref, basis_ref, field_ref, out_ref, cross_ref, dots_ref):
     at_step = pl.program_id(0)
 
     @pl.when(at_step == 0)
@@ -96,16 +96,18 @@
         row, lane = cells()
         for k in range(K):
             out = jnp.where((row == k) & (lane == DOTS), total_of(dots_ref[k]), out)
-        out_ref[...] = jnp.where((row == 0) & (lane == SELF), total_of(dots_ref[K]), out)
-
-
-def gram(basis, field):
+        out = jnp.where((row == 0) & (lane == SELF), total_of(dots_ref[K]), out)
+        out_ref[...] = before_ref[...] + out
+
+
+def gram(before, basis, field):
     rows = field.shape[0] // 4
     return pl.pallas_call(
         gram_kernel,
         out_shape=jax.ShapeDtypeStruct((8, 128), jnp.float32),
         grid=(4,),
         in_specs=[
+            pl.BlockSpec(memory_space=pltpu.VMEM),
             pl.BlockSpec((K, rows, 128), lambda t: (0, t, 0)),
             pl.BlockSpec((rows, 128), lambda t: (t, 0)),
         ],
@@ -117,7 +119,7 @@
         compiler_params=pltpu.CompilerParams(vmem_limit_bytes=8 * MB),
         cost_estimate=pl.CostEstimate(flops=24 * MB, bytes_accessed=18 * MB, transcendentals=0),
         name="gram",
-    )(basis, field)
+    )(before, basis, field)
 
 
 def matched(cross, slots, lane):
@@ -186,47 +188,47 @@
     return jnp.sum(sum_everywhere(parts))
 
 
-def finish_kernel(given, squares_ref, sums_ref, rotation_ref, basis_ref, field_ref, *out_refs):
-    new_ref, hessenberg_ref, influence_ref, little_ref, spread_ref = out_refs
-
-    @pl.when(pl.program_id(0) == 0)
-    def _():
-        sums = sums_ref[...]
-        column, squares, whole = weigh(sums)
-        little_ref[0] = (squares * 256.0 < whole).astype(jnp.int32)[0, 0]
-        if given:
-            squares = squares_ref[...]
-        length = jnp.sqrt(squares + 1e-06)
-        for k, weight in enumerate(spread(column)):
-            spread_ref[k] = weight
-        spread_ref[K] = jnp.broadcast_to(1.0 / length, (16, 128))
-        row, lane = cells()
-        across = total_of(jnp.where(lane == row, column, 0.0), 0)
-        hessenberg_ref[...] = jnp.where(lane[:1] == K, length, across)[:, : K + 1]
-        influence_ref[...] = lax.dot_general(
-            rotation_ref[...],
-            jnp.where(lane < K, sums, 0.0),
-            (((1,), (1,)), ((), ())),
-            precision=HIGHEST,
-            preferred_element_type=jnp.float32,
-        )[:TOP]
-
-    weights = [spread_ref[k] for k in range(K)]
-    scale = spread_ref[K]
-
-    def step(at, carry):
-        rows = pl.ds(pl.multiple_of(at * 16, 16), 16)
-        rest = take_off(weights, basis_ref, field_ref, rows)
-        new_ref[rows, :] = (rest * scale).astype(jnp.bfloat16)
-        return carry
-
-    lax.fori_loop(0, field_ref.shape[0] // 16, step, 0, unroll=4)
+def finish_kernel(given, squares_ref, sums_ref, rotation_ref, far_basis_ref, far_field_ref, *refs):
+    new_ref, hessenberg_ref, influence_ref, little_ref, basis_ref, field_ref, sems = refs
+    quarters = [slice(at, at + 512) for at in range(0, field_ref.shape[0], 512)]
+    pairs = []
+    for part in quarters:
+        pairs.append((far_basis_ref.at[:, part], basis_ref.at[:, part]))
+        pairs.append((far_field_ref.at[part], field_ref.at[part]))
+    copies = fetch(pairs, sems)
+    sums = sums_ref[...]
+    column, squares, whole = weigh(sums)
+    little_ref[0] = (squares * 256.0 < whole).astype(jnp.int32)[0, 0]
+    if given:
+        squares = squares_ref[...]
+    length = jnp.sqrt(squares + 1e-06)
+    weights = spread(column)
+    scale = jnp.broadcast_to(1.0 / length, (16, 128))
+    row, lane = cells()
+    across = total_of(jnp.where(lane == row, column, 0.0), 0)
+    hessenberg_ref[...] = jnp.where(lane[:1] == K, length, across)[:, : K + 1]
+    influence_ref[...] = lax.dot_general(
+        rotation_ref[...],
+        jnp.where(lane < K, sums, 0.0),
+        (((1,), (1,)), ((), ())),
+        precision=HIGHEST,
+        preferred_element_type=jnp.float32,
+    )[:TOP]
+    for at, part in enumerate(quarters):
+        copies[2 * at].wait()
+        copies[2 * at + 1].wait()
+
+        def step(i, carry):
+            rows = pl.ds(pl.multiple_of(part.start + i * 16, 16), 16)
+            rest = take_off(weights, basis_ref, field_ref, rows)
+            new_ref[rows, :] = (rest * scale).astype(jnp.bfloat16)
+            return carry
+
+        lax.fori_loop(0, 32, step, 0, unroll=4)
 
 
 def finish(given, squares, sums, rotation, basis, field):
-    vmem = pl.BlockSpec(memory_space=pltpu.VMEM)
-    rows = field.shape[0] // 4
-    block = pl.BlockSpec((rows, 128), lambda t: (t, 0))
+    vmem, anywhere = (pl.BlockSpec(memory_space=m) for m in (pltpu.VMEM, pl.ANY))
     return pl.pallas_call(
         functools.partial(finish_kernel, given),
         out_shape=[
@@ -235,10 +237,13 @@
             jax.ShapeDtypeStruct((TOP, SEQS), jnp.float32),
             jax.ShapeDtypeStruct((1,), jnp.int32),
         ],
-        grid=(4,),
-        in_specs=[vmem] * 3 + [pl.BlockSpec((K, rows, 128), lambda t: (0, t, 0)), block],
-        out_specs=[block, vmem, vmem, pl.BlockSpec(memory_space=pltpu.SMEM)],
-        scratch_shapes=[pltpu.VMEM((K + 1, 16, 128), jnp.float32)],
+        in_specs=[vmem] * 3 + [anywhere] * 2,
+        out_specs=[vmem] * 3 + [pl.BlockSpec(memory_space=pltpu.SMEM)],
+        scratch_shapes=[
+            pltpu.VMEM(basis.shape, jnp.bfloat16),
+            pltpu.VMEM(field.shape, jnp.float32),
+            pltpu.SemaphoreType.DMA((8,)),
+        ],
         compiler_params=pltpu.CompilerParams(vmem_limit_bytes=8 * MB),
         cost_estimate=pl.CostEstimate(flops=6 * MB, bytes_accessed=6 * MB, transcendentals=0),
         name="finish",
@@ -462,31 +467,31 @@
     )
     b1, b7 = toward(b, "z", 1), toward(b, "z", -1)
     a1, a3 = toward(a, "y", 1), toward(a, "y", -1)
-    b1, b7, a1, a3, krylov, layer = together(b1, b7, a1, a3, krylov_basis, layer_inputs)
+    b1, b7, a1, a3, krylov = together(b1, b7, a1, a3, krylov_basis)
+    b2, b6 = toward(b1, "z", 1), toward(b7, "z", -1)
+    a2 = toward(a1, "y", 1)
+    l0 = jnp.concatenate([a, a1, a2, a3])
+    l0, layer = together(l0, layer_inputs)
     x0 = turn_inputs(core_id, layer, swap_core(layer))
     x1, x3 = toward(x0, "x", 1), toward(x0, "x", -1)
     left_basis, right_basis = turn_basis(core_id, krylov, swap_core(krylov))
-    b2, b6 = toward(b1, "z", 1), toward(b7, "z", -1)
-    a2 = toward(a1, "y", 1)
-    l0 = jnp.concatenate([a, a1, a2, a3])
-    l0, field = together(l0, hessian_product)
     l1, l7 = toward(l0, "z", 1), toward(l0, "z", -1)
     b3, b5 = toward(b2, "z", 1), toward(b6, "z", -1)
     b4 = toward(b3, "z", 1)
     b4, left_basis, right_basis = together(b4, left_basis, right_basis)
     r0 = jnp.concatenate([b, b1, b2, b3, b4, b5, b6, b7])
     r1, r3 = toward(r0, "y", 1), toward(r0, "y", -1)
-    sums = gram(krylov_basis, field)
     l1, l7 = together(l1, l7)
     l2, l6 = toward(l1, "z", 1), toward(l7, "z", -1)
     x2 = toward(x1, "x", 1)
-    l2, l6, sums = together(l2, l6, sums)
+    l2, l6 = together(l2, l6)
     l3, l5 = toward(l2, "z", 1), toward(l6, "z", -1)
     r2 = toward(r1, "y", 1)
     inputs = [x0, x1, x2, x3]
     sems = pltpu.SemaphoreType.DMA((12,))
     basis = pltpu.VMEM(left_basis.shape, jnp.bfloat16)
     held = [basis, pltpu.VMEM((3, ZS * CHIP, WIDE), jnp.bfloat16), sems]
+    sums = jnp.zeros((8, 128), jnp.float32)
     sums = project(
         right_kernel, place, inputs, [right_basis], sums, [r0, r1, r3], pl.ANY, 6, held
     )
@@ -496,6 +501,7 @@
     held = [basis, pltpu.VMEM((ZS, YS * CHIP, WIDE), jnp.bfloat16), sems]
     lefts = [l0, l1, l2, l3, l5, l6, l7]
     sums = project(left_kernel, place, inputs, [left_basis], sums, lefts, pl.ANY, SEQS, held)
+    sums = gram(sums, krylov_basis, hessian_product)
     bases = [left_basis, right_basis]
     sums = project(far_kernel, place, inputs, bases, sums, [l4, r2], pltpu.VMEM, YS, [])
     rotation = jnp.pad(rotation.T, ((0, 8 - TOP), (0, 128 - K)))

time: 122 us -> 120 us (0.984)
  waiting for transfers between devices: 23.9 us -> 20.8 us
  local copies, waits for them, and re-layouts: 8.14 us -> 9.8 us
  starting transfers between devices: 36.5 us -> 38.1 us
  blocking collectives: 26.8 us -> 25.5 us
    ppermute x23, waiting for transfers between devices: 23.4 us -> 20.3 us  [toward(): return lax.ppermute(value, axes, pairs)]
    unnamed x42, local copies, waits for them, and re-layouts: 8.1 us -> 9.76 us
    ppermute x23, starting transfers between devices: 33.1 us -> 34.7 us  [toward(): return lax.ppermute(value, axes, pairs)]
    all_to_all x2, blocking collectives: 26.8 us -> 25.5 us  [sum_over(): return jnp.sum(lax.all_to_all(copies, axes, 0, 0), axis=0)]
    pallas_call x1, Pallas kernels: 4.83 us -> 3.61 us  [finish(): pl.pallas_call(functools.partial(finish_kernel, given), out_shape=[jax.Sh...]
  transfers between devices with their start and end apart: 26 -> 26, of which waited for: 10 -> 9; matrix products, arithmetic and copies ran while one was open for 1% -> 1% of each run, Pallas kernels for 13% -> 14%
where the time goes in v4:
time: 120 us
  starting transfers between devices  38.1 us (32%)
  blocking collectives  25.5 us (21%)
  Pallas kernels  23.8 us (20%)
  waiting for transfers between devices  20.8 us (17%)
  local copies, waits for them, and re-layouts  9.8 us (8%)
  between operations  1.73 us (1%)
    ppermute x23, starting transfers between devices, toward(): return lax.ppermute(value, axes, pairs)  34.7 us
    all_to_all x2, blocking collectives, sum_over(): return jnp.sum(lax.all_to_all(copies, axes, 0, 0), axis=0)  25.5 us
    ppermute x23, waiting for transfers between devices, toward(): return lax.ppermute(value, axes, pairs)  20.3 us
    pallas_call x3, Pallas kernels, project(): pl.pallas_call(kernel, out_shape=jax.ShapeDtypeStruct((8, 128), jnp.float...  14.3 us
    unnamed x42, local copies, waits for them, and re-layouts  9.76 us
    pallas_call x1, Pallas kernels, finish(): pl.pallas_call(functools.partial(finish_kernel, given), out_shape=[jax.Sh...  3.61 us
    ppermute x3, starting transfers between devices, swap_core(): return lax.ppermute(value, 'core', [(0, 1), (1, 0)])  3.42 us
    pallas_call x1, Pallas kernels, turn_basis(): pl.pallas_call(turn_basis_kernel, out_shape=[jax.ShapeDtypeStruct((K, 256...  3.18 us
  transfers between devices with their start and end apart: 26, of which 9 were waited for; matrix products, arithmetic and copies ran while one was open for 1% of the time, Pallas kernels for 14%

profile of v4, /device:TPU:1, one launch (start us, length us, event | category | flops | bytes accessed | tf_op | source)
XLA Modules:
  0.0 119.9 jit_solution(2657032371811212850)
XLA Ops:
  0.6 3.3 %collective-permute-start = (bf16[64,2048]{1,0:T(8,128)(2,1)}, bf16[64,2048]{1,0:T(8,128)(2,1)S(1)}, u32[]{:S(2)}, u32[]{:S(2)}) collective-permute-start(bf16[64,2048]{1,0:T(8,128)(2,1)} %param.9), channel_id=1, source_target_pairs={{0,4},{4,0},{1,5},{5,1},{2,6},{6,2},{3,7},{7,3},{8,12},{12,8},{9,1... | collective-permute-start | bytes 786440 | tf_op jit(solution)/shard_map/ppermute | solution.py:42
  5.4 1.1 collective-permute-start.3
  6.9 5.2 %collective-permute-start.1 = (bf16[128,512]{1,0:T(8,128)(2,1)S(1)}, bf16[128,512]{1,0:T(8,128)(2,1)S(1)}, u32[]{:S(2)}, u32[]{:S(2)}) collective-permute-start(bf16[128,512]{1,0:T(8,128)(2,1)S(1)} %pad_maximum_fusion), channel_id=1, source_target_pairs={{0,8},{4,60},{8,16},{12,4},{16,24},{20,12},{24,32},{28,20},{32,40}... | collective-permute-start | bytes 393224 | tf_op jit(solution)/shard_map/ppermute | solution.py:38
  12.8 1.2 %collective-permute-done.1 = bf16[128,512]{1,0:T(8,128)(2,1)S(1)} collective-permute-done((bf16[128,512]{1,0:T(8,128)(2,1)S(1)}, bf16[128,512]{1,0:T(8,128)(2,1)S(1)}, u32[]{:S(2)}, u32[]{:S(2)}) %collective-permute-start.1) | collective-permute-done | bytes 131104 | tf_op jit(solution)/shard_map/ppermute | solution.py:38
  14.1 3.1 %collective-permute-done.2 = bf16[128,512]{1,0:T(8,128)(2,1)S(1)} collective-permute-done((bf16[128,512]{1,0:T(8,128)(2,1)S(1)}, bf16[128,512]{1,0:T(8,128)(2,1)S(1)}, u32[]{:S(2)}, u32[]{:S(2)}) %collective-permute-start.2) | collective-permute-done | bytes 131104 | tf_op jit(solution)/shard_map/ppermute | solution.py:38
  17.1 2.1 %collective-permute-start.5 = (bf16[128,512]{1,0:T(8,128)(2,1)S(1)}, bf16[128,512]{1,0:T(8,128)(2,1)S(1)}, u32[]{:S(2)}, u32[]{:S(2)}) collective-permute-start(bf16[128,512]{1,0:T(8,128)(2,1)S(1)} %collective-permute-done.1), channel_id=1, source_target_pairs={{0,8},{4,60},{8,16},{12,4},{16,24},{20,12},{24,32},{28,20},{32,40}... | collective-permute-start | bytes 393224 | tf_op jit(solution)/shard_map/ppermute | solution.py:38
  19.3 2.7 %collective-permute-start.9 = (bf16[128,512]{1,0:T(8,128)(2,1)S(1)}, bf16[128,512]{1,0:T(8,128)(2,1)S(1)}, u32[]{:S(2)}, u32[]{:S(2)}) collective-permute-start(bf16[128,512]{1,0:T(8,128)(2,1)S(1)} %collective-permute-done.3), channel_id=1, source_target_pairs={{0,64},{4,196},{64,128},{68,4},{128,192},{132,68},{192,0},{196,132... | collective-permute-start | bytes 393224 | tf_op jit(solution)/shard_map/ppermute | solution.py:38
  21.9 2.7 %collective-permute-start.6 = (bf16[128,512]{1,0:T(8,128)(2,1)S(1)}, bf16[128,512]{1,0:T(8,128)(2,1)S(1)}, u32[]{:S(2)}, u32[]{:S(2)}) collective-permute-start(bf16[128,512]{1,0:T(8,128)(2,1)S(1)} %collective-permute-done.5), channel_id=1, source_target_pairs={{0,8},{4,60},{8,16},{12,4},{16,24},{20,12},{24,32},{28,20},{32,40}... | collective-permute-start | bytes 393224 | tf_op jit(solution)/shard_map/ppermute | solution.py:38
  24.8 2.2 %collective-permute-start.10 = (bf16[512,512]{1,0:T(8,128)(2,1)S(1)}, bf16[512,512]{1,0:T(8,128)(2,1)S(1)}, u32[]{:S(2)}, u32[]{:S(2)}) collective-permute-start(bf16[512,512]{1,0:T(8,128)(2,1)S(1)} %constant_dynamic-update-slice_fusion.refs_4_), channel_id=1, source_target_pairs={{0,8},{4,60},{8,16},{12,4},{16,24},{20,12},{24,32},{28,20},{32,40}... | collective-permute-start | bytes 1572872 | tf_op jit(solution)/shard_map/ppermute | solution.py:38
  27.0 2.7 %collective-permute-start.7 = (bf16[128,512]{1,0:T(8,128)(2,1)S(1)}, bf16[128,512]{1,0:T(8,128)(2,1)S(1)}, u32[]{:S(2)}, u32[]{:S(2)}) collective-permute-start(bf16[128,512]{1,0:T(8,128)(2,1)S(1)} %collective-permute-done.6), channel_id=1, source_target_pairs={{0,8},{4,60},{8,16},{12,4},{16,24},{20,12},{24,32},{28,20},{32,40}... | collective-permute-start | bytes 393224 | tf_op jit(solution)/shard_map/ppermute | solution.py:38
  31.2 2.7 %collective-permute-start.17 = (bf16[256,1024]{1,0:T(8,128)(2,1)S(1)}, bf16[256,1024]{1,0:T(8,128)(2,1)}, u32[]{:S(2)}, u32[]{:S(2)}) collective-permute-start(bf16[256,1024]{1,0:T(8,128)(2,1)S(1)} %turn_inputs.1.refs_0_), channel_id=1, source_target_pairs={{0,1},{4,7},{1,2},{5,4},{2,3},{6,5},{3,0},{7,6},{8,9},{12,15},{9,1... | collective-permute-start | bytes 1572872 | tf_op jit(solution)/shard_map/ppermute | solution.py:38
  33.9 3.2 %turn_basis.1 = (bf16[8,256,512]{2,1,0:T(8,128)(2,1)S(1)}, bf16[8,256,512]{2,1,0:T(8,128)(2,1)S(1)}) custom-call(s32[1]{0:T(128)} %bitcast.5.core_ref, bf16[8,2048,128]{2,1,0:T(8,128)(2,1)} %far_basis_ref.1, bf16[8,2048,128]{2,1,0:T(8,128)(2,1)S(1)} %collective-permute-done.8.other_ref), custom_call_target="tpu_custom_call" | custom-call | bytes 8388608 | tf_op jit(solution)/shard_map/turn_basis/pallas_call | solution.py:263
  37.1 1.4 %copy-done.1 = bf16[8,256,512]{2,1,0:T(8,128)(2,1)} copy-done((bf16[8,256,512]{2,1,0:T(8,128)(2,1)}, bf16[8,256,512]{2,1,0:T(8,128)(2,1)S(1)}, u32[]{:S(2)}) %copy-start.1) | copy-done | bytes 2097176
  38.5 1.3 %copy-done.3 = bf16[8,256,512]{2,1,0:T(8,128)(2,1)} copy-done((bf16[8,256,512]{2,1,0:T(8,128)(2,1)}, bf16[8,256,512]{2,1,0:T(8,128)(2,1)S(1)}, u32[]{:S(2)}) %copy-start.3) | copy-done | bytes 2097176
  39.9 2.3 %collective-permute-start.22 = (bf16[1024,512]{1,0:T(8,128)(2,1)S(1)}, bf16[1024,512]{1,0:T(8,128)(2,1)S(1)}, u32[]{:S(2)}, u32[]{:S(2)}) collective-permute-start(bf16[1024,512]{1,0:T(8,128)(2,1)S(1)} %constant_dynamic-update-slice_fusion.5.refs_4_), channel_id=1, source_target_pairs={{0,64},{4,196},{64,128},{68,4},{128,192},{132,68},{192,0},{196,132... | collective-permute-start | bytes 3145736 | tf_op jit(solution)/shard_map/ppermute | solution.py:38
  42.2 1.8 %collective-permute-done.11.refs_10_ = bf16[512,512]{1,0:T(8,128)(2,1)S(1)} collective-permute-done((bf16[512,512]{1,0:T(8,128)(2,1)S(1)}, bf16[512,512]{1,0:T(8,128)(2,1)S(1)}, u32[]{:S(2)}, u32[]{:S(2)}) %collective-permute-start.11) | collective-permute-done | bytes 524320 | tf_op jit(solution)/shard_map/ppermute | solution.py:38
  47.9 4.9 %collective-permute-done.12.refs_6_ = bf16[512,512]{1,0:T(8,128)(2,1)} collective-permute-done((bf16[512,512]{1,0:T(8,128)(2,1)S(1)}, bf16[512,512]{1,0:T(8,128)(2,1)}, u32[]{:S(2)}, u32[]{:S(2)}) %collective-permute-start.12) | collective-permute-done | bytes 524320 | tf_op jit(solution)/shard_map/ppermute | solution.py:38
  52.8 2.7 %collective-permute-start.18 = (bf16[256,1024]{1,0:T(8,128)(2,1)}, bf16[256,1024]{1,0:T(8,128)(2,1)}, u32[]{:S(2)}, u32[]{:S(2)}) collective-permute-start(bf16[256,1024]{1,0:T(8,128)(2,1)} %collective-permute-done.17.refs_1_), channel_id=1, source_target_pairs={{0,1},{4,7},{1,2},{5,4},{2,3},{6,5},{3,0},{7,6},{8,9},{12,15},{9,1... | collective-permute-start | bytes 1572872 | tf_op jit(solution)/shard_map/ppermute | solution.py:38
  55.5 2.9 %collective-permute-done.13.refs_9_ = bf16[512,512]{1,0:T(8,128)(2,1)} collective-permute-done((bf16[512,512]{1,0:T(8,128)(2,1)S(1)}, bf16[512,512]{1,0:T(8,128)(2,1)}, u32[]{:S(2)}, u32[]{:S(2)}) %collective-permute-start.13) | collective-permute-done | bytes 524320 | tf_op jit(solution)/shard_map/ppermute | solution.py:38
  58.4 1.5 %collective-permute-start.14 = (bf16[512,512]{1,0:T(8,128)(2,1)}, bf16[512,512]{1,0:T(8,128)(2,1)}, u32[]{:S(2)}, u32[]{:S(2)}) collective-permute-start(bf16[512,512]{1,0:T(8,128)(2,1)} %collective-permute-done.12.refs_6_), channel_id=1, source_target_pairs={{0,8},{4,60},{8,16},{12,4},{16,24},{20,12},{24,32},{28,20},{32,40}... | collective-permute-start | bytes 1572872 | tf_op jit(solution)/shard_map/ppermute | solution.py:38
  60.7 2.9 %collective-permute-start.25 = (bf16[1024,512]{1,0:T(8,128)(2,1)S(1)}, bf16[1024,512]{1,0:T(8,128)(2,1)}, u32[]{:S(2)}, u32[]{:S(2)}) collective-permute-start(bf16[1024,512]{1,0:T(8,128)(2,1)S(1)} %collective-permute-done.22.refs_5_), channel_id=1, source_target_pairs={{0,64},{4,196},{64,128},{68,4},{128,192},{132,68},{192,0},{196,132... | collective-permute-start | bytes 3145736 | tf_op jit(solution)/shard_map/ppermute | solution.py:38
  63.7 1.9 %collective-permute-done.18.refs_2_ = bf16[256,1024]{1,0:T(8,128)(2,1)} collective-permute-done((bf16[256,1024]{1,0:T(8,128)(2,1)}, bf16[256,1024]{1,0:T(8,128)(2,1)}, u32[]{:S(2)}, u32[]{:S(2)}) %collective-permute-start.18) | collective-permute-done | bytes 524320 | tf_op jit(solution)/shard_map/ppermute | solution.py:38
  65.5 3.8 %collective-permute-done.23.refs_6_ = bf16[1024,512]{1,0:T(8,128)(2,1)} collective-permute-done((bf16[1024,512]{1,0:T(8,128)(2,1)S(1)}, bf16[1024,512]{1,0:T(8,128)(2,1)}, u32[]{:S(2)}, u32[]{:S(2)}) %collective-permute-start.23) | collective-permute-done | bytes 1048608 | tf_op jit(solution)/shard_map/ppermute | solution.py:38
  69.4 1.6 %copy-done.4 = bf16[8,256,512]{2,1,0:T(8,128)(2,1)S(1)} copy-done((bf16[8,256,512]{2,1,0:T(8,128)(2,1)S(1)}, bf16[8,256,512]{2,1,0:T(8,128)(2,1)}, u32[]{:S(2)}) %copy-start.4) | copy-done | bytes 2097176
  71.0 1.0 copy-done.10
  72.0 4.8 %right_kernel.1.before_ref = f32[8,128]{1,0:T(8,128)S(1)} custom-call(s32[4]{0:T(128)S(1)} %pad_add_fusion.place_ref, bf16[8,256,512]{2,1,0:T(8,128)(2,1)S(1)} %copy-done.4, f32[8,128]{1,0:T(8,128)S(1)} %broadcast_in_dim.15.before_ref, bf16[256,1024]{1,0:T(8,128)(2,1)S(1)} %turn_inputs.1.refs_0_, bf16[256,1024]{1,0:T(8,128)(2,1)} %collective-permute-done.17.refs_1_, ...), custom_call_target="tpu_custom_call" | custom-call | flops 4026531840 | bytes 4194304 | tf_op jit(solution)/shard_map/right_kernel/pallas_call | solution.py:431
  77.9 5.6 %left_kernel.1.before_ref = f32[8,128]{1,0:T(8,128)S(1)} custom-call(s32[4]{0:T(128)S(1)} %pad_add_fusion.place_ref, bf16[8,256,512]{2,1,0:T(8,128)(2,1)S(1)} %copy-done.2, f32[8,128]{1,0:T(8,128)S(1)} %right_kernel.1.before_ref, bf16[256,1024]{1,0:T(8,128)(2,1)S(1)} %turn_inputs.1.refs_0_, bf16[256,1024]{1,0:T(8,128)(2,1)} %collective-permute-done.17.refs_1_, ...), custom_call_target="tpu_custom_call" | custom-call | flops 5234491392 | bytes 4194304 | tf_op jit(solution)/shard_map/left_kernel/pallas_call | solution.py:431
  83.5 2.5 %gram.1.before_ref = f32[8,128]{1,0:T(8,128)S(1)} custom-call(f32[8,128]{1,0:T(8,128)S(1)} %left_kernel.1.before_ref, bf16[8,2048,128]{2,1,0:T(8,128)(2,1)S(1)} %copy-done.12, f32[2048,128]{1,0:T(8,128)S(1)} %copy-done.13), custom_call_target="tpu_custom_call" | custom-call | flops 25165824 | bytes 18874368 | tf_op jit(solution)/shard_map/gram/pallas_call | solution.py:105
  86.1 3.8 %far_kernel.1 = f32[8,128]{1,0:T(8,128)S(1)} custom-call(s32[4]{0:T(128)S(1)} %pad_add_fusion.place_ref, bf16[8,256,512]{2,1,0:T(8,128)(2,1)S(1)} %copy-done.2, bf16[8,256,512]{2,1,0:T(8,128)(2,1)S(1)} %copy-done.4, f32[8,128]{1,0:T(8,128)S(1)} %gram.1.before_ref, bf16[256,1024]{1,0:T(8,128)(2,1)S(1)} %turn_inputs.1.refs_0_, ...), custom_call_target="tpu_custom_call" | custom-call | flops 2550136832 | bytes 4194304 | tf_op jit(solution)/shard_map/far_kernel/pallas_call | solution.py:431
  89.9 13.5 %all_to_all.20 = f32[16,8,128]{2,1,0:T(8,128)S(1)} all-to-all(f32[16,8,128]{2,1,0:T(8,128)S(1)} %broadcast_in_dim.16), channel_id=1, replica_groups=mesh['y'=4,'z'=8,'core'=2,'x'=4] {'z','core'}, dimensions={0} | all-to-all | bytes 131072 | tf_op jit(solution)/shard_map/all_to_all | solution.py:51
  103.5 12.0 %all_to_all.21 = f32[16,8,128]{2,1,0:T(8,128)S(1)} all-to-all(f32[16,8,128]{2,1,0:T(8,128)S(1)} %broadcast_in_dim.17), channel_id=1, replica_groups=mesh['y'=4,'z'=8,'core'=2,'x'=4] {'y','x'}, dimensions={0} | all-to-all | bytes 131072 | tf_op jit(solution)/shard_map/all_to_all | solution.py:51
  115.5 3.6 %finish.3 = (bf16[2048,128]{1,0:T(8,128)(2,1)}, f32[1,9]{1,0:T(1,128)}, f32[4,8]{1,0:T(4,128)}, s32[1]{0:T(128)}) custom-call(f32[1,1]{1,0:T(1,128)} %constant.11.clone.1.squares_ref, f32[8,128]{1,0:T(8,128)S(1)} %reduce_sum.41.sums_ref, f32[8,128]{1,0:T(8,128)S(1)} %pad.4.rotation_ref, bf16[8,2048,128]{2,1,0:T(8,128)(2,1)} %far_basis_ref.1, ...), custom_call_target="tpu_custom_call" | custom-call | flops 6291456 | bytes 6291456 | tf_op jit(solution)/shard_map/finish/pallas_call | solution.py:232
  (83 shorter events, 10.0 us)
Async XLA Ops:
  0.6 4.7 %collective-permute-start = (bf16[64,2048]{1,0:T(8,128)(2,1)}, bf16[64,2048]{1,0:T(8,128)(2,1)S(1)}, u32[]{:S(2)}, u32[]{:S(2)}) collective-permute-start(bf16[64,2048]{1,0:T(8,128)(2,1)} %param.9), channel_id=1, source_target_pairs={{0,4},{4,0},{1,5},{5,1},{2,6},{6,2},{3,7},{7,3},{8,12},{12,8},{9,1... | collective-permute-start | bytes 786440 | tf_op jit(solution)/shard_map/ppermute | solution.py:42
  5.4 6.8 %collective-permute-start.3 = (bf16[128,512]{1,0:T(8,128)(2,1)S(1)}, bf16[128,512]{1,0:T(8,128)(2,1)S(1)}, u32[]{:S(2)}, u32[]{:S(2)}) collective-permute-start(bf16[128,512]{1,0:T(8,128)(2,1)S(1)} %pad_maximum_fusion.1), channel_id=1, source_target_pairs={{0,64},{4,196},{64,128},{68,4},{128,192},{132,68},{192,0},{196,132... | collective-permute-start | bytes 393224 | tf_op jit(solution)/shard_map/ppermute | solution.py:38
  6.4 6.4 %collective-permute-start.4 = (bf16[128,512]{1,0:T(8,128)(2,1)S(1)}, bf16[128,512]{1,0:T(8,128)(2,1)S(1)}, u32[]{:S(2)}, u32[]{:S(2)}) collective-permute-start(bf16[128,512]{1,0:T(8,128)(2,1)S(1)} %pad_maximum_fusion.1), channel_id=1, source_target_pairs={{0,192},{4,68},{64,0},{68,132},{128,64},{132,196},{192,128},{196,4... | collective-permute-start | bytes 393224 | tf_op jit(solution)/shard_map/ppermute | solution.py:38
  6.9 7.1 %collective-permute-start.1 = (bf16[128,512]{1,0:T(8,128)(2,1)S(1)}, bf16[128,512]{1,0:T(8,128)(2,1)S(1)}, u32[]{:S(2)}, u32[]{:S(2)}) collective-permute-start(bf16[128,512]{1,0:T(8,128)(2,1)S(1)} %pad_maximum_fusion), channel_id=1, source_target_pairs={{0,8},{4,60},{8,16},{12,4},{16,24},{20,12},{24,32},{28,20},{32,40}... | collective-permute-start | bytes 393224 | tf_op jit(solution)/shard_map/ppermute | solution.py:38
  12.1 5.0 %collective-permute-start.2 = (bf16[128,512]{1,0:T(8,128)(2,1)S(1)}, bf16[128,512]{1,0:T(8,128)(2,1)S(1)}, u32[]{:S(2)}, u32[]{:S(2)}) collective-permute-start(bf16[128,512]{1,0:T(8,128)(2,1)S(1)} %pad_maximum_fusion), channel_id=1, source_target_pairs={{0,56},{4,12},{8,0},{12,20},{16,8},{20,28},{24,16},{28,36},{32,24}... | collective-permute-start | bytes 393224 | tf_op jit(solution)/shard_map/ppermute | solution.py:38
  17.1 14.0 %collective-permute-start.8 = (bf16[8,2048,128]{2,1,0:T(8,128)(2,1)}, bf16[8,2048,128]{2,1,0:T(8,128)(2,1)S(1)}, u32[]{:S(2)}, u32[]{:S(2)}) collective-permute-start(bf16[8,2048,128]{2,1,0:T(8,128)(2,1)} %far_basis_ref.1), channel_id=1, source_target_pairs={{0,4},{4,0},{1,5},{5,1},{2,6},{6,2},{3,7},{7,3},{8,12},{12,8},{9,1... | collective-permute-start | bytes 12582920 | tf_op jit(solution)/shard_map/ppermute | solution.py:42
  17.1 4.8 %collective-permute-start.5 = (bf16[128,512]{1,0:T(8,128)(2,1)S(1)}, bf16[128,512]{1,0:T(8,128)(2,1)S(1)}, u32[]{:S(2)}, u32[]{:S(2)}) collective-permute-start(bf16[128,512]{1,0:T(8,128)(2,1)S(1)} %collective-permute-done.1), channel_id=1, source_target_pairs={{0,8},{4,60},{8,16},{12,4},{16,24},{20,12},{24,32},{28,20},{32,40}... | collective-permute-start | bytes 393224 | tf_op jit(solution)/shard_map/ppermute | solution.py:38
  19.3 5.4 %collective-permute-start.9 = (bf16[128,512]{1,0:T(8,128)(2,1)S(1)}, bf16[128,512]{1,0:T(8,128)(2,1)S(1)}, u32[]{:S(2)}, u32[]{:S(2)}) collective-permute-start(bf16[128,512]{1,0:T(8,128)(2,1)S(1)} %collective-permute-done.3), channel_id=1, source_target_pairs={{0,64},{4,196},{64,128},{68,4},{128,192},{132,68},{192,0},{196,132... | collective-permute-start | bytes 393224 | tf_op jit(solution)/shard_map/ppermute | solution.py:38
  21.9 7.8 %collective-permute-start.20 = (bf16[128,512]{1,0:T(8,128)(2,1)S(1)}, bf16[128,512]{1,0:T(8,128)(2,1)S(1)}, u32[]{:S(2)}, u32[]{:S(2)}) collective-permute-start(bf16[128,512]{1,0:T(8,128)(2,1)S(1)} %collective-permute-done.2), channel_id=1, source_target_pairs={{0,56},{4,12},{8,0},{12,20},{16,8},{20,28},{24,16},{28,36},{32,24}... | collective-permute-start | bytes 393224 | tf_op jit(solution)/shard_map/ppermute | solution.py:38
  21.9 5.1 %collective-permute-start.6 = (bf16[128,512]{1,0:T(8,128)(2,1)S(1)}, bf16[128,512]{1,0:T(8,128)(2,1)S(1)}, u32[]{:S(2)}, u32[]{:S(2)}) collective-permute-start(bf16[128,512]{1,0:T(8,128)(2,1)S(1)} %collective-permute-done.5), channel_id=1, source_target_pairs={{0,8},{4,60},{8,16},{12,4},{16,24},{20,12},{24,32},{28,20},{32,40}... | collective-permute-start | bytes 393224 | tf_op jit(solution)/shard_map/ppermute | solution.py:38
  24.7 5.1 %collective-permute-start.16 = (bf16[1024,128]{1,0:T(8,128)(2,1)}, bf16[1024,128]{1,0:T(8,128)(2,1)S(1)}, u32[]{:S(2)}, u32[]{:S(2)}) collective-permute-start(bf16[1024,128]{1,0:T(8,128)(2,1)} %own_ref.1), channel_id=1, source_target_pairs={{0,4},{4,0},{1,5},{5,1},{2,6},{6,2},{3,7},{7,3},{8,12},{12,8},{9,1... | collective-permute-start | bytes 786440 | tf_op jit(solution)/shard_map/ppermute | solution.py:42
  24.8 17.3 %collective-permute-start.10 = (bf16[512,512]{1,0:T(8,128)(2,1)S(1)}, bf16[512,512]{1,0:T(8,128)(2,1)S(1)}, u32[]{:S(2)}, u32[]{:S(2)}) collective-permute-start(bf16[512,512]{1,0:T(8,128)(2,1)S(1)} %constant_dynamic-update-slice_fusion.refs_4_), channel_id=1, source_target_pairs={{0,8},{4,60},{8,16},{12,4},{16,24},{20,12},{24,32},{28,20},{32,40}... | collective-permute-start | bytes 1572872 | tf_op jit(solution)/shard_map/ppermute | solution.py:38
  27.0 12.8 %collective-permute-start.7 = (bf16[128,512]{1,0:T(8,128)(2,1)S(1)}, bf16[128,512]{1,0:T(8,128)(2,1)S(1)}, u32[]{:S(2)}, u32[]{:S(2)}) collective-permute-start(bf16[128,512]{1,0:T(8,128)(2,1)S(1)} %collective-permute-done.6), channel_id=1, source_target_pairs={{0,8},{4,60},{8,16},{12,4},{16,24},{20,12},{24,32},{28,20},{32,40}... | collective-permute-start | bytes 393224 | tf_op jit(solution)/shard_map/ppermute | solution.py:38
  29.7 10.1 %collective-permute-start.21 = (bf16[128,512]{1,0:T(8,128)(2,1)S(1)}, bf16[128,512]{1,0:T(8,128)(2,1)S(1)}, u32[]{:S(2)}, u32[]{:S(2)}) collective-permute-start(bf16[128,512]{1,0:T(8,128)(2,1)S(1)} %collective-permute-done.20), channel_id=1, source_target_pairs={{0,56},{4,12},{8,0},{12,20},{16,8},{20,28},{24,16},{28,36},{32,24}... | collective-permute-start | bytes 393224 | tf_op jit(solution)/shard_map/ppermute | solution.py:38
  29.9 14.1 %collective-permute-start.11 = (bf16[512,512]{1,0:T(8,128)(2,1)S(1)}, bf16[512,512]{1,0:T(8,128)(2,1)S(1)}, u32[]{:S(2)}, u32[]{:S(2)}) collective-permute-start(bf16[512,512]{1,0:T(8,128)(2,1)S(1)} %constant_dynamic-update-slice_fusion.refs_4_), channel_id=1, source_target_pairs={{0,56},{4,12},{8,0},{12,20},{16,8},{20,28},{24,16},{28,36},{32,24}... | collective-permute-start | bytes 1572872 | tf_op jit(solution)/shard_map/ppermute | solution.py:38
  31.2 15.9 %collective-permute-start.17 = (bf16[256,1024]{1,0:T(8,128)(2,1)S(1)}, bf16[256,1024]{1,0:T(8,128)(2,1)}, u32[]{:S(2)}, u32[]{:S(2)}) collective-permute-start(bf16[256,1024]{1,0:T(8,128)(2,1)S(1)} %turn_inputs.1.refs_0_), channel_id=1, source_target_pairs={{0,1},{4,7},{1,2},{5,4},{2,3},{6,5},{3,0},{7,6},{8,9},{12,15},{9,1... | collective-permute-start | bytes 1572872 | tf_op jit(solution)/shard_map/ppermute | solution.py:38
  39.9 20.8 %collective-permute-start.22 = (bf16[1024,512]{1,0:T(8,128)(2,1)S(1)}, bf16[1024,512]{1,0:T(8,128)(2,1)S(1)}, u32[]{:S(2)}, u32[]{:S(2)}) collective-permute-start(bf16[1024,512]{1,0:T(8,128)(2,1)S(1)} %constant_dynamic-update-slice_fusion.5.refs_4_), channel_id=1, source_target_pairs={{0,64},{4,196},{64,128},{68,4},{128,192},{132,68},{192,0},{196,132... | collective-permute-start | bytes 3145736 | tf_op jit(solution)/shard_map/ppermute | solution.py:38
  43.9 8.9 %collective-permute-start.12 = (bf16[512,512]{1,0:T(8,128)(2,1)S(1)}, bf16[512,512]{1,0:T(8,128)(2,1)}, u32[]{:S(2)}, u32[]{:S(2)}) collective-permute-start(bf16[512,512]{1,0:T(8,128)(2,1)S(1)} %collective-permute-done.10.refs_5_), channel_id=1, source_target_pairs={{0,8},{4,60},{8,16},{12,4},{16,24},{20,12},{24,32},{28,20},{32,40}... | collective-permute-start | bytes 1572872 | tf_op jit(solution)/shard_map/ppermute | solution.py:38
  45.7 23.7 %collective-permute-start.23 = (bf16[1024,512]{1,0:T(8,128)(2,1)S(1)}, bf16[1024,512]{1,0:T(8,128)(2,1)}, u32[]{:S(2)}, u32[]{:S(2)}) collective-permute-start(bf16[1024,512]{1,0:T(8,128)(2,1)S(1)} %constant_dynamic-update-slice_fusion.5.refs_4_), channel_id=1, source_target_pairs={{0,192},{4,68},{64,0},{68,132},{128,64},{132,196},{192,128},{196,4... | collective-permute-start | bytes 3145736 | tf_op jit(solution)/shard_map/ppermute | solution.py:38
  45.7 12.7 %collective-permute-start.13 = (bf16[512,512]{1,0:T(8,128)(2,1)S(1)}, bf16[512,512]{1,0:T(8,128)(2,1)}, u32[]{:S(2)}, u32[]{:S(2)}) collective-permute-start(bf16[512,512]{1,0:T(8,128)(2,1)S(1)} %collective-permute-done.11.refs_10_), channel_id=1, source_target_pairs={{0,56},{4,12},{8,0},{12,20},{16,8},{20,28},{24,16},{28,36},{32,24}... | collective-permute-start | bytes 1572872 | tf_op jit(solution)/shard_map/ppermute | solution.py:38
  47.1 12.8 %collective-permute-start.19 = (bf16[256,1024]{1,0:T(8,128)(2,1)S(1)}, bf16[256,1024]{1,0:T(8,128)(2,1)S(1)}, u32[]{:S(2)}, u32[]{:S(2)}) collective-permute-start(bf16[256,1024]{1,0:T(8,128)(2,1)S(1)} %turn_inputs.1.refs_0_), channel_id=1, source_target_pairs={{0,3},{4,5},{1,0},{5,6},{2,1},{6,7},{3,2},{7,4},{8,11},{12,13},{9,... | collective-permute-start | bytes 1572872 | tf_op jit(solution)/shard_map/ppermute | solution.py:38
  52.8 12.7 %collective-permute-start.18 = (bf16[256,1024]{1,0:T(8,128)(2,1)}, bf16[256,1024]{1,0:T(8,128)(2,1)}, u32[]{:S(2)}, u32[]{:S(2)}) collective-permute-start(bf16[256,1024]{1,0:T(8,128)(2,1)} %collective-permute-done.17.refs_1_), channel_id=1, source_target_pairs={{0,1},{4,7},{1,2},{5,4},{2,3},{6,5},{3,0},{7,6},{8,9},{12,15},{9,1... | collective-permute-start | bytes 1572872 | tf_op jit(solution)/shard_map/ppermute | solution.py:38
  58.4 18.5 %collective-permute-start.14 = (bf16[512,512]{1,0:T(8,128)(2,1)}, bf16[512,512]{1,0:T(8,128)(2,1)}, u32[]{:S(2)}, u32[]{:S(2)}) collective-permute-start(bf16[512,512]{1,0:T(8,128)(2,1)} %collective-permute-done.12.refs_6_), channel_id=1, source_target_pairs={{0,8},{4,60},{8,16},{12,4},{16,24},{20,12},{24,32},{28,20},{32,40}... | collective-permute-start | bytes 1572872 | tf_op jit(solution)/shard_map/ppermute | solution.py:38
  60.7 16.2 %collective-permute-start.15 = (bf16[512,512]{1,0:T(8,128)(2,1)}, bf16[512,512]{1,0:T(8,128)(2,1)}, u32[]{:S(2)}, u32[]{:S(2)}) collective-permute-start(bf16[512,512]{1,0:T(8,128)(2,1)} %collective-permute-done.13.refs_9_), channel_id=1, source_target_pairs={{0,56},{4,12},{8,0},{12,20},{16,8},{20,28},{24,16},{28,36},{32,24}... | collective-permute-start | bytes 1572872 | tf_op jit(solution)/shard_map/ppermute | solution.py:38
  60.7 25.4 %collective-permute-start.25 = (bf16[1024,512]{1,0:T(8,128)(2,1)S(1)}, bf16[1024,512]{1,0:T(8,128)(2,1)}, u32[]{:S(2)}, u32[]{:S(2)}) collective-permute-start(bf16[1024,512]{1,0:T(8,128)(2,1)S(1)} %collective-permute-done.22.refs_5_), channel_id=1, source_target_pairs={{0,64},{4,196},{64,128},{68,4},{128,192},{132,68},{192,0},{196,132... | collective-permute-start | bytes 3145736 | tf_op jit(solution)/shard_map/ppermute | solution.py:38
  72.0 5.8 %copy-start.15 = (f32[8,4]{0,1:T(4,128)S(1)}, f32[8,4]{0,1:T(4,128)}, u32[]{:S(2)}) copy-start(f32[8,4]{0,1:T(4,128)} %param.11) | copy-start | bytes 388
  72.0 5.8 %copy-start.2 = (bf16[8,256,512]{2,1,0:T(8,128)(2,1)S(1)}, bf16[8,256,512]{2,1,0:T(8,128)(2,1)}, u32[]{:S(2)}) copy-start(bf16[8,256,512]{2,1,0:T(8,128)(2,1)} %copy-done.1) | copy-start | bytes 6291460
  72.0 5.8 %copy-start.6 = (bf16[512,512]{1,0:T(8,128)(2,1)S(1)}, bf16[512,512]{1,0:T(8,128)(2,1)}, u32[]{:S(2)}) copy-start(bf16[512,512]{1,0:T(8,128)(2,1)} %copy-done.5) | copy-start | bytes 1572868
  72.0 5.8 %copy-start.8 = (bf16[512,512]{1,0:T(8,128)(2,1)S(1)}, bf16[512,512]{1,0:T(8,128)(2,1)}, u32[]{:S(2)}) copy-start(bf16[512,512]{1,0:T(8,128)(2,1)} %copy-done.7) | copy-start | bytes 1572868
  72.0 5.8 %copy-start.11 = (bf16[256,1024]{1,0:T(8,128)(2,1)S(1)}, bf16[256,1024]{1,0:T(8,128)(2,1)}, u32[]{:S(2)}) copy-start(bf16[256,1024]{1,0:T(8,128)(2,1)} %copy-done.9) | copy-start | bytes 1572868
  76.9 9.2 %collective-permute-start.24 = (bf16[512,512]{1,0:T(8,128)(2,1)}, bf16[512,512]{1,0:T(8,128)(2,1)S(1)}, u32[]{:S(2)}, u32[]{:S(2)}) collective-permute-start(bf16[512,512]{1,0:T(8,128)(2,1)} %collective-permute-done.14.refs_7_), channel_id=1, source_target_pairs={{0,8},{4,60},{8,16},{12,4},{16,24},{20,12},{24,32},{28,20},{32,40}... | collective-permute-start | bytes 1572872 | tf_op jit(solution)/shard_map/ppermute | solution.py:38
  89.9 29.8 %copy-start.14 = (f32[2048,128]{1,0:T(8,128)S(1)}, f32[2048,128]{1,0:T(8,128)}, u32[]{:S(2)}) copy-start(f32[2048,128]{1,0:T(8,128)} %far_field_ref.1) | copy-start | bytes 3145732
  (10 other events, 20.1 us)

commit v5 on v4

--- a/solution.py
+++ b/solution.py
@@ -481,7 +481,7 @@
     b4, left_basis, right_basis = together(b4, left_basis, right_basis)
     r0 = jnp.concatenate([b, b1, b2, b3, b4, b5, b6, b7])
     r1, r3 = toward(r0, "y", 1), toward(r0, "y", -1)
-    l1, l7 = together(l1, l7)
+    l1, l7, x3 = together(l1, l7, x3)
     l2, l6 = toward(l1, "z", 1), toward(l7, "z", -1)
     x2 = toward(x1, "x", 1)
     l2, l6 = together(l2, l6)

time: 120 us -> 122 us (1.017)
  starting transfers between devices: 38.1 us -> 41 us
  waiting for transfers between devices: 20.8 us -> 18.4 us
  blocking collectives: 25.5 us -> 27.1 us
    ppermute x23, starting transfers between devices: 34.7 us -> 37.5 us  [toward(): return lax.ppermute(value, axes, pairs)]
    ppermute x23, waiting for transfers between devices: 20.3 us -> 17.9 us  [toward(): return lax.ppermute(value, axes, pairs)]
    all_to_all x2, blocking collectives: 25.5 us -> 27.1 us  [sum_over(): return jnp.sum(lax.all_to_all(copies, axes, 0, 0), axis=0)]
  transfers between devices with their start and end apart: 26 -> 26, of which waited for: 9 -> 9; matrix products, arithmetic and copies ran while one was open for 1% -> 1% of each run, Pallas kernels for 14% -> 13%
where the time goes in v5:
time: 122 us
  starting transfers between devices  41 us (34%)
  blocking collectives  27.1 us (22%)
  Pallas kernels  23.8 us (20%)
  waiting for transfers between devices  18.4 us (15%)
  local copies, waits for them, and re-layouts  9.76 us (8%)
  between operations  1.73 us (1%)
    ppermute x23, starting transfers between devices, toward(): return lax.ppermute(value, axes, pairs)  37.5 us
    all_to_all x2, blocking collectives, sum_over(): return jnp.sum(lax.all_to_all(copies, axes, 0, 0), axis=0)  27.1 us
    ppermute x23, waiting for transfers between devices, toward(): return lax.ppermute(value, axes, pairs)  17.9 us
    pallas_call x3, Pallas kernels, project(): pl.pallas_call(kernel, out_shape=jax.ShapeDtypeStruct((8, 128), jnp.float...  14.3 us
    unnamed x42, local copies, waits for them, and re-layouts  9.72 us
    pallas_call x1, Pallas kernels, finish(): pl.pallas_call(functools.partial(finish_kernel, given), out_shape=[jax.Sh...  3.61 us
    ppermute x3, starting transfers between devices, swap_core(): return lax.ppermute(value, 'core', [(0, 1), (1, 0)])  3.42 us
    pallas_call x1, Pallas kernels, turn_basis(): pl.pallas_call(turn_basis_kernel, out_shape=[jax.ShapeDtypeStruct((K, 256...  3.18 us
  transfers between devices with their start and end apart: 26, of which 9 were waited for; matrix products, arithmetic and copies ran while one was open for 1% of the time, Pallas kernels for 13%

profile of v5, /device:TPU:1, one launch (start us, length us, event | category | flops | bytes accessed | tf_op | source)
XLA Modules:
  0.0 121.9 jit_solution(9300922823868912902)
XLA Ops:
  0.6 3.3 %collective-permute-start = (bf16[64,2048]{1,0:T(8,128)(2,1)}, bf16[64,2048]{1,0:T(8,128)(2,1)S(1)}, u32[]{:S(2)}, u32[]{:S(2)}) collective-permute-start(bf16[64,2048]{1,0:T(8,128)(2,1)} %param.9), channel_id=1, source_target_pairs={{0,4},{4,0},{1,5},{5,1},{2,6},{6,2},{3,7},{7,3},{8,12},{12,8},{9,1... | collective-permute-start | bytes 786440 | tf_op jit(solution)/shard_map/ppermute | solution.py:42
  5.4 1.1 collective-permute-start.3
  6.9 5.2 %collective-permute-start.1 = (bf16[128,512]{1,0:T(8,128)(2,1)S(1)}, bf16[128,512]{1,0:T(8,128)(2,1)S(1)}, u32[]{:S(2)}, u32[]{:S(2)}) collective-permute-start(bf16[128,512]{1,0:T(8,128)(2,1)S(1)} %pad_maximum_fusion), channel_id=1, source_target_pairs={{0,8},{4,60},{8,16},{12,4},{16,24},{20,12},{24,32},{28,20},{32,40}... | collective-permute-start | bytes 393224 | tf_op jit(solution)/shard_map/ppermute | solution.py:38
  12.8 1.2 %collective-permute-done.1 = bf16[128,512]{1,0:T(8,128)(2,1)S(1)} collective-permute-done((bf16[128,512]{1,0:T(8,128)(2,1)S(1)}, bf16[128,512]{1,0:T(8,128)(2,1)S(1)}, u32[]{:S(2)}, u32[]{:S(2)}) %collective-permute-start.1) | collective-permute-done | bytes 131104 | tf_op jit(solution)/shard_map/ppermute | solution.py:38
  14.1 3.1 %collective-permute-done.2 = bf16[128,512]{1,0:T(8,128)(2,1)S(1)} collective-permute-done((bf16[128,512]{1,0:T(8,128)(2,1)S(1)}, bf16[128,512]{1,0:T(8,128)(2,1)S(1)}, u32[]{:S(2)}, u32[]{:S(2)}) %collective-permute-start.2) | collective-permute-done | bytes 131104 | tf_op jit(solution)/shard_map/ppermute | solution.py:38
  17.1 2.1 %collective-permute-start.5 = (bf16[128,512]{1,0:T(8,128)(2,1)S(1)}, bf16[128,512]{1,0:T(8,128)(2,1)S(1)}, u32[]{:S(2)}, u32[]{:S(2)}) collective-permute-start(bf16[128,512]{1,0:T(8,128)(2,1)S(1)} %collective-permute-done.1), channel_id=1, source_target_pairs={{0,8},{4,60},{8,16},{12,4},{16,24},{20,12},{24,32},{28,20},{32,40}... | collective-permute-start | bytes 393224 | tf_op jit(solution)/shard_map/ppermute | solution.py:38
  19.3 2.7 %collective-permute-start.9 = (bf16[128,512]{1,0:T(8,128)(2,1)S(1)}, bf16[128,512]{1,0:T(8,128)(2,1)S(1)}, u32[]{:S(2)}, u32[]{:S(2)}) collective-permute-start(bf16[128,512]{1,0:T(8,128)(2,1)S(1)} %collective-permute-done.3), channel_id=1, source_target_pairs={{0,64},{4,196},{64,128},{68,4},{128,192},{132,68},{192,0},{196,132... | collective-permute-start | bytes 393224 | tf_op jit(solution)/shard_map/ppermute | solution.py:38
  21.9 2.7 %collective-permute-start.6 = (bf16[128,512]{1,0:T(8,128)(2,1)S(1)}, bf16[128,512]{1,0:T(8,128)(2,1)S(1)}, u32[]{:S(2)}, u32[]{:S(2)}) collective-permute-start(bf16[128,512]{1,0:T(8,128)(2,1)S(1)} %collective-permute-done.5), channel_id=1, source_target_pairs={{0,8},{4,60},{8,16},{12,4},{16,24},{20,12},{24,32},{28,20},{32,40}... | collective-permute-start | bytes 393224 | tf_op jit(solution)/shard_map/ppermute | solution.py:38
  24.8 2.2 %collective-permute-start.10 = (bf16[512,512]{1,0:T(8,128)(2,1)S(1)}, bf16[512,512]{1,0:T(8,128)(2,1)S(1)}, u32[]{:S(2)}, u32[]{:S(2)}) collective-permute-start(bf16[512,512]{1,0:T(8,128)(2,1)S(1)} %constant_dynamic-update-slice_fusion.refs_4_), channel_id=1, source_target_pairs={{0,8},{4,60},{8,16},{12,4},{16,24},{20,12},{24,32},{28,20},{32,40}... | collective-permute-start | bytes 1572872 | tf_op jit(solution)/shard_map/ppermute | solution.py:38
  27.0 2.7 %collective-permute-start.7 = (bf16[128,512]{1,0:T(8,128)(2,1)S(1)}, bf16[128,512]{1,0:T(8,128)(2,1)S(1)}, u32[]{:S(2)}, u32[]{:S(2)}) collective-permute-start(bf16[128,512]{1,0:T(8,128)(2,1)S(1)} %collective-permute-done.6), channel_id=1, source_target_pairs={{0,8},{4,60},{8,16},{12,4},{16,24},{20,12},{24,32},{28,20},{32,40}... | collective-permute-start | bytes 393224 | tf_op jit(solution)/shard_map/ppermute | solution.py:38
  31.2 1.5 %collective-permute-start.13 = (bf16[256,1024]{1,0:T(8,128)(2,1)S(1)}, bf16[256,1024]{1,0:T(8,128)(2,1)S(1)}, u32[]{:S(2)}, u32[]{:S(2)}) collective-permute-start(bf16[256,1024]{1,0:T(8,128)(2,1)S(1)} %turn_inputs.1.refs_0_), channel_id=1, source_target_pairs={{0,3},{4,5},{1,0},{5,6},{2,1},{6,7},{3,2},{7,4},{8,11},{12,13},{9,... | collective-permute-start | bytes 1572872 | tf_op jit(solution)/shard_map/ppermute | solution.py:38
  32.6 3.2 %turn_basis.1 = (bf16[8,256,512]{2,1,0:T(8,128)(2,1)S(1)}, bf16[8,256,512]{2,1,0:T(8,128)(2,1)S(1)}) custom-call(s32[1]{0:T(128)} %bitcast.5.core_ref, bf16[8,2048,128]{2,1,0:T(8,128)(2,1)} %far_basis_ref.1, bf16[8,2048,128]{2,1,0:T(8,128)(2,1)S(1)} %collective-permute-done.8.other_ref), custom_call_target="tpu_custom_call" | custom-call | bytes 8388608 | tf_op jit(solution)/shard_map/turn_basis/pallas_call | solution.py:263
  35.8 1.4 %copy-done.1 = bf16[8,256,512]{2,1,0:T(8,128)(2,1)} copy-done((bf16[8,256,512]{2,1,0:T(8,128)(2,1)}, bf16[8,256,512]{2,1,0:T(8,128)(2,1)S(1)}, u32[]{:S(2)}) %copy-start.1) | copy-done | bytes 2097176
  37.2 1.3 %copy-done.3 = bf16[8,256,512]{2,1,0:T(8,128)(2,1)} copy-done((bf16[8,256,512]{2,1,0:T(8,128)(2,1)}, bf16[8,256,512]{2,1,0:T(8,128)(2,1)S(1)}, u32[]{:S(2)}) %copy-start.3) | copy-done | bytes 2097176
  38.6 2.3 %collective-permute-start.22 = (bf16[1024,512]{1,0:T(8,128)(2,1)S(1)}, bf16[1024,512]{1,0:T(8,128)(2,1)S(1)}, u32[]{:S(2)}, u32[]{:S(2)}) collective-permute-start(bf16[1024,512]{1,0:T(8,128)(2,1)S(1)} %constant_dynamic-update-slice_fusion.5.refs_4_), channel_id=1, source_target_pairs={{0,64},{4,196},{64,128},{68,4},{128,192},{132,68},{192,0},{196,132... | collective-permute-start | bytes 3145736 | tf_op jit(solution)/shard_map/ppermute | solution.py:38
  40.9 1.5 %collective-permute-start.18 = (bf16[256,1024]{1,0:T(8,128)(2,1)S(1)}, bf16[256,1024]{1,0:T(8,128)(2,1)}, u32[]{:S(2)}, u32[]{:S(2)}) collective-permute-start(bf16[256,1024]{1,0:T(8,128)(2,1)S(1)} %turn_inputs.1.refs_0_), channel_id=1, source_target_pairs={{0,1},{4,7},{1,2},{5,4},{2,3},{6,5},{3,0},{7,6},{8,9},{12,15},{9,1... | collective-permute-start | bytes 1572872 | tf_op jit(solution)/shard_map/ppermute | solution.py:38
  42.4 1.2 collective-permute-done.11.refs_10_
  44.3 1.5 %collective-permute-start.14 = (bf16[512,512]{1,0:T(8,128)(2,1)S(1)}, bf16[512,512]{1,0:T(8,128)(2,1)}, u32[]{:S(2)}, u32[]{:S(2)}) collective-permute-start(bf16[512,512]{1,0:T(8,128)(2,1)S(1)} %collective-permute-done.10.refs_5_), channel_id=1, source_target_pairs={{0,8},{4,60},{8,16},{12,4},{16,24},{20,12},{24,32},{28,20},{32,40}... | collective-permute-start | bytes 1572872 | tf_op jit(solution)/shard_map/ppermute | solution.py:38
  47.5 2.1 %collective-permute-done.18.refs_1_ = bf16[256,1024]{1,0:T(8,128)(2,1)} collective-permute-done((bf16[256,1024]{1,0:T(8,128)(2,1)S(1)}, bf16[256,1024]{1,0:T(8,128)(2,1)}, u32[]{:S(2)}, u32[]{:S(2)}) %collective-permute-start.18) | collective-permute-done | bytes 524320 | tf_op jit(solution)/shard_map/ppermute | solution.py:38
  49.6 3.4 %collective-permute-start.19 = (bf16[256,1024]{1,0:T(8,128)(2,1)}, bf16[256,1024]{1,0:T(8,128)(2,1)}, u32[]{:S(2)}, u32[]{:S(2)}) collective-permute-start(bf16[256,1024]{1,0:T(8,128)(2,1)} %collective-permute-done.18.refs_1_), channel_id=1, source_target_pairs={{0,1},{4,7},{1,2},{5,4},{2,3},{6,5},{3,0},{7,6},{8,9},{12,15},{9,1... | collective-permute-start | bytes 1572872 | tf_op jit(solution)/shard_map/ppermute | solution.py:38
  53.0 7.1 %collective-permute-done.15.refs_9_ = bf16[512,512]{1,0:T(8,128)(2,1)} collective-permute-done((bf16[512,512]{1,0:T(8,128)(2,1)S(1)}, bf16[512,512]{1,0:T(8,128)(2,1)}, u32[]{:S(2)}, u32[]{:S(2)}) %collective-permute-start.15) | collective-permute-done | bytes 524320 | tf_op jit(solution)/shard_map/ppermute | solution.py:38
  61.5 3.2 %collective-permute-start.25 = (bf16[1024,512]{1,0:T(8,128)(2,1)S(1)}, bf16[1024,512]{1,0:T(8,128)(2,1)}, u32[]{:S(2)}, u32[]{:S(2)}) collective-permute-start(bf16[1024,512]{1,0:T(8,128)(2,1)S(1)} %collective-permute-done.22.refs_5_), channel_id=1, source_target_pairs={{0,64},{4,196},{64,128},{68,4},{128,192},{132,68},{192,0},{196,132... | collective-permute-start | bytes 3145736 | tf_op jit(solution)/shard_map/ppermute | solution.py:38
  64.8 2.1 %collective-permute-done.23.refs_6_ = bf16[1024,512]{1,0:T(8,128)(2,1)} collective-permute-done((bf16[1024,512]{1,0:T(8,128)(2,1)S(1)}, bf16[1024,512]{1,0:T(8,128)(2,1)}, u32[]{:S(2)}, u32[]{:S(2)}) %collective-permute-start.23) | collective-permute-done | bytes 1048608 | tf_op jit(solution)/shard_map/ppermute | solution.py:38
  66.9 1.6 %copy-done.4 = bf16[8,256,512]{2,1,0:T(8,128)(2,1)S(1)} copy-done((bf16[8,256,512]{2,1,0:T(8,128)(2,1)S(1)}, bf16[8,256,512]{2,1,0:T(8,128)(2,1)}, u32[]{:S(2)}) %copy-start.4) | copy-done | bytes 2097176
  69.5 4.8 %right_kernel.1.before_ref = f32[8,128]{1,0:T(8,128)S(1)} custom-call(s32[4]{0:T(128)S(1)} %pad_add_fusion.place_ref, bf16[8,256,512]{2,1,0:T(8,128)(2,1)S(1)} %copy-done.4, f32[8,128]{1,0:T(8,128)S(1)} %broadcast_in_dim.15.before_ref, bf16[256,1024]{1,0:T(8,128)(2,1)S(1)} %turn_inputs.1.refs_0_, bf16[256,1024]{1,0:T(8,128)(2,1)} %collective-permute-done.18.refs_1_, ...), custom_call_target="tpu_custom_call" | custom-call | flops 4026531840 | bytes 4194304 | tf_op jit(solution)/shard_map/right_kernel/pallas_call | solution.py:431
  74.8 3.4 %collective-permute-start.24 = (bf16[512,512]{1,0:T(8,128)(2,1)}, bf16[512,512]{1,0:T(8,128)(2,1)S(1)}, u32[]{:S(2)}, u32[]{:S(2)}) collective-permute-start(bf16[512,512]{1,0:T(8,128)(2,1)} %collective-permute-done.16.refs_7_), channel_id=1, source_target_pairs={{0,8},{4,60},{8,16},{12,4},{16,24},{20,12},{24,32},{28,20},{32,40}... | collective-permute-start | bytes 1572872 | tf_op jit(solution)/shard_map/ppermute | solution.py:38
  78.3 5.6 %left_kernel.1.before_ref = f32[8,128]{1,0:T(8,128)S(1)} custom-call(s32[4]{0:T(128)S(1)} %pad_add_fusion.place_ref, bf16[8,256,512]{2,1,0:T(8,128)(2,1)S(1)} %copy-done.2, f32[8,128]{1,0:T(8,128)S(1)} %right_kernel.1.before_ref, bf16[256,1024]{1,0:T(8,128)(2,1)S(1)} %turn_inputs.1.refs_0_, bf16[256,1024]{1,0:T(8,128)(2,1)} %collective-permute-done.18.refs_1_, ...), custom_call_target="tpu_custom_call" | custom-call | flops 5234491392 | bytes 4194304 | tf_op jit(solution)/shard_map/left_kernel/pallas_call | solution.py:431
  83.9 2.5 %gram.1.before_ref = f32[8,128]{1,0:T(8,128)S(1)} custom-call(f32[8,128]{1,0:T(8,128)S(1)} %left_kernel.1.before_ref, bf16[8,2048,128]{2,1,0:T(8,128)(2,1)S(1)} %copy-done.12, f32[2048,128]{1,0:T(8,128)S(1)} %copy-done.13), custom_call_target="tpu_custom_call" | custom-call | flops 25165824 | bytes 18874368 | tf_op jit(solution)/shard_map/gram/pallas_call | solution.py:105
  86.5 3.8 %far_kernel.1 = f32[8,128]{1,0:T(8,128)S(1)} custom-call(s32[4]{0:T(128)S(1)} %pad_add_fusion.place_ref, bf16[8,256,512]{2,1,0:T(8,128)(2,1)S(1)} %copy-done.2, bf16[8,256,512]{2,1,0:T(8,128)(2,1)S(1)} %copy-done.4, f32[8,128]{1,0:T(8,128)S(1)} %gram.1.before_ref, bf16[256,1024]{1,0:T(8,128)(2,1)S(1)} %turn_inputs.1.refs_0_, ...), custom_call_target="tpu_custom_call" | custom-call | flops 2550136832 | bytes 4194304 | tf_op jit(solution)/shard_map/far_kernel/pallas_call | solution.py:431
  90.3 14.6 %all_to_all.20 = f32[16,8,128]{2,1,0:T(8,128)S(1)} all-to-all(f32[16,8,128]{2,1,0:T(8,128)S(1)} %broadcast_in_dim.16), channel_id=1, replica_groups=mesh['y'=4,'z'=8,'core'=2,'x'=4] {'z','core'}, dimensions={0} | all-to-all | bytes 131072 | tf_op jit(solution)/shard_map/all_to_all | solution.py:51
  104.9 12.6 %all_to_all.21 = f32[16,8,128]{2,1,0:T(8,128)S(1)} all-to-all(f32[16,8,128]{2,1,0:T(8,128)S(1)} %broadcast_in_dim.17), channel_id=1, replica_groups=mesh['y'=4,'z'=8,'core'=2,'x'=4] {'y','x'}, dimensions={0} | all-to-all | bytes 131072 | tf_op jit(solution)/shard_map/all_to_all | solution.py:51
  117.5 3.6 %finish.3 = (bf16[2048,128]{1,0:T(8,128)(2,1)}, f32[1,9]{1,0:T(1,128)}, f32[4,8]{1,0:T(4,128)}, s32[1]{0:T(128)}) custom-call(f32[1,1]{1,0:T(1,128)} %constant.11.clone.1.squares_ref, f32[8,128]{1,0:T(8,128)S(1)} %reduce_sum.41.sums_ref, f32[8,128]{1,0:T(8,128)S(1)} %pad.4.rotation_ref, bf16[8,2048,128]{2,1,0:T(8,128)(2,1)} %far_basis_ref.1, ...), custom_call_target="tpu_custom_call" | custom-call | flops 6291456 | bytes 6291456 | tf_op jit(solution)/shard_map/finish/pallas_call | solution.py:232
  (83 shorter events, 9.7 us)
Async XLA Ops:
  0.6 4.7 %collective-permute-start = (bf16[64,2048]{1,0:T(8,128)(2,1)}, bf16[64,2048]{1,0:T(8,128)(2,1)S(1)}, u32[]{:S(2)}, u32[]{:S(2)}) collective-permute-start(bf16[64,2048]{1,0:T(8,128)(2,1)} %param.9), channel_id=1, source_target_pairs={{0,4},{4,0},{1,5},{5,1},{2,6},{6,2},{3,7},{7,3},{8,12},{12,8},{9,1... | collective-permute-start | bytes 786440 | tf_op jit(solution)/shard_map/ppermute | solution.py:42
  5.4 6.8 %collective-permute-start.3 = (bf16[128,512]{1,0:T(8,128)(2,1)S(1)}, bf16[128,512]{1,0:T(8,128)(2,1)S(1)}, u32[]{:S(2)}, u32[]{:S(2)}) collective-permute-start(bf16[128,512]{1,0:T(8,128)(2,1)S(1)} %pad_maximum_fusion.1), channel_id=1, source_target_pairs={{0,64},{4,196},{64,128},{68,4},{128,192},{132,68},{192,0},{196,132... | collective-permute-start | bytes 393224 | tf_op jit(solution)/shard_map/ppermute | solution.py:38
  6.4 6.4 %collective-permute-start.4 = (bf16[128,512]{1,0:T(8,128)(2,1)S(1)}, bf16[128,512]{1,0:T(8,128)(2,1)S(1)}, u32[]{:S(2)}, u32[]{:S(2)}) collective-permute-start(bf16[128,512]{1,0:T(8,128)(2,1)S(1)} %pad_maximum_fusion.1), channel_id=1, source_target_pairs={{0,192},{4,68},{64,0},{68,132},{128,64},{132,196},{192,128},{196,4... | collective-permute-start | bytes 393224 | tf_op jit(solution)/shard_map/ppermute | solution.py:38
  6.9 7.1 %collective-permute-start.1 = (bf16[128,512]{1,0:T(8,128)(2,1)S(1)}, bf16[128,512]{1,0:T(8,128)(2,1)S(1)}, u32[]{:S(2)}, u32[]{:S(2)}) collective-permute-start(bf16[128,512]{1,0:T(8,128)(2,1)S(1)} %pad_maximum_fusion), channel_id=1, source_target_pairs={{0,8},{4,60},{8,16},{12,4},{16,24},{20,12},{24,32},{28,20},{32,40}... | collective-permute-start | bytes 393224 | tf_op jit(solution)/shard_map/ppermute | solution.py:38
  12.1 5.0 %collective-permute-start.2 = (bf16[128,512]{1,0:T(8,128)(2,1)S(1)}, bf16[128,512]{1,0:T(8,128)(2,1)S(1)}, u32[]{:S(2)}, u32[]{:S(2)}) collective-permute-start(bf16[128,512]{1,0:T(8,128)(2,1)S(1)} %pad_maximum_fusion), channel_id=1, source_target_pairs={{0,56},{4,12},{8,0},{12,20},{16,8},{20,28},{24,16},{28,36},{32,24}... | collective-permute-start | bytes 393224 | tf_op jit(solution)/shard_map/ppermute | solution.py:38
  17.1 14.0 %collective-permute-start.8 = (bf16[8,2048,128]{2,1,0:T(8,128)(2,1)}, bf16[8,2048,128]{2,1,0:T(8,128)(2,1)S(1)}, u32[]{:S(2)}, u32[]{:S(2)}) collective-permute-start(bf16[8,2048,128]{2,1,0:T(8,128)(2,1)} %far_basis_ref.1), channel_id=1, source_target_pairs={{0,4},{4,0},{1,5},{5,1},{2,6},{6,2},{3,7},{7,3},{8,12},{12,8},{9,1... | collective-permute-start | bytes 12582920 | tf_op jit(solution)/shard_map/ppermute | solution.py:42
  17.1 4.8 %collective-permute-start.5 = (bf16[128,512]{1,0:T(8,128)(2,1)S(1)}, bf16[128,512]{1,0:T(8,128)(2,1)S(1)}, u32[]{:S(2)}, u32[]{:S(2)}) collective-permute-start(bf16[128,512]{1,0:T(8,128)(2,1)S(1)} %collective-permute-done.1), channel_id=1, source_target_pairs={{0,8},{4,60},{8,16},{12,4},{16,24},{20,12},{24,32},{28,20},{32,40}... | collective-permute-start | bytes 393224 | tf_op jit(solution)/shard_map/ppermute | solution.py:38
  19.3 5.4 %collective-permute-start.9 = (bf16[128,512]{1,0:T(8,128)(2,1)S(1)}, bf16[128,512]{1,0:T(8,128)(2,1)S(1)}, u32[]{:S(2)}, u32[]{:S(2)}) collective-permute-start(bf16[128,512]{1,0:T(8,128)(2,1)S(1)} %collective-permute-done.3), channel_id=1, source_target_pairs={{0,64},{4,196},{64,128},{68,4},{128,192},{132,68},{192,0},{196,132... | collective-permute-start | bytes 393224 | tf_op jit(solution)/shard_map/ppermute | solution.py:38
  21.9 7.8 %collective-permute-start.20 = (bf16[128,512]{1,0:T(8,128)(2,1)S(1)}, bf16[128,512]{1,0:T(8,128)(2,1)S(1)}, u32[]{:S(2)}, u32[]{:S(2)}) collective-permute-start(bf16[128,512]{1,0:T(8,128)(2,1)S(1)} %collective-permute-done.2), channel_id=1, source_target_pairs={{0,56},{4,12},{8,0},{12,20},{16,8},{20,28},{24,16},{28,36},{32,24}... | collective-permute-start | bytes 393224 | tf_op jit(solution)/shard_map/ppermute | solution.py:38
  21.9 5.1 %collective-permute-start.6 = (bf16[128,512]{1,0:T(8,128)(2,1)S(1)}, bf16[128,512]{1,0:T(8,128)(2,1)S(1)}, u32[]{:S(2)}, u32[]{:S(2)}) collective-permute-start(bf16[128,512]{1,0:T(8,128)(2,1)S(1)} %collective-permute-done.5), channel_id=1, source_target_pairs={{0,8},{4,60},{8,16},{12,4},{16,24},{20,12},{24,32},{28,20},{32,40}... | collective-permute-start | bytes 393224 | tf_op jit(solution)/shard_map/ppermute | solution.py:38
  24.7 5.1 %collective-permute-start.12 = (bf16[1024,128]{1,0:T(8,128)(2,1)}, bf16[1024,128]{1,0:T(8,128)(2,1)S(1)}, u32[]{:S(2)}, u32[]{:S(2)}) collective-permute-start(bf16[1024,128]{1,0:T(8,128)(2,1)} %own_ref.1), channel_id=1, source_target_pairs={{0,4},{4,0},{1,5},{5,1},{2,6},{6,2},{3,7},{7,3},{8,12},{12,8},{9,1... | collective-permute-start | bytes 786440 | tf_op jit(solution)/shard_map/ppermute | solution.py:42
  24.8 17.5 %collective-permute-start.10 = (bf16[512,512]{1,0:T(8,128)(2,1)S(1)}, bf16[512,512]{1,0:T(8,128)(2,1)S(1)}, u32[]{:S(2)}, u32[]{:S(2)}) collective-permute-start(bf16[512,512]{1,0:T(8,128)(2,1)S(1)} %constant_dynamic-update-slice_fusion.refs_4_), channel_id=1, source_target_pairs={{0,8},{4,60},{8,16},{12,4},{16,24},{20,12},{24,32},{28,20},{32,40}... | collective-permute-start | bytes 1572872 | tf_op jit(solution)/shard_map/ppermute | solution.py:38
  27.0 11.5 %collective-permute-start.7 = (bf16[128,512]{1,0:T(8,128)(2,1)S(1)}, bf16[128,512]{1,0:T(8,128)(2,1)S(1)}, u32[]{:S(2)}, u32[]{:S(2)}) collective-permute-start(bf16[128,512]{1,0:T(8,128)(2,1)S(1)} %collective-permute-done.6), channel_id=1, source_target_pairs={{0,8},{4,60},{8,16},{12,4},{16,24},{20,12},{24,32},{28,20},{32,40}... | collective-permute-start | bytes 393224 | tf_op jit(solution)/shard_map/ppermute | solution.py:38
  29.7 8.8 %collective-permute-start.21 = (bf16[128,512]{1,0:T(8,128)(2,1)S(1)}, bf16[128,512]{1,0:T(8,128)(2,1)S(1)}, u32[]{:S(2)}, u32[]{:S(2)}) collective-permute-start(bf16[128,512]{1,0:T(8,128)(2,1)S(1)} %collective-permute-done.20), channel_id=1, source_target_pairs={{0,56},{4,12},{8,0},{12,20},{16,8},{20,28},{24,16},{28,36},{32,24}... | collective-permute-start | bytes 393224 | tf_op jit(solution)/shard_map/ppermute | solution.py:38
  29.9 13.7 %collective-permute-start.11 = (bf16[512,512]{1,0:T(8,128)(2,1)S(1)}, bf16[512,512]{1,0:T(8,128)(2,1)S(1)}, u32[]{:S(2)}, u32[]{:S(2)}) collective-permute-start(bf16[512,512]{1,0:T(8,128)(2,1)S(1)} %constant_dynamic-update-slice_fusion.refs_4_), channel_id=1, source_target_pairs={{0,56},{4,12},{8,0},{12,20},{16,8},{20,28},{24,16},{28,36},{32,24}... | collective-permute-start | bytes 1572872 | tf_op jit(solution)/shard_map/ppermute | solution.py:38
  31.2 12.4 %collective-permute-start.13 = (bf16[256,1024]{1,0:T(8,128)(2,1)S(1)}, bf16[256,1024]{1,0:T(8,128)(2,1)S(1)}, u32[]{:S(2)}, u32[]{:S(2)}) collective-permute-start(bf16[256,1024]{1,0:T(8,128)(2,1)S(1)} %turn_inputs.1.refs_0_), channel_id=1, source_target_pairs={{0,3},{4,5},{1,0},{5,6},{2,1},{6,7},{3,2},{7,4},{8,11},{12,13},{9,... | collective-permute-start | bytes 1572872 | tf_op jit(solution)/shard_map/ppermute | solution.py:38
  38.6 23.0 %collective-permute-start.22 = (bf16[1024,512]{1,0:T(8,128)(2,1)S(1)}, bf16[1024,512]{1,0:T(8,128)(2,1)S(1)}, u32[]{:S(2)}, u32[]{:S(2)}) collective-permute-start(bf16[1024,512]{1,0:T(8,128)(2,1)S(1)} %constant_dynamic-update-slice_fusion.5.refs_4_), channel_id=1, source_target_pairs={{0,64},{4,196},{64,128},{68,4},{128,192},{132,68},{192,0},{196,132... | collective-permute-start | bytes 3145736 | tf_op jit(solution)/shard_map/ppermute | solution.py:38
  40.9 8.7 %collective-permute-start.18 = (bf16[256,1024]{1,0:T(8,128)(2,1)S(1)}, bf16[256,1024]{1,0:T(8,128)(2,1)}, u32[]{:S(2)}, u32[]{:S(2)}) collective-permute-start(bf16[256,1024]{1,0:T(8,128)(2,1)S(1)} %turn_inputs.1.refs_0_), channel_id=1, source_target_pairs={{0,1},{4,7},{1,2},{5,4},{2,3},{6,5},{3,0},{7,6},{8,9},{12,15},{9,1... | collective-permute-start | bytes 1572872 | tf_op jit(solution)/shard_map/ppermute | solution.py:38
  42.4 24.5 %collective-permute-start.23 = (bf16[1024,512]{1,0:T(8,128)(2,1)S(1)}, bf16[1024,512]{1,0:T(8,128)(2,1)}, u32[]{:S(2)}, u32[]{:S(2)}) collective-permute-start(bf16[1024,512]{1,0:T(8,128)(2,1)S(1)} %constant_dynamic-update-slice_fusion.5.refs_4_), channel_id=1, source_target_pairs={{0,192},{4,68},{64,0},{68,132},{128,64},{132,196},{192,128},{196,4... | collective-permute-start | bytes 3145736 | tf_op jit(solution)/shard_map/ppermute | solution.py:38
  44.3 8.6 %collective-permute-start.14 = (bf16[512,512]{1,0:T(8,128)(2,1)S(1)}, bf16[512,512]{1,0:T(8,128)(2,1)}, u32[]{:S(2)}, u32[]{:S(2)}) collective-permute-start(bf16[512,512]{1,0:T(8,128)(2,1)S(1)} %collective-permute-done.10.refs_5_), channel_id=1, source_target_pairs={{0,8},{4,60},{8,16},{12,4},{16,24},{20,12},{24,32},{28,20},{32,40}... | collective-permute-start | bytes 1572872 | tf_op jit(solution)/shard_map/ppermute | solution.py:38
  46.6 13.5 %collective-permute-start.15 = (bf16[512,512]{1,0:T(8,128)(2,1)S(1)}, bf16[512,512]{1,0:T(8,128)(2,1)}, u32[]{:S(2)}, u32[]{:S(2)}) collective-permute-start(bf16[512,512]{1,0:T(8,128)(2,1)S(1)} %collective-permute-done.11.refs_10_), channel_id=1, source_target_pairs={{0,56},{4,12},{8,0},{12,20},{16,8},{20,28},{24,16},{28,36},{32,24}... | collective-permute-start | bytes 1572872 | tf_op jit(solution)/shard_map/ppermute | solution.py:38
  49.6 15.3 %collective-permute-start.19 = (bf16[256,1024]{1,0:T(8,128)(2,1)}, bf16[256,1024]{1,0:T(8,128)(2,1)}, u32[]{:S(2)}, u32[]{:S(2)}) collective-permute-start(bf16[256,1024]{1,0:T(8,128)(2,1)} %collective-permute-done.18.refs_1_), channel_id=1, source_target_pairs={{0,1},{4,7},{1,2},{5,4},{2,3},{6,5},{3,0},{7,6},{8,9},{12,15},{9,1... | collective-permute-start | bytes 1572872 | tf_op jit(solution)/shard_map/ppermute | solution.py:38
  60.1 14.3 %collective-permute-start.16 = (bf16[512,512]{1,0:T(8,128)(2,1)}, bf16[512,512]{1,0:T(8,128)(2,1)}, u32[]{:S(2)}, u32[]{:S(2)}) collective-permute-start(bf16[512,512]{1,0:T(8,128)(2,1)} %collective-permute-done.14.refs_6_), channel_id=1, source_target_pairs={{0,8},{4,60},{8,16},{12,4},{16,24},{20,12},{24,32},{28,20},{32,40}... | collective-permute-start | bytes 1572872 | tf_op jit(solution)/shard_map/ppermute | solution.py:38
  61.1 13.7 %collective-permute-start.17 = (bf16[512,512]{1,0:T(8,128)(2,1)}, bf16[512,512]{1,0:T(8,128)(2,1)}, u32[]{:S(2)}, u32[]{:S(2)}) collective-permute-start(bf16[512,512]{1,0:T(8,128)(2,1)} %collective-permute-done.15.refs_9_), channel_id=1, source_target_pairs={{0,56},{4,12},{8,0},{12,20},{16,8},{20,28},{24,16},{28,36},{32,24}... | collective-permute-start | bytes 1572872 | tf_op jit(solution)/shard_map/ppermute | solution.py:38
  61.5 24.9 %collective-permute-start.25 = (bf16[1024,512]{1,0:T(8,128)(2,1)S(1)}, bf16[1024,512]{1,0:T(8,128)(2,1)}, u32[]{:S(2)}, u32[]{:S(2)}) collective-permute-start(bf16[1024,512]{1,0:T(8,128)(2,1)S(1)} %collective-permute-done.22.refs_5_), channel_id=1, source_target_pairs={{0,64},{4,196},{64,128},{68,4},{128,192},{132,68},{192,0},{196,132... | collective-permute-start | bytes 3145736 | tf_op jit(solution)/shard_map/ppermute | solution.py:38
  69.5 8.7 %copy-start.15 = (f32[8,4]{0,1:T(4,128)S(1)}, f32[8,4]{0,1:T(4,128)}, u32[]{:S(2)}) copy-start(f32[8,4]{0,1:T(4,128)} %param.11) | copy-start | bytes 388
  69.5 8.7 %copy-start.2 = (bf16[8,256,512]{2,1,0:T(8,128)(2,1)S(1)}, bf16[8,256,512]{2,1,0:T(8,128)(2,1)}, u32[]{:S(2)}) copy-start(bf16[8,256,512]{2,1,0:T(8,128)(2,1)} %copy-done.1) | copy-start | bytes 6291460
  69.5 8.7 %copy-start.6 = (bf16[512,512]{1,0:T(8,128)(2,1)S(1)}, bf16[512,512]{1,0:T(8,128)(2,1)}, u32[]{:S(2)}) copy-start(bf16[512,512]{1,0:T(8,128)(2,1)} %copy-done.5) | copy-start | bytes 1572868
  69.5 8.7 %copy-start.9 = (bf16[256,1024]{1,0:T(8,128)(2,1)S(1)}, bf16[256,1024]{1,0:T(8,128)(2,1)}, u32[]{:S(2)}) copy-start(bf16[256,1024]{1,0:T(8,128)(2,1)} %copy-done.7) | copy-start | bytes 1572868
  69.5 8.7 %copy-start.11 = (bf16[512,512]{1,0:T(8,128)(2,1)S(1)}, bf16[512,512]{1,0:T(8,128)(2,1)}, u32[]{:S(2)}) copy-start(bf16[512,512]{1,0:T(8,128)(2,1)} %copy-done.10) | copy-start | bytes 1572868
  74.8 11.7 %collective-permute-start.24 = (bf16[512,512]{1,0:T(8,128)(2,1)}, bf16[512,512]{1,0:T(8,128)(2,1)S(1)}, u32[]{:S(2)}, u32[]{:S(2)}) collective-permute-start(bf16[512,512]{1,0:T(8,128)(2,1)} %collective-permute-done.16.refs_7_), channel_id=1, source_target_pairs={{0,8},{4,60},{8,16},{12,4},{16,24},{20,12},{24,32},{28,20},{32,40}... | collective-permute-start | bytes 1572872 | tf_op jit(solution)/shard_map/ppermute | solution.py:38
  90.3 31.4 %copy-start.14 = (f32[2048,128]{1,0:T(8,128)S(1)}, f32[2048,128]{1,0:T(8,128)}, u32[]{:S(2)}) copy-start(f32[2048,128]{1,0:T(8,128)} %far_field_ref.1) | copy-start | bytes 3145732
  (10 other events, 20.0 us)
